TPU v7x, 128 devices: a whole 4x4x4 slice. The times are simulated.
128 devices in a mesh: expert: 4 (over z), sector: 32 (over y, x, core).
Axes of the slice: x: 4, y: 4, z: 4, core: 2. Of those that a mesh axis runs over, the one named last changes fastest.
Arguments:
- tokens: bfloat16 [65536, 512], P('sector'), may hold values from -6 to 6
- norm_gain: float32 [512], replicated, may hold values from 0.5 to 1.5
- routes: int32 [65536, 2], P('sector'), may hold values from 0 to 63, all different within a row; in each aligned block of 2048 rows (0 to 2047, 2048 to 4095, ...) at most 128 rows name the same one
- gates: float32 [65536, 2], P('sector'), may hold values from 0.2 to 1
- expert_gate: bfloat16 [64, 512, 2048], P('sector', None, 'expert'), may hold values from -0.25 to 0.25
- expert_up: bfloat16 [64, 512, 2048], P('sector', None, 'expert'), may hold values from -0.25 to 0.25
- expert_down: bfloat16 [64, 2048, 512], P('sector', 'expert'), may hold values from -0.125 to 0.125
- shared_gate: bfloat16 [512, 2048], P(None, 'expert'), may hold values from -0.25 to 0.25
- shared_up: bfloat16 [512, 2048], P(None, 'expert'), may hold values from -0.25 to 0.25
- shared_down: bfloat16 [2048, 512], P('expert'), may hold values from -0.125 to 0.125
Outputs:
- mixed: bfloat16 [65536, 512], P('sector', 'expert')
Inputs may be any that keep to these rules, and one draw needn't show every extreme that they name: `routes`: the 2 experts of a token differ. Among the tokens of one sector (aligned blocks of 2048 tokens) each expert is named at most 128 times, a bound that some block reaches in each draw.
All inputs are finite; a program needn't handle non-finite values.
Results may differ from a plain program's by a relative error of at most 0.009.
Values may be sent and summed in bfloat16 or wider, within the bound.
No kernel may reach another device: no remote copies, remote signals or barrier semaphores. Data moves between devices by JAX's collectives and lax.ppermute only.
A program may use at most 128 MiB of HBM per device.

v0:
```python
import jax
import jax.numpy as jnp
from jax import lax
from jax.sharding import PartitionSpec as P


def per_device(
    tokens,
    norm_gain,
    routes,
    gates,
    expert_gate,
    expert_up,
    expert_down,
    shared_gate,
    shared_up,
    shared_down,
):
    tok_rows = tokens.shape[0]
    width = tokens.shape[1]
    local_experts = expert_gate.shape[0]
    sectors = lax.axis_size("sector")
    experts_all = local_experts * sectors
    capacity = 4 * tok_rows // experts_all
    choices_per = routes.shape[1]
    values = tokens.astype(jnp.float32)
    scale = lax.rsqrt(jnp.mean(values * values, axis=-1, keepdims=True) + 1e-05)
    normed = (values * scale * norm_gain).astype(jnp.bfloat16)
    flat = routes.reshape(-1)
    onehot = (flat[:, None] == jnp.arange(experts_all, dtype=jnp.int32)).astype(jnp.int32)
    rank = jnp.sum(jnp.cumsum(onehot, axis=0) * onehot, axis=-1) - 1
    position = flat * capacity + rank
    rows = jnp.repeat(normed, choices_per, axis=0)
    outgoing = jnp.zeros((experts_all * capacity, width), jnp.bfloat16).at[position].set(rows)
    outgoing = outgoing.reshape(sectors, local_experts, capacity, width)
    slots = lax.all_to_all(outgoing, "sector", split_axis=0, concat_axis=0, tiled=True)
    gate = jnp.einsum("sjkd,jdf->sjkf", slots, expert_gate, preferred_element_type=jnp.float32)
    up = jnp.einsum("sjkd,jdf->sjkf", slots, expert_up, preferred_element_type=jnp.float32)
    hidden = (jax.nn.silu(gate) * up).astype(jnp.bfloat16)
    partial_out = jnp.einsum(
        "sjkf,jfd->sjkd", hidden, expert_down, preferred_element_type=jnp.float32
    )
    shared_gate_val = jnp.dot(normed, shared_gate, preferred_element_type=jnp.float32)
    shared_up_val = jnp.dot(normed, shared_up, preferred_element_type=jnp.float32)
    shared_hidden = (jax.nn.silu(shared_gate_val) * shared_up_val).astype(jnp.bfloat16)
    shared_part = jnp.dot(shared_hidden, shared_down, preferred_element_type=jnp.float32)
    back = lax.all_to_all(partial_out, "sector", split_axis=0, concat_axis=0, tiled=True)
    picked = back.reshape(experts_all * capacity, width)[position].reshape(
        tok_rows, choices_per, width
    )
    stacked = jnp.concatenate([picked, shared_part[:, None, :]], axis=1)
    summed = lax.psum_scatter(stacked, "expert", scatter_dimension=2, tiled=True)
    expert_out = summed[:, :choices_per, :].astype(jnp.bfloat16).astype(jnp.float32)
    shared_out = summed[:, choices_per, :]
    mixed = shared_out + jnp.sum(gates[:, :, None] * expert_out, axis=1)
    return mixed.astype(jnp.bfloat16)


def solution(mesh):
    in_specs = (
        P("sector", None),
        P(),
        P("sector", None),
        P("sector", None),
        P("sector", None, "expert"),
        P("sector", None, "expert"),
        P("sector", "expert", None),
        P(None, "expert"),
        P(None, "expert"),
        P("expert", None),
    )
    out_specs = P("sector", "expert")
    return jax.shard_map(
        per_device, mesh=mesh, in_specs=in_specs, out_specs=out_specs, check_vma=False
    )
```

profile of v0, /device:TPU:1, one launch (start us, length us, event | category | flops | bytes accessed | tf_op | source)
XLA Modules:
  0.0 611.0 jit_solution(10997631554128821699)
XLA Ops:
  6.5 1.2 copy.21
  7.7 0.5 eq.29
  8.2 0.5 eq.25
  8.6 0.7 broadcast_multiply_fusion
  9.5 18.4 %reduce-window.6 = s32[64,32,128]{2,1,0:T(8,128)S(1)} reduce-window(s32[64,32,128]{2,1,0:T(8,128)S(1)} %fusion.30, s32[]{:T(128)} %constant.11.clone.1), window={size=1x1x128 pad=0_0x0_0x127_0}, to_apply=%region_0.0 | reduce-window | flops 33292288 | bytes 2097156 | tf_op jit(solution)/shard_map/reduce-window
  27.9 0.3 slice.19
  28.3 0.4 copy.32
  28.9 0.3 broadcast_add_fusion
  29.3 0.8 fusion.23
  30.1 1.4 copy.20
  31.5 1.8 mul.62
  33.3 0.5 fusion.13
  33.9 2.1 fusion.15
  36.0 3.6 broadcast_in_dim.7
  39.6 7.2 %reshape.90 = bf16[4096,512]{1,0:T(8,128)(2,1)} reshape(bf16[2048,2,512]{2,1,0:T(2,128)(2,1)} %broadcast_in_dim.7) | data formatting | bytes 8388608 | tf_op jit(solution)/shard_map/reshape | solution.py:33
  46.8 23.5 %scatter_custom_fusion = bf16[8192,512]{1,0:T(8,128)(2,1)} fusion(s32[4096]{0:T(1024)S(1)} %bitcast.78, bf16[4096,512]{1,0:T(8,128)(2,1)} %reshape.90, bf16[]{:T(256)} %constant.9.clone.1), kind=kCustom, calls=%fused_computation.22 | custom fusion | bytes 8389120 | tf_op jit(solution)/shard_map/scatter | solution.py:34
  70.3 104.4 %all_to_all.10 = bf16[32,2,128,512]{3,2,1,0:T(8,128)(2,1)S(1)} all-to-all(bf16[32,2,128,512]{3,2,1,0:T(8,128)(2,1)} %bitcast.74), channel_id=1, replica_groups=mesh['expert'=4,'sector'=32] {'sector'}, dimensions={0} | all-to-all | bytes 16777216 | tf_op jit(solution)/shard_map/all_to_all | solution.py:36
  174.7 3.2 copy-done.2
  177.9 8.1 %fusion.6 = f32[2,32,128,512]{3,2,1,0:T(8,128)} fusion(bf16[32,2,128,512]{3,2,1,0:T(8,128)(2,1)S(1)} %all_to_all.10, bf16[2,512,512]{2,1,0:T(8,128)(2,1)S(1)} %copy-done), kind=kOutput, calls=%fused_computation.11 | convolution fusion | flops 4294967296 | bytes 26214400 | tf_op jit(solution)/shard_map/sjkd,jdf->sjkf/dot_general | solution.py:38
  185.9 19.3 %fusion.10 = f32[32,2,128,512]{3,2,0,1:T(8,128)} fusion(f32[2,32,128,512]{3,2,1,0:T(8,128)} %fusion.6, bf16[32,2,128,512]{3,2,1,0:T(8,128)(2,1)} %copy-done.2, bf16[2,512,512]{2,1,0:T(8,128)(2,1)} %param.16, bf16[2,512,512]{2,1,0:T(8,128)(2,1)} %param.14), kind=kOutput, calls=%fused_computation.15 | convolution fusion | flops 8615100416 | bytes 44040192 | tf_op jit(solution)/shard_map/sjkf,jfd->sjkd/dot_general | solution.py:40
  205.2 11.8 %copy.27 = f32[32,2,128,512]{3,2,1,0:T(8,128)} copy(f32[32,2,128,512]{3,2,0,1:T(8,128)} %fusion.10) | data formatting | bytes 33554432 | tf_op jit(solution)/shard_map/sjkf,jfd->sjkd/transpose | solution.py:40
  217.0 5.3 all-to-all-start.1
  222.6 3.2 fusion.33
  225.8 7.1 %convolution_bitcast_fusion = f32[2048,1,512]{2,0,1:T(8,128)} fusion(bf16[512,512]{1,0:T(8,128)(2,1)} %param.19, f32[2048,512]{1,0:T(8,128)} %fusion.33, bf16[2048,512]{1,0:T(8,128)(2,1)S(1)} %fusion.15, bf16[512,512]{1,0:T(8,128)(2,1)} %param.18), kind=kOutput, calls=%fused_computation.24 | convolution fusion | flops 2153775104 | bytes 11534336 | tf_op jit(solution)/shard_map/dot_general | solution.py:46
  232.9 190.9 %all-to-all-done.1 = f32[32,2,128,512]{3,2,1,0:T(8,128)} async-done(((f32[32,2,128,512]{3,2,1,0:T(8,128)}), f32[32,2,128,512]{3,2,1,0:T(8,128)}, u32[]{:S(2)}, u32[]{:S(2)}) %all-to-all-start.1) | async-done | bytes 16777248 | tf_op jit(solution)/shard_map/all_to_all | solution.py:47
  423.8 23.8 %gather_fusion = f32[4096,512]{1,0:T(8,128)} fusion(f32[8192,512]{1,0:T(8,128)} %bitcast.15, s32[4096]{0:T(1024)S(1)} %broadcast_clamp_fusion), kind=kCustom, calls=%fused_computation | custom fusion | bytes 16793600 | tf_op jit(solution)/shard_map/gather | solution.py:48
  447.6 10.6 %reshape.77 = f32[2048,2,512]{2,1,0:T(2,128)} reshape(f32[4096,512]{1,0:T(8,128)} %gather_fusion) | data formatting | bytes 16777216 | tf_op jit(solution)/shard_map/reshape | solution.py:48
  458.2 8.3 %copy.28 = f32[2048,2,512]{2,0,1:T(8,128)} copy(f32[2048,2,512]{2,1,0:T(2,128)} %reshape.77) | data formatting | bytes 16777216 | tf_op jit(solution)/shard_map/reshape | solution.py:48
  466.5 9.5 %pad_maximum_fusion = f32[2048,3,512]{2,0,1:T(8,128)} fusion(f32[2048,1,512]{2,0,1:T(8,128)S(1)} %copy-done.4, f32[2048,2,512]{2,0,1:T(8,128)} %copy.28), kind=kLoop, calls=%fused_computation.9 | loop fusion | flops 3145728 | bytes 25165824 | tf_op jit(solution)/shard_map/concatenate | solution.py:51
  476.0 124.0 %reduce-scatter.2.cloned.1.call-done = f32[2048,3,128]{2,0,1:T(8,128)} async-done(((f32[2048,3,512]{2,0,1:T(8,128)}), f32[2048,3,128]{2,0,1:T(8,128)}) %reduce-scatter.2.cloned.1.call-update) | async-done | bytes 3145744 | tf_op jit(solution)/shard_map/reduce_scatter | solution.py:52
  600.0 2.0 multiply_reduce_fusion
  602.0 2.1 fusion.25
  (23 shorter events, 0.7 us)
Async XLA Ops:
  6.5 171.3 %copy-start = (bf16[2,512,512]{2,1,0:T(8,128)(2,1)S(1)}, bf16[2,512,512]{2,1,0:T(8,128)(2,1)}, u32[]{:S(2)}) copy-start(bf16[2,512,512]{2,1,0:T(8,128)(2,1)} %param.15) | copy-start | bytes 3145732
  28.3 5.6 copy-start.7
  29.3 4.1 copy-start.3
  174.7 3.2 copy-start.2
  217.0 5.6 copy-start.5
  217.0 206.8 %all-to-all-start.1 = ((f32[32,2,128,512]{3,2,1,0:T(8,128)}), f32[32,2,128,512]{3,2,1,0:T(8,128)}, u32[]{:S(2)}, u32[]{:S(2)}) async-start(f32[32,2,128,512]{3,2,1,0:T(8,128)} %copy.27), calls=%async_computation.1 | async-start | bytes 33554432 | tf_op jit(solution)/shard_map/all_to_all | solution.py:47
  222.3 377.7 %reduce-scatter.2.cloned.1.call-start = ((), (), s32[]{:S(2)}) async-start(), calls=%async_computation.3 | async-start | bytes 15728640 | tf_op jit(solution)/shard_map/reduce_scatter | solution.py:52
  458.2 8.3 %copy-start.4 = (f32[2048,1,512]{2,0,1:T(8,128)S(1)}, f32[2048,1,512]{2,0,1:T(8,128)}, u32[]{:S(2)}) copy-start(f32[2048,1,512]{2,0,1:T(8,128)} %convolution_bitcast_fusion) | copy-start | bytes 12582916
  476.0 124.0 %copy-start.6 = (f32[2048,2]{0,1:T(2,128)S(1)}, f32[2048,2]{0,1:T(2,128)}, u32[]{:S(2)}) copy-start(f32[2048,2]{0,1:T(2,128)} %param.13) | copy-start | bytes 49156
  476.0 128.1 %copy-start.1 = (bf16[2,512,512]{2,1,0:T(8,128)(2,1)S(1)}, bf16[2,512,512]{2,1,0:T(8,128)(2,1)}, u32[]{:S(2)}) copy-start(bf16[2,512,512]{2,1,0:T(8,128)(2,1)} %param.15) | copy-start | bytes 3145732
Sparse Core Ops, SparseCore 0:
  476.1 123.8 reduce-scatter.1
where the time goes:
time: 612 us; the launch traced here: 611 us
  waiting for transfers between devices  315 us (51%)
  blocking collectives  104 us (17%)
  local copies, waits for them, and re-layouts  98.1 us (16%)
  matrix products  37.6 us (6%)
  other arithmetic  36.9 us (6%)
  between operations  13.6 us (2%)
    all_to_all x1, waiting for transfers between devices, per_device(): lax.all_to_all(partial_out, 'sector', split_axis=0, concat_axis=0, tiled=...  191 us
    reduce_scatter x1, waiting for transfers between devices, per_device(): lax.psum_scatter(stacked, 'expert', scatter_dimension=2, tiled=True)  124 us
    all_to_all x1, blocking collectives, per_device(): lax.all_to_all(outgoing, 'sector', split_axis=0, concat_axis=0, tiled=True)  104 us
    gather x1, local copies, waits for them, and re-layouts, per_device(): back.reshape(experts_all * capacity, width)[position]  23.8 us
    scatter x1, local copies, waits for them, and re-layouts, per_device(): jnp.zeros((experts_all * capacity, width), jnp.bfloat16).at[position]  23.5 us
    dot_general x1, matrix products, per_device(): jnp.einsum('sjkf,jfd->sjkd', hidden, expert_down, preferred_element_type=...  19.3 us
    another operation x3, other arithmetic  19 us
    reshape x2, local copies, waits for them, and re-layouts, per_device(): back.reshape(experts_all * capacity, width)[position]  18.9 us
  transfers between devices with their start and end apart: 2, of which 2 were waited for; matrix products, arithmetic and copies ran while one was open for 2% of the time, Pallas kernels for 0%

commit v1 on v0

v1 whole, which is shorter than its diff:
```python
import functools

import jax
import jax.numpy as jnp
from jax import lax
from jax.experimental import pallas as pl
from jax.experimental.pallas import tpu as pltpu
from jax.sharding import PartitionSpec as P

F32 = jnp.float32
BF16 = jnp.bfloat16
VMEM_LIMIT = 56 * 1024 * 1024


def dot(a, b):
    return jnp.dot(a, b, preferred_element_type=F32)


def swish(gate, up):
    return (gate / (1.0 + jnp.exp(-gate)) * up).astype(BF16)


def pack_kernel(half, place, gate, up, down, *sends):
    for r, send in enumerate(sends):
        pick = place[0] ^ r
        expert, part = pick // 2, pick % 2
        cols = pl.ds(pl.multiple_of(part * half, half), half)
        for n, w in enumerate((gate, up)):
            send[n, :, :half] = w[expert, :half, cols]
            send[n, :, half:] = w[expert, half:, cols]
        send[2] = down[expert, cols, :]


def pack(gate, up, down, place):
    _, width, hidden = gate.shape
    half = hidden // 2
    shape = jax.ShapeDtypeStruct((3, half, width), BF16)
    return pl.pallas_call(
        functools.partial(pack_kernel, half),
        out_shape=[shape] * 4,
        in_specs=[pl.BlockSpec(memory_space=pltpu.SMEM)] + [pl.BlockSpec(memory_space=pltpu.VMEM)] * 3,
        out_specs=[pl.BlockSpec(memory_space=pltpu.VMEM)] * 4,
        compiler_params=pltpu.CompilerParams(vmem_limit_bytes=VMEM_LIMIT),
        cost_estimate=pl.CostEstimate(flops=0, bytes_accessed=6 * gate.size * 2, transcendentals=0),
    )(place, gate, up, down)


def route_kernel(block, cap, stack, plane, tokens, gain, routes, outgoing, normed, position, chosen):
    step = pl.program_id(0)
    rows, width = tokens.shape
    experts = chosen.shape[0]
    z = plane[0]

    @pl.when(step == 0)
    def _():
        earlier = (
            lax.broadcasted_iota(jnp.int32, (block, block), 0) < lax.broadcasted_iota(jnp.int32, (block, block), 1)
        ).astype(F32).astype(BF16)
        mine = lax.broadcasted_iota(jnp.int32, (experts, block), 0) * stack + z
        column = lax.broadcasted_iota(jnp.int32, (experts, block), 0) * cap
        seen = jnp.zeros((experts, 1), F32)
        for b in range(rows // block):
            at = pl.ds(b * block, block)
            first = routes[0:1, at] == mine
            second = routes[1:2, at] == mine
            named = jnp.where(first | second, 1.0, 0.0).astype(F32)
            rank = dot(named.astype(BF16), earlier) + seen
            chosen[:, at] = jnp.where(first | second, rank, -1.0)
            seen = seen + jnp.sum(named, axis=1, keepdims=True)
            slot = rank + column.astype(F32)
            place = jnp.max(jnp.where(first, slot, -1.0), axis=0, keepdims=True)
            other = jnp.max(jnp.where(second, slot, -1.0), axis=0, keepdims=True)
            position[0:1, at] = place
            position[1:2, at] = other
            values = tokens[at, :].astype(F32)
            scale = lax.rsqrt(jnp.mean(values * values, axis=-1, keepdims=True) + 1e-05)
            normed[at, :] = (values * scale * gain[...]).astype(BF16)

    ranks = lax.broadcasted_iota(jnp.int32, (cap, rows), 0).astype(F32)
    per = outgoing.shape[0] // cap
    masks = [
        jnp.where(ranks == chosen[pl.ds(step * per + i, 1), :], 1.0, 0.0).astype(BF16) for i in range(per)
    ]
    outgoing[...] = dot(jnp.concatenate(masks, axis=0), normed[...]).astype(BF16)


def route(tokens, gain, routes, plane, experts, cap, stack):
    rows, width = tokens.shape
    slots = experts * cap
    block, per = 256, 2 * cap
    return pl.pallas_call(
        functools.partial(route_kernel, block, cap, stack),
        grid=(slots // per,),
        out_shape=[
            jax.ShapeDtypeStruct((slots, width), BF16),
            jax.ShapeDtypeStruct((rows, width), BF16),
            jax.ShapeDtypeStruct((2, rows), F32),
        ],
        in_specs=[
            pl.BlockSpec(memory_space=pltpu.SMEM),
            pl.BlockSpec((rows, width), lambda i: (0, 0)),
            pl.BlockSpec((1, width), lambda i: (0, 0)),
            pl.BlockSpec((2, rows), lambda i: (0, 0)),
        ],
        out_specs=[
            pl.BlockSpec((per, width), lambda i: (i, 0)),
            pl.BlockSpec((rows, width), lambda i: (0, 0)),
            pl.BlockSpec((2, rows), lambda i: (0, 0)),
        ],
        scratch_shapes=[pltpu.VMEM((experts, rows), F32)],
        compiler_params=pltpu.CompilerParams(vmem_limit_bytes=VMEM_LIMIT),
        cost_estimate=pl.CostEstimate(
            flops=2 * slots * rows * width, bytes_accessed=6 * rows * width + 2 * slots * width, transcendentals=rows
        ),
    )(plane, tokens, gain, routes)


def shared_kernel(normed, gate, up, down, out):
    x = normed[...]
    out[...] = dot(swish(dot(x, gate[...]), dot(x, up[...])), down[...])


def shared_expert(normed, gate, up, down):
    rows, width = normed.shape
    hidden = gate.shape[1]
    block = 256
    whole = [pl.BlockSpec(w.shape, lambda i: (0, 0)) for w in (gate, up, down)]
    return pl.pallas_call(
        shared_kernel,
        grid=(rows // block,),
        out_shape=jax.ShapeDtypeStruct((rows, width), F32),
        in_specs=[pl.BlockSpec((block, width), lambda i: (i, 0))] + whole,
        out_specs=pl.BlockSpec((block, width), lambda i: (i, 0)),
        compiler_params=pltpu.CompilerParams(vmem_limit_bytes=VMEM_LIMIT),
        cost_estimate=pl.CostEstimate(
            flops=6 * rows * width * hidden, bytes_accessed=6 * rows * width, transcendentals=rows * hidden
        ),
    )(normed, gate, up, down)


def expert_kernel(slots, *refs):
    weights, out = refs[:-1], refs[-1]
    half = slots.shape[1] // 2
    low, high = slots[:, :half], slots[:, half:]
    total = None
    for w in weights:
        gate = dot(low, w[0, :, :half]) + dot(high, w[0, :, half:])
        up = dot(low, w[1, :, :half]) + dot(high, w[1, :, half:])
        part = dot(swish(gate, up), w[2])
        total = part if total is None else total + part
    out[...] = total.astype(BF16)


def expert(slots, weights):
    rows, width = slots.shape
    block = 256
    hidden = sum(w.shape[1] for w in weights)
    return pl.pallas_call(
        expert_kernel,
        grid=(rows // block,),
        out_shape=jax.ShapeDtypeStruct((rows, width), BF16),
        in_specs=[pl.BlockSpec((block, width), lambda i: (i, 0))]
        + [pl.BlockSpec(w.shape, lambda i: (0, 0, 0)) for w in weights],
        out_specs=pl.BlockSpec((block, width), lambda i: (i, 0)),
        compiler_params=pltpu.CompilerParams(vmem_limit_bytes=VMEM_LIMIT),
        cost_estimate=pl.CostEstimate(
            flops=6 * rows * width * hidden, bytes_accessed=4 * rows * width + 6 * width * hidden,
            transcendentals=rows * hidden,
        ),
    )(slots, *weights)


def combine_kernel(position, gates, back, shared, out):
    slots = back.shape[0]
    rows = shared.shape[0]
    table = jnp.concatenate([position[...], gates[...], jnp.zeros((4, rows), F32)], axis=0).T
    number = lax.broadcasted_iota(jnp.int32, (rows, slots), 1).astype(F32)
    weight = jnp.where(
        number == table[:, 0:1], table[:, 2:3], jnp.where(number == table[:, 1:2], table[:, 3:4], 0.0)
    )
    mixed = (dot(weight.astype(BF16), back[...]) + shared[...]).astype(BF16)
    part = out.shape[2]
    for q in range(out.shape[0]):
        out[q] = mixed[:, q * part : (q + 1) * part]


def combine(position, gates, back, shared, planes):
    rows, width = shared.shape
    slots = back.shape[0]
    block = 256
    return pl.pallas_call(
        combine_kernel,
        grid=(rows // block,),
        out_shape=jax.ShapeDtypeStruct((planes, rows, width // planes), BF16),
        in_specs=[
            pl.BlockSpec((2, block), lambda i: (0, i)),
            pl.BlockSpec((2, block), lambda i: (0, i)),
            pl.BlockSpec((slots, width), lambda i: (0, 0)),
            pl.BlockSpec((block, width), lambda i: (i, 0)),
        ],
        out_specs=pl.BlockSpec((planes, block, width // planes), lambda i: (0, i, 0)),
        compiler_params=pltpu.CompilerParams(vmem_limit_bytes=VMEM_LIMIT),
        cost_estimate=pl.CostEstimate(
            flops=2 * rows * slots * width, bytes_accessed=6 * rows * width + 2 * slots * width, transcendentals=0
        ),
    )(position, gates, back, shared)


def per_device(
    tokens,
    norm_gain,
    routes,
    gates,
    expert_gate,
    expert_up,
    expert_down,
    shared_gate,
    shared_up,
    shared_down,
):
    rows, width = tokens.shape
    planes, sectors = lax.axis_size("expert"), lax.axis_size("sector")
    columns = sectors // 2
    cap = 128
    both = ("expert", "sector")
    z = lax.axis_index("expert").astype(jnp.int32).reshape(1)

    sends = pack(expert_gate, expert_up, expert_down, z)
    weights = []
    for r, send in enumerate(sends):
        moves = []
        for source in range(planes):
            for s in range(sectors):
                pick = source ^ r
                target = 2 * (s % 2) + pick // 2
                moves.append((source * sectors + s, target * sectors + (s // 2) * 2 + pick % 2))
        half = lax.ppermute(send, both, moves)
        other = lax.ppermute(half, "sector", [(s, s ^ 1) for s in range(sectors)])
        weights += [half, other]

    outgoing, normed, position = route(tokens, norm_gain.reshape(1, width), routes.T, z, columns, cap, planes)
    slots = lax.all_to_all(outgoing.reshape(sectors, -1, width), "sector", 0, 0, tiled=True)
    shared = shared_expert(normed, shared_gate, shared_up, shared_down)
    results = expert(slots.reshape(-1, width), weights)
    back = lax.all_to_all(results.reshape(sectors, -1, width), "sector", 0, 0, tiled=True)
    parts = combine(position, gates.T, back.reshape(-1, width), shared, planes)
    parts = lax.all_to_all(parts, "expert", 0, 0, tiled=True)
    return jnp.sum(parts.astype(F32), axis=0).astype(BF16)


def solution(mesh):
    in_specs = (
        P("sector", None),
        P(),
        P("sector", None),
        P("sector", None),
        P("sector", None, "expert"),
        P("sector", None, "expert"),
        P("sector", "expert", None),
        P(None, "expert"),
        P(None, "expert"),
        P("expert", None),
    )
    out_specs = P("sector", "expert")
    return jax.shard_map(
        per_device, mesh=mesh, in_specs=in_specs, out_specs=out_specs, check_vma=False
    )
```

time: 612 us -> 173 us (0.28)
  waiting for transfers between devices: 315 us -> 50.8 us
  local copies, waits for them, and re-layouts: 98.1 us -> 4.71 us
  blocking collectives: 104 us -> 27.6 us
  Pallas kernels: 0 us -> 56.6 us
  matrix products: 37.6 us -> 0 us
  other arithmetic: 36.9 us -> 1.23 us
  starting transfers between devices: 5.53 us -> 29.5 us
  between operations: 13.6 us -> 0.11 us
    all_to_all x1 -> x2, waiting for transfers between devices: 191 us -> 18.7 us  [the longest x1 18.7 us: per_device(): lax.all_to_all(results.reshape(sectors, -1, width), 'sector', 0, 0, tiled...]
    reduce_scatter x1 -> x0, waiting for transfers between devices: 124 us -> none  [per_device(): lax.psum_scatter(stacked, 'expert', scatter_dimension=2, tiled=True)]
    all_to_all x1, blocking collectives: 104 us -> 27.6 us  [per_device(): parts = lax.all_to_all(parts, 'expert', 0, 0, tiled=True)]
    pallas_call x0 -> x5, Pallas kernels: none -> 56.6 us  [the longest x1 23.8 us: expert(): pl.pallas_call(expert_kernel, grid=(rows // block,), out_shape=jax.ShapeD...]
    dot_general x4 -> x0, matrix products: 37.6 us -> none  [the longest x1 19.3 us: per_device(): jnp.einsum('sjkf,jfd->sjkd', hidden, expert_down, preferred_element_type=...]
    ppermute x0 -> x8, waiting for transfers between devices: none -> 32.1 us  [the longest x4 32.1 us: per_device(): half = lax.ppermute(send, both, moves)]
    reshape x3 -> x0, local copies, waits for them, and re-layouts: 26.1 us -> none  [the longest x2 18.9 us: per_device(): back.reshape(experts_all * capacity, width)[position]]
    gather x1 -> x0, local copies, waits for them, and re-layouts: 23.8 us -> none  [per_device(): back.reshape(experts_all * capacity, width)[position]]
  transfers between devices with their start and end apart: 2 -> 10, of which waited for: 2 -> 4; matrix products, arithmetic and copies ran while one was open for 2% -> 0% of each run, Pallas kernels for 0% -> 8%
where the time goes in v1:
time: 173 us; the launch traced here: 171 us
  Pallas kernels  56.6 us (33%)
  waiting for transfers between devices  50.8 us (29%)
  starting transfers between devices  29.5 us (17%)
  blocking collectives  27.6 us (16%)
  local copies, waits for them, and re-layouts  4.71 us (3%)
    ppermute x4, waiting for transfers between devices, per_device(): half = lax.ppermute(send, both, moves)  32.1 us
    all_to_all x1, blocking collectives, per_device(): parts = lax.all_to_all(parts, 'expert', 0, 0, tiled=True)  27.6 us
    pallas_call x1, Pallas kernels, expert(): pl.pallas_call(expert_kernel, grid=(rows // block,), out_shape=jax.ShapeD...  23.8 us
    all_to_all x1, waiting for transfers between devices, per_device(): lax.all_to_all(results.reshape(sectors, -1, width), 'sector', 0, 0, tiled...  18.7 us
    pallas_call x1, Pallas kernels, combine(): pl.pallas_call(combine_kernel, grid=(rows // block,), out_shape=jax.Shape...  10.8 us
    ppermute x4, starting transfers between devices, per_device(): half = lax.ppermute(send, both, moves)  9.3 us
    pallas_call x1, Pallas kernels, shared_expert(): pl.pallas_call(shared_kernel, grid=(rows // block,), out_shape=jax.ShapeD...  9.11 us
    pallas_call x1, Pallas kernels, route(): pl.pallas_call(functools.partial(route_kernel, block, cap, stack), grid=(...  9.1 us
  transfers between devices with their start and end apart: 10, of which 4 were waited for; matrix products, arithmetic and copies ran while one was open for 0% of the time, Pallas kernels for 8%

profile of v1, /device:TPU:1, one launch (start us, length us, event | category | flops | bytes accessed | tf_op | source)
XLA Modules:
  0.0 170.5 jit_solution(11895454299398849313)
XLA Ops:
  0.0 9.1 %shard_map.100 = (bf16[2048,512]{1,0:T(8,128)(2,1)}, bf16[2048,512]{1,0:T(8,128)(2,1)}, f32[2,2048]{1,0:T(2,128)}) custom-call(s32[1]{0:T(128)} %bitcast.plane.place, bf16[2048,512]{1,0:T(8,128)(2,1)} %tokens.1, f32[1,512]{1,0:T(1,128)} %bitcast.14, s32[2,2048]{1,0:T(2,128)} %bitcast.12), custom_call_target="tpu_custom_call" | custom-call | flops 4294967296 | bytes 8388608 | tf_op jit(solution)/shard_map/pallas_call | solution.py:91
  9.1 8.6 %all-to-all-start = ((bf16[32,64,512]{2,1,0:T(8,128)(2,1)}), bf16[32,64,512]{2,1,0:T(8,128)(2,1)S(1)}, u32[]{:S(2)}, u32[]{:S(2)}) async-start(bf16[32,64,512]{2,1,0:T(8,128)(2,1)} %bitcast.9), calls=%async_computation | async-start | bytes 4194304 | tf_op jit(solution)/shard_map/all_to_all | solution.py:242
  17.7 3.7 %shard_map.101 = (bf16[3,256,512]{2,1,0:T(8,128)(2,1)}, bf16[3,256,512]{2,1,0:T(8,128)(2,1)}, bf16[3,256,512]{2,1,0:T(8,128)(2,1)}, bf16[3,256,512]{2,1,0:T(8,128)(2,1)}) custom-call(s32[1]{0:T(128)} %bitcast.plane.place, bf16[2,512,512]{2,1,0:T(8,128)(2,1)} %gate.2, bf16[2,512,512]{2,1,0:T(8,128)(2,1)} %up.2, bf16[2,512,512]{2,1,0:T(8,128)(2,1)} %down.2), custom_call_target="tpu_custom_call" | custom-call | bytes 6291456 | tf_op jit(solution)/shard_map/pallas_call | solution.py:38
  21.4 5.6 %collective-permute-start = (bf16[3,256,512]{2,1,0:T(8,128)(2,1)}, bf16[3,256,512]{2,1,0:T(8,128)(2,1)S(1)}, u32[]{:S(2)}, u32[]{:S(2)}) collective-permute-start(bf16[3,256,512]{2,1,0:T(8,128)(2,1)} %get-tuple-element.14), channel_id=1, source_target_pairs={{0,0},{1,64},{2,2},{3,66},{4,4},{5,68},{6,6},{7,70},{8,8},{9,72},{... | collective-permute-start | bytes 2359304 | tf_op jit(solution)/shard_map/ppermute | solution.py:237
  27.0 1.4 collective-permute-start.2
  28.4 0.0 collective-permute-start.4
  28.5 2.3 %collective-permute-start.6 = (bf16[3,256,512]{2,1,0:T(8,128)(2,1)}, bf16[3,256,512]{2,1,0:T(8,128)(2,1)S(1)}, u32[]{:S(2)}, u32[]{:S(2)}) collective-permute-start(bf16[3,256,512]{2,1,0:T(8,128)(2,1)} %get-tuple-element.17), channel_id=1, source_target_pairs={{0,33},{1,97},{2,35},{3,99},{4,37},{5,101},{6,39},{7,103},{8,41},{... | collective-permute-start | bytes 2359304 | tf_op jit(solution)/shard_map/ppermute | solution.py:237
  30.7 13.2 %collective-permute-done.refs_0_ = bf16[3,256,512]{2,1,0:T(8,128)(2,1)S(1)} collective-permute-done((bf16[3,256,512]{2,1,0:T(8,128)(2,1)}, bf16[3,256,512]{2,1,0:T(8,128)(2,1)S(1)}, u32[]{:S(2)}, u32[]{:S(2)}) %collective-permute-start) | collective-permute-done | bytes 786464 | tf_op jit(solution)/shard_map/ppermute | solution.py:237
  43.9 0.0 collective-permute-start.1
  43.9 16.8 %collective-permute-done.2.refs_2_ = bf16[3,256,512]{2,1,0:T(8,128)(2,1)S(1)} collective-permute-done((bf16[3,256,512]{2,1,0:T(8,128)(2,1)}, bf16[3,256,512]{2,1,0:T(8,128)(2,1)S(1)}, u32[]{:S(2)}, u32[]{:S(2)}) %collective-permute-start.2) | collective-permute-done | bytes 786464 | tf_op jit(solution)/shard_map/ppermute | solution.py:237
  60.8 0.0 collective-permute-start.3
  60.8 0.0 collective-permute-done.4.refs_4_
  60.8 0.5 collective-permute-start.5
  61.3 2.0 %collective-permute-done.6.refs_6_ = bf16[3,256,512]{2,1,0:T(8,128)(2,1)S(1)} collective-permute-done((bf16[3,256,512]{2,1,0:T(8,128)(2,1)}, bf16[3,256,512]{2,1,0:T(8,128)(2,1)S(1)}, u32[]{:S(2)}, u32[]{:S(2)}) %collective-permute-start.6) | collective-permute-done | bytes 786464 | tf_op jit(solution)/shard_map/ppermute | solution.py:237
  63.3 3.6 %collective-permute-start.7 = (bf16[3,256,512]{2,1,0:T(8,128)(2,1)S(1)}, bf16[3,256,512]{2,1,0:T(8,128)(2,1)}, u32[]{:S(2)}, u32[]{:S(2)}) collective-permute-start(bf16[3,256,512]{2,1,0:T(8,128)(2,1)S(1)} %collective-permute-done.6.refs_6_), channel_id=1, source_target_pairs={{0,1},{1,0},{2,3},{3,2},{4,5},{5,4},{6,7},{7,6},{8,9},{9,8},{10,11... | collective-permute-start | bytes 2359304 | tf_op jit(solution)/shard_map/ppermute | solution.py:238
  67.0 0.0 collective-permute-done.1.refs_1_
  67.0 0.0 collective-permute-done.3.refs_3_
  67.0 0.0 collective-permute-done.5.refs_5_
  67.0 0.8 copy-done.6
  67.9 0.3 copy-done.7
  68.1 0.9 copy-done.8
  69.1 0.0 collective-permute-done.7.refs_7_
  69.1 0.0 all-to-all-done
  69.1 1.3 copy-done
  70.4 23.8 %shard_map.102 = bf16[2048,512]{1,0:T(8,128)(2,1)} custom-call(bf16[2048,512]{1,0:T(8,128)(2,1)} %bitcast.8, bf16[3,256,512]{2,1,0:T(8,128)(2,1)} %copy-done.2, bf16[3,256,512]{2,1,0:T(8,128)(2,1)} %copy-done.6, bf16[3,256,512]{2,1,0:T(8,128)(2,1)} %copy-done.3, bf16[3,256,512]{2,1,0:T(8,128)(2,1)} %copy-done.7, bf16[3,256,512]{2,1,0:T(8,128)(2,1)} %copy-done.4, ...), custom_call_target="tpu_custom_call" | custom-call | flops 12884901888 | bytes 10485760 | tf_op jit(solution)/shard_map/pallas_call | solution.py:158
  94.2 7.5 %all-to-all-start.1 = ((bf16[32,64,512]{2,1,0:T(8,128)(2,1)}), bf16[32,64,512]{2,1,0:T(8,128)(2,1)S(1)}, u32[]{:S(2)}, u32[]{:S(2)}) async-start(bf16[32,64,512]{2,1,0:T(8,128)(2,1)} %bitcast.10), calls=%async_computation.1 | async-start | bytes 4194304 | tf_op jit(solution)/shard_map/all_to_all | solution.py:245
  101.7 9.1 %shard_map.103.shared = f32[2048,512]{1,0:T(8,128)} custom-call(bf16[2048,512]{1,0:T(8,128)(2,1)} %get-tuple-element.18.normed, bf16[512,512]{1,0:T(8,128)(2,1)} %gate.3, bf16[512,512]{1,0:T(8,128)(2,1)} %up.3, bf16[512,512]{1,0:T(8,128)(2,1)} %down.3), custom_call_target="tpu_custom_call" | custom-call | flops 3221225472 | bytes 6291456 | tf_op jit(solution)/shard_map/pallas_call | solution.py:128
  110.8 18.7 %all-to-all-done.1 = bf16[32,64,512]{2,1,0:T(8,128)(2,1)S(1)} async-done(((bf16[32,64,512]{2,1,0:T(8,128)(2,1)}), bf16[32,64,512]{2,1,0:T(8,128)(2,1)S(1)}, u32[]{:S(2)}, u32[]{:S(2)}) %all-to-all-start.1) | async-done | bytes 2097184 | tf_op jit(solution)/shard_map/all_to_all | solution.py:245
  129.5 1.3 copy-done.1
  130.9 10.8 %shard_map.104 = bf16[4,2048,128]{2,1,0:T(8,128)(2,1)} custom-call(f32[2,2048]{1,0:T(2,128)} %get-tuple-element.12.position, f32[2,2048]{1,0:T(2,128)} %bitcast.13, bf16[2048,512]{1,0:T(8,128)(2,1)} %bitcast.11, f32[2048,512]{1,0:T(8,128)} %shard_map.103.shared), custom_call_target="tpu_custom_call" | custom-call | flops 4294967296 | bytes 8388608 | tf_op jit(solution)/shard_map/pallas_call | solution.py:191
  141.7 27.6 %all_to_all.15 = bf16[4,2048,128]{2,1,0:T(8,128)(2,1)S(1)} all-to-all(bf16[4,2048,128]{2,1,0:T(8,128)(2,1)} %shard_map.104), channel_id=1, replica_groups=mesh['expert'=4,'sector'=32] {'expert'}, dimensions={0} | all-to-all | bytes 4194304 | tf_op jit(solution)/shard_map/all_to_all | solution.py:247
  169.3 1.2 reduce_sum.12
  (13 shorter events, 0.0 us)
Async XLA Ops:
  9.1 60.0 %all-to-all-start = ((bf16[32,64,512]{2,1,0:T(8,128)(2,1)}), bf16[32,64,512]{2,1,0:T(8,128)(2,1)S(1)}, u32[]{:S(2)}, u32[]{:S(2)}) async-start(bf16[32,64,512]{2,1,0:T(8,128)(2,1)} %bitcast.9), calls=%async_computation | async-start | bytes 4194304 | tf_op jit(solution)/shard_map/all_to_all | solution.py:242
  21.4 22.5 %collective-permute-start = (bf16[3,256,512]{2,1,0:T(8,128)(2,1)}, bf16[3,256,512]{2,1,0:T(8,128)(2,1)S(1)}, u32[]{:S(2)}, u32[]{:S(2)}) collective-permute-start(bf16[3,256,512]{2,1,0:T(8,128)(2,1)} %get-tuple-element.14), channel_id=1, source_target_pairs={{0,0},{1,64},{2,2},{3,66},{4,4},{5,68},{6,6},{7,70},{8,8},{9,72},{... | collective-permute-start | bytes 2359304 | tf_op jit(solution)/shard_map/ppermute | solution.py:237
  27.0 33.7 %collective-permute-start.2 = (bf16[3,256,512]{2,1,0:T(8,128)(2,1)}, bf16[3,256,512]{2,1,0:T(8,128)(2,1)S(1)}, u32[]{:S(2)}, u32[]{:S(2)}) collective-permute-start(bf16[3,256,512]{2,1,0:T(8,128)(2,1)} %get-tuple-element.15), channel_id=1, source_target_pairs={{0,1},{1,65},{2,3},{3,67},{4,5},{5,69},{6,7},{7,71},{8,9},{9,73},{... | collective-permute-start | bytes 2359304 | tf_op jit(solution)/shard_map/ppermute | solution.py:237
  28.4 32.3 %collective-permute-start.4 = (bf16[3,256,512]{2,1,0:T(8,128)(2,1)}, bf16[3,256,512]{2,1,0:T(8,128)(2,1)S(1)}, u32[]{:S(2)}, u32[]{:S(2)}) collective-permute-start(bf16[3,256,512]{2,1,0:T(8,128)(2,1)} %get-tuple-element.16), channel_id=1, source_target_pairs={{0,32},{1,96},{2,34},{3,98},{4,36},{5,100},{6,38},{7,102},{8,40},{... | collective-permute-start | bytes 2359304 | tf_op jit(solution)/shard_map/ppermute | solution.py:237
  28.5 34.9 %collective-permute-start.6 = (bf16[3,256,512]{2,1,0:T(8,128)(2,1)}, bf16[3,256,512]{2,1,0:T(8,128)(2,1)S(1)}, u32[]{:S(2)}, u32[]{:S(2)}) collective-permute-start(bf16[3,256,512]{2,1,0:T(8,128)(2,1)} %get-tuple-element.17), channel_id=1, source_target_pairs={{0,33},{1,97},{2,35},{3,99},{4,37},{5,101},{6,39},{7,103},{8,41},{... | collective-permute-start | bytes 2359304 | tf_op jit(solution)/shard_map/ppermute | solution.py:237
  43.9 25.1 %copy-start.2 = (bf16[3,256,512]{2,1,0:T(8,128)(2,1)}, bf16[3,256,512]{2,1,0:T(8,128)(2,1)S(1)}, u32[]{:S(2)}) copy-start(bf16[3,256,512]{2,1,0:T(8,128)(2,1)S(1)} %collective-permute-done.refs_0_) | copy-start | bytes 2359300
  43.9 23.0 %collective-permute-start.1 = (bf16[3,256,512]{2,1,0:T(8,128)(2,1)S(1)}, bf16[3,256,512]{2,1,0:T(8,128)(2,1)S(1)}, u32[]{:S(2)}, u32[]{:S(2)}) collective-permute-start(bf16[3,256,512]{2,1,0:T(8,128)(2,1)S(1)} %collective-permute-done.refs_0_), channel_id=1, source_target_pairs={{0,1},{1,0},{2,3},{3,2},{4,5},{5,4},{6,7},{7,6},{8,9},{9,8},{10,11... | collective-permute-start | bytes 2359304 | tf_op jit(solution)/shard_map/ppermute | solution.py:238
  60.8 6.2 %copy-start.3 = (bf16[3,256,512]{2,1,0:T(8,128)(2,1)}, bf16[3,256,512]{2,1,0:T(8,128)(2,1)S(1)}, u32[]{:S(2)}) copy-start(bf16[3,256,512]{2,1,0:T(8,128)(2,1)S(1)} %collective-permute-done.2.refs_2_) | copy-start | bytes 2359300
  60.8 6.2 %collective-permute-start.3 = (bf16[3,256,512]{2,1,0:T(8,128)(2,1)S(1)}, bf16[3,256,512]{2,1,0:T(8,128)(2,1)S(1)}, u32[]{:S(2)}, u32[]{:S(2)}) collective-permute-start(bf16[3,256,512]{2,1,0:T(8,128)(2,1)S(1)} %collective-permute-done.2.refs_2_), channel_id=1, source_target_pairs={{0,1},{1,0},{2,3},{3,2},{4,5},{5,4},{6,7},{7,6},{8,9},{9,8},{10,11... | collective-permute-start | bytes 2359304 | tf_op jit(solution)/shard_map/ppermute | solution.py:238
  60.8 6.2 %copy-start.4 = (bf16[3,256,512]{2,1,0:T(8,128)(2,1)}, bf16[3,256,512]{2,1,0:T(8,128)(2,1)S(1)}, u32[]{:S(2)}) copy-start(bf16[3,256,512]{2,1,0:T(8,128)(2,1)S(1)} %collective-permute-done.4.refs_4_) | copy-start | bytes 2359300
  60.8 6.2 %collective-permute-start.5 = (bf16[3,256,512]{2,1,0:T(8,128)(2,1)S(1)}, bf16[3,256,512]{2,1,0:T(8,128)(2,1)S(1)}, u32[]{:S(2)}, u32[]{:S(2)}) collective-permute-start(bf16[3,256,512]{2,1,0:T(8,128)(2,1)S(1)} %collective-permute-done.4.refs_4_), channel_id=1, source_target_pairs={{0,1},{1,0},{2,3},{3,2},{4,5},{5,4},{6,7},{7,6},{8,9},{9,8},{10,11... | collective-permute-start | bytes 2359304 | tf_op jit(solution)/shard_map/ppermute | solution.py:238
  63.3 3.7 %copy-start.5 = (bf16[3,256,512]{2,1,0:T(8,128)(2,1)}, bf16[3,256,512]{2,1,0:T(8,128)(2,1)S(1)}, u32[]{:S(2)}) copy-start(bf16[3,256,512]{2,1,0:T(8,128)(2,1)S(1)} %collective-permute-done.6.refs_6_) | copy-start | bytes 2359300
  63.3 5.7 %collective-permute-start.7 = (bf16[3,256,512]{2,1,0:T(8,128)(2,1)S(1)}, bf16[3,256,512]{2,1,0:T(8,128)(2,1)}, u32[]{:S(2)}, u32[]{:S(2)}) collective-permute-start(bf16[3,256,512]{2,1,0:T(8,128)(2,1)S(1)} %collective-permute-done.6.refs_6_), channel_id=1, source_target_pairs={{0,1},{1,0},{2,3},{3,2},{4,5},{5,4},{6,7},{7,6},{8,9},{9,8},{10,11... | collective-permute-start | bytes 2359304 | tf_op jit(solution)/shard_map/ppermute | solution.py:238
  67.0 0.9 copy-start.6
  67.0 1.1 copy-start.7
  68.1 0.9 copy-start.8
  69.1 1.3 copy-start
  94.2 35.3 %all-to-all-start.1 = ((bf16[32,64,512]{2,1,0:T(8,128)(2,1)}), bf16[32,64,512]{2,1,0:T(8,128)(2,1)S(1)}, u32[]{:S(2)}, u32[]{:S(2)}) async-start(bf16[32,64,512]{2,1,0:T(8,128)(2,1)} %bitcast.10), calls=%async_computation.1 | async-start | bytes 4194304 | tf_op jit(solution)/shard_map/all_to_all | solution.py:245
  129.5 1.3 copy-start.1

commit v2 on v1

v2 whole, which is shorter than its diff:
```python
import functools

import jax
import jax.numpy as jnp
from jax import lax
from jax.experimental import pallas as pl
from jax.experimental.pallas import tpu as pltpu
from jax.sharding import PartitionSpec as P

F32 = jnp.float32
BF16 = jnp.bfloat16
VMEM_LIMIT = 56 * 1024 * 1024


def dot(a, b):
    return jnp.dot(a, b, preferred_element_type=F32)


def swish(gate, up):
    half = 0.5 * gate
    return ((half + half * jnp.tanh(half)) * up).astype(BF16)


def pack_kernel(half, place, gate, up, down, *sends):
    for r, send in enumerate(sends):
        pick = place[0] ^ r
        expert, part = pick // 2, pick % 2
        cols = pl.ds(pl.multiple_of(part * half, half), half)
        for n, w in enumerate((gate, up)):
            send[n, :, :half] = w[expert, :half, cols]
            send[n, :, half:] = w[expert, half:, cols]
        send[2] = down[expert, cols, :]


def pack(gate, up, down, place):
    _, width, hidden = gate.shape
    half = hidden // 2
    shape = jax.ShapeDtypeStruct((3, half, width), BF16)
    return pl.pallas_call(
        functools.partial(pack_kernel, half),
        out_shape=[shape] * 4,
        in_specs=[pl.BlockSpec(memory_space=pltpu.SMEM)] + [pl.BlockSpec(memory_space=pltpu.VMEM)] * 3,
        out_specs=[pl.BlockSpec(memory_space=pltpu.VMEM)] * 4,
        compiler_params=pltpu.CompilerParams(vmem_limit_bytes=VMEM_LIMIT),
        cost_estimate=pl.CostEstimate(flops=0, bytes_accessed=6 * gate.size * 2, transcendentals=0),
    )(place, gate, up, down)


def route_kernel(block, cap, stack, plane, tokens, gain, routes, after, outgoing, normed, position, chosen):
    step = pl.program_id(0)
    rows, width = tokens.shape
    experts = chosen.shape[0]
    columns = experts // stack
    per = outgoing.shape[0] // cap

    @pl.when(step == 0)
    def _():
        earlier = (
            lax.broadcasted_iota(jnp.int32, (block, block), 0) < lax.broadcasted_iota(jnp.int32, (block, block), 1)
        ).astype(F32).astype(BF16)
        m = lax.broadcasted_iota(jnp.int32, (experts, block), 0)
        name = (m % columns) * stack + m // columns
        base = (m * cap).astype(F32)
        seen = jnp.zeros((experts, 1), F32)
        for b in range(rows // block):
            at = pl.ds(b * block, block)
            first = routes[0:1, at] == name
            second = routes[1:2, at] == name
            named = jnp.where(first | second, 1.0, 0.0).astype(F32)
            rank = dot(named.astype(BF16), earlier) + seen
            chosen[:, at] = jnp.where(first | second, rank, -1.0)
            seen = seen + jnp.sum(named, axis=1, keepdims=True)
            slot = rank + base
            position[0:1, at] = jnp.max(jnp.where(first, slot, -1.0), axis=0, keepdims=True)
            position[1:2, at] = jnp.max(jnp.where(second, slot, -1.0), axis=0, keepdims=True)
            values = tokens[at, :].astype(F32)
            scale = lax.rsqrt(jnp.mean(values * values, axis=-1, keepdims=True) + 1e-05)
            normed[at, :] = (values * scale * gain[...]).astype(BF16)

    ranks = lax.broadcasted_iota(jnp.int32, (cap, rows), 0).astype(F32)
    start = plane[0] * columns + step * per
    masks = [jnp.where(ranks == chosen[pl.ds(start + i, 1), :], 1.0, 0.0).astype(BF16) for i in range(per)]
    outgoing[...] = dot(jnp.concatenate(masks, axis=0), normed[...]).astype(BF16)


def route(tokens, gain, routes, plane, experts, cap, stack, after):
    rows, width = tokens.shape
    slots = experts // stack * cap
    block, per = 256, 4 * cap
    return pl.pallas_call(
        functools.partial(route_kernel, block, cap, stack),
        grid=(slots // per,),
        out_shape=[
            jax.ShapeDtypeStruct((slots, width), BF16),
            jax.ShapeDtypeStruct((rows, width), BF16),
            jax.ShapeDtypeStruct((2, rows), F32),
        ],
        in_specs=[
            pl.BlockSpec(memory_space=pltpu.SMEM),
            pl.BlockSpec((rows, width), lambda i: (0, 0)),
            pl.BlockSpec((1, width), lambda i: (0, 0)),
            pl.BlockSpec((2, rows), lambda i: (0, 0)),
            pl.BlockSpec(memory_space=pl.ANY),
        ],
        out_specs=[
            pl.BlockSpec((per, width), lambda i: (i, 0)),
            pl.BlockSpec((rows, width), lambda i: (0, 0)),
            pl.BlockSpec((2, rows), lambda i: (0, 0)),
        ],
        scratch_shapes=[pltpu.VMEM((experts, rows), F32)],
        compiler_params=pltpu.CompilerParams(vmem_limit_bytes=VMEM_LIMIT),
        cost_estimate=pl.CostEstimate(
            flops=2 * slots * rows * width, bytes_accessed=6 * rows * width + 2 * slots * width, transcendentals=rows
        ),
    )(plane, tokens, gain, routes, after)


def split_columns(out, values):
    part = out.shape[2]
    for q in range(out.shape[0]):
        out[q] = values[:, q * part : (q + 1) * part]


def shared_kernel(normed, gate, up, down, *rest):
    out = rest[-1]
    x = normed[...]
    split_columns(out, dot(swish(dot(x, gate[...]), dot(x, up[...])), down[...]).astype(BF16))


def shared_expert(normed, gate, up, down, planes, after):
    rows, width = normed.shape
    hidden = gate.shape[1]
    block = 512
    whole = [pl.BlockSpec(w.shape, lambda i: (0, 0)) for w in (gate, up, down)]
    return pl.pallas_call(
        shared_kernel,
        grid=(rows // block,),
        out_shape=jax.ShapeDtypeStruct((planes, rows, width // planes), BF16),
        in_specs=[pl.BlockSpec((block, width), lambda i: (i, 0))] + whole + [pl.BlockSpec(memory_space=pl.ANY)] * len(after),
        out_specs=pl.BlockSpec((planes, block, width // planes), lambda i: (0, i, 0)),
        compiler_params=pltpu.CompilerParams(vmem_limit_bytes=VMEM_LIMIT),
        cost_estimate=pl.CostEstimate(
            flops=60 * rows * width * hidden, bytes_accessed=4 * rows * width, transcendentals=rows * hidden
        ),
    )(normed, gate, up, down, *after)


def expert_kernel(slots, after, *refs):
    weights, (out, w_gate, w_up, w_down, hidden) = refs[:-5], refs[-5:]
    half = slots.shape[1] // 2

    @pl.when(pl.program_id(0) == 0)
    def _():
        for n, w in enumerate(weights):
            at = pl.ds(n * half, half)
            for whole, part in ((w_gate, 0), (w_up, 1)):
                whole[:half, at] = w[part, :, :half]
                whole[half:, at] = w[part, :, half:]
            w_down[at, :] = w[2]

    x = slots[...]
    step = 512
    for n in range(hidden.shape[1] // step):
        at = pl.ds(n * step, step)
        hidden[:, at] = swish(dot(x, w_gate[:, at]), dot(x, w_up[:, at]))
    split_columns(out, dot(hidden[...], w_down[...]).astype(BF16))


def expert(slots, weights, planes, after):
    rows, width = slots.shape
    block = 512
    hidden = sum(w.shape[1] for w in weights)
    return pl.pallas_call(
        expert_kernel,
        grid=(rows // block,),
        out_shape=jax.ShapeDtypeStruct((planes, rows, width // planes), BF16),
        in_specs=[pl.BlockSpec((block, width), lambda i: (i, 0)), pl.BlockSpec(memory_space=pl.ANY)]
        + [pl.BlockSpec(w.shape, lambda i: (0, 0, 0)) for w in weights],
        out_specs=pl.BlockSpec((planes, block, width // planes), lambda i: (0, i, 0)),
        scratch_shapes=[
            pltpu.VMEM((width, hidden), BF16),
            pltpu.VMEM((width, hidden), BF16),
            pltpu.VMEM((hidden, width), BF16),
            pltpu.VMEM((block, hidden), BF16),
        ],
        compiler_params=pltpu.CompilerParams(vmem_limit_bytes=VMEM_LIMIT),
        cost_estimate=pl.CostEstimate(
            flops=6 * rows * width * hidden, bytes_accessed=4 * rows * width + 6 * width * hidden,
            transcendentals=rows * hidden,
        ),
    )(slots, after, *weights)


def combine_kernel(position, gates, back, shared, out, table, total):
    step = pl.program_id(0)
    chunk = back.shape[0]
    rows = out.shape[0]
    block = 512

    @pl.when(step == 0)
    def _():
        for b in range(rows // block):
            at = pl.ds(b * block, block)
            columns = jnp.concatenate([position[:, at], gates[:, at], jnp.zeros((4, block), F32)], axis=0).T
            for n in range(4):
                table[n, at, :] = jnp.broadcast_to(columns[:, n : n + 1], (block, 128))
            total[at, :] = sum(shared[q, at, :].astype(F32) for q in range(shared.shape[0]))

    lane = lax.broadcasted_iota(jnp.int32, (block, 128), 1).astype(F32)
    low = (step * chunk).astype(F32)
    for b in range(rows // block):
        at = pl.ds(b * block, block)
        first, second = table[0, at, :] - low, table[1, at, :] - low
        gate, other = table[2, at, :], table[3, at, :]
        weight = [
            jnp.where(lane + j * 128 == first, gate, jnp.where(lane + j * 128 == second, other, 0.0)).astype(BF16)
            for j in range(chunk // 128)
        ]
        total[at, :] += dot(jnp.concatenate(weight, axis=1), back[...])

    @pl.when(step == pl.num_programs(0) - 1)
    def _():
        out[...] = total[...].astype(BF16)


def combine(position, gates, back, shared):
    planes, rows, part = shared.shape
    slots = back.shape[0]
    chunk = 1024
    return pl.pallas_call(
        combine_kernel,
        grid=(slots // chunk,),
        out_shape=jax.ShapeDtypeStruct((rows, part), BF16),
        in_specs=[
            pl.BlockSpec((2, rows), lambda i: (0, 0)),
            pl.BlockSpec((2, rows), lambda i: (0, 0)),
            pl.BlockSpec((chunk, part), lambda i: (i, 0)),
            pl.BlockSpec((planes, rows, part), lambda i: (0, 0, 0)),
        ],
        out_specs=pl.BlockSpec((rows, part), lambda i: (0, 0)),
        scratch_shapes=[pltpu.VMEM((4, rows, 128), F32), pltpu.VMEM((rows, part), F32)],
        compiler_params=pltpu.CompilerParams(vmem_limit_bytes=VMEM_LIMIT),
        cost_estimate=pl.CostEstimate(
            flops=2 * rows * slots * part, bytes_accessed=10 * rows * part + 2 * slots * part, transcendentals=0
        ),
    )(position, gates, back, shared)


def per_device(
    tokens,
    norm_gain,
    routes,
    gates,
    expert_gate,
    expert_up,
    expert_down,
    shared_gate,
    shared_up,
    shared_down,
):
    rows, width = tokens.shape
    planes, sectors = lax.axis_size("expert"), lax.axis_size("sector")
    columns = sectors // 2
    cap = 128
    both = ("expert", "sector")
    z = lax.axis_index("expert").astype(jnp.int32).reshape(1)

    sends = pack(expert_gate, expert_up, expert_down, z)
    weights = []
    for r, send in enumerate(sends):
        moves = []
        for source in range(planes):
            for s in range(sectors):
                pick = source ^ r
                target = 2 * (s % 2) + pick // 2
                moves.append((source * sectors + s, target * sectors + (s // 2) * 2 + pick % 2))
        half = lax.ppermute(send, both, moves)
        other = lax.ppermute(half, "sector", [(s, s ^ 1) for s in range(sectors)])
        weights += [half, other]

    outgoing, normed, position = route(
        tokens, norm_gain.reshape(1, width), routes.T, z, columns * planes, cap, planes, sends[-1]
    )
    slots = lax.all_to_all(outgoing.reshape(sectors, -1, width), "sector", 0, 0, tiled=True)
    shared = shared_expert(normed, shared_gate, shared_up, shared_down, planes, weights[::2])
    shared_parts = lax.psum_scatter(shared, "expert", scatter_dimension=0, tiled=True)
    results = expert(slots.reshape(-1, width), weights, planes, shared)
    part = width // planes
    back = lax.all_to_all(results.reshape(planes * sectors, -1, part), both, 0, 0, tiled=True)
    return combine(position, gates.T, back.reshape(-1, part), shared_parts)


def solution(mesh):
    in_specs = (
        P("sector", None),
        P(),
        P("sector", None),
        P("sector", None),
        P("sector", None, "expert"),
        P("sector", None, "expert"),
        P("sector", "expert", None),
        P(None, "expert"),
        P(None, "expert"),
        P("expert", None),
    )
    out_specs = P("sector", "expert")
    return jax.shard_map(
        per_device, mesh=mesh, in_specs=in_specs, out_specs=out_specs, check_vma=False
    )
```

time: 173 us -> 158 us (0.913)
  waiting for transfers between devices: 50.8 us -> 21.9 us
  between operations: 0.11 us -> 13.5 us
  blocking collectives: 27.6 us -> 37.5 us
  starting transfers between devices: 29.5 us -> 21.8 us
  Pallas kernels: 56.6 us -> 58.8 us
    all_to_all x1 -> x0, waiting for transfers between devices: 18.7 us -> none  [per_device(): lax.all_to_all(results.reshape(sectors, -1, width), 'sector', 0, 0, tiled...]
    ppermute x4, waiting for transfers between devices: 32.1 us -> 16.9 us  [per_device(): half = lax.ppermute(send, both, moves)]
    all_to_all x1, blocking collectives: 27.6 us -> 37.5 us  [per_device(): lax.all_to_all(results.reshape(planes * sectors, -1, part), both, 0, 0, t...]
    pallas_call x1, Pallas kernels: 10.8 us -> 20.1 us  [combine(): pl.pallas_call(combine_kernel, grid=(slots // chunk,), out_shape=jax.Shap...]
    all_to_all x1 -> x0, starting transfers between devices: 7.47 us -> none  [per_device(): lax.all_to_all(results.reshape(sectors, -1, width), 'sector', 0, 0, tiled...]
    ppermute x4, waiting for transfers between devices: 0.01 us -> 4.98 us  [per_device(): other = lax.ppermute(half, 'sector', [(s, s ^ 1) for s in range(sectors)])]
    pallas_call x1, Pallas kernels: 23.8 us -> 19.5 us  [expert(): pl.pallas_call(expert_kernel, grid=(rows // block,), out_shape=jax.ShapeD...]
    pallas_call x1, Pallas kernels: 9.11 us -> 6.88 us  [shared_expert(): pl.pallas_call(shared_kernel, grid=(rows // block,), out_shape=jax.ShapeD...]
  transfers between devices with their start and end apart: 10 -> 10, of which waited for: 4 -> 5; matrix products, arithmetic and copies ran while one was open for 0% -> 0% of each run, Pallas kernels for 8% -> 22%
where the time goes in v2:
time: 158 us; the launch traced here: 157 us
  Pallas kernels  58.8 us (37%)
  blocking collectives  37.5 us (24%)
  waiting for transfers between devices  21.9 us (14%)
  starting transfers between devices  21.8 us (14%)
  between operations  13.5 us (9%)
  local copies, waits for them, and re-layouts  3.35 us (2%)
    all_to_all x1, blocking collectives, per_device(): lax.all_to_all(results.reshape(planes * sectors, -1, part), both, 0, 0, t...  37.5 us
    pallas_call x1, Pallas kernels, combine(): pl.pallas_call(combine_kernel, grid=(slots // chunk,), out_shape=jax.Shap...  20.1 us
    pallas_call x1, Pallas kernels, expert(): pl.pallas_call(expert_kernel, grid=(rows // block,), out_shape=jax.ShapeD...  19.5 us
    ppermute x4, waiting for transfers between devices, per_device(): half = lax.ppermute(send, both, moves)  16.9 us
    ppermute x4, starting transfers between devices, per_device(): half = lax.ppermute(send, both, moves)  10.6 us
    pallas_call x1, Pallas kernels, route(): pl.pallas_call(functools.partial(route_kernel, block, cap, stack), grid=(...  8.65 us
    all_to_all x1, starting transfers between devices, per_device(): lax.all_to_all(outgoing.reshape(sectors, -1, width), 'sector', 0, 0, tile...  7.2 us
    pallas_call x1, Pallas kernels, shared_expert(): pl.pallas_call(shared_kernel, grid=(rows // block,), out_shape=jax.ShapeD...  6.88 us
  transfers between devices with their start and end apart: 10, of which 5 were waited for; matrix products, arithmetic and copies ran while one was open for 0% of the time, Pallas kernels for 22%

profile of v2, /device:TPU:1, one launch (start us, length us, event | category | flops | bytes accessed | tf_op | source)
XLA Modules:
  0.0 156.8 jit_solution(8775283174231102421)
XLA Ops:
  6.5 3.7 %shard_map.100 = (bf16[3,256,512]{2,1,0:T(8,128)(2,1)}, bf16[3,256,512]{2,1,0:T(8,128)(2,1)}, bf16[3,256,512]{2,1,0:T(8,128)(2,1)}, bf16[3,256,512]{2,1,0:T(8,128)(2,1)}) custom-call(s32[1]{0:T(128)} %bitcast.place.plane, bf16[2,512,512]{2,1,0:T(8,128)(2,1)} %gate.2, bf16[2,512,512]{2,1,0:T(8,128)(2,1)} %up.2, bf16[2,512,512]{2,1,0:T(8,128)(2,1)} %down.2), custom_call_target="tpu_custom_call" | custom-call | bytes 6291456 | tf_op jit(solution)/shard_map/pallas_call | solution.py:39
  10.2 6.9 %collective-permute-start = (bf16[3,256,512]{2,1,0:T(8,128)(2,1)}, bf16[3,256,512]{2,1,0:T(8,128)(2,1)S(1)}, u32[]{:S(2)}, u32[]{:S(2)}) collective-permute-start(bf16[3,256,512]{2,1,0:T(8,128)(2,1)} %get-tuple-element.16), channel_id=1, source_target_pairs={{0,0},{1,64},{2,2},{3,66},{4,4},{5,68},{6,6},{7,70},{8,8},{9,72},{... | collective-permute-start | bytes 2359304 | tf_op jit(solution)/shard_map/ppermute | solution.py:277
  17.1 1.4 collective-permute-start.1
  18.5 0.0 collective-permute-start.2
  18.5 2.3 %collective-permute-start.3 = (bf16[3,256,512]{2,1,0:T(8,128)(2,1)}, bf16[3,256,512]{2,1,0:T(8,128)(2,1)}, u32[]{:S(2)}, u32[]{:S(2)}) collective-permute-start(bf16[3,256,512]{2,1,0:T(8,128)(2,1)} %get-tuple-element.12.after), channel_id=1, source_target_pairs={{0,33},{1,97},{2,35},{3,99},{4,37},{5,101},{6,39},{7,103},{8,41},{... | collective-permute-start | bytes 2359304 | tf_op jit(solution)/shard_map/ppermute | solution.py:277
  20.8 8.7 %shard_map.101 = (bf16[2048,512]{1,0:T(8,128)(2,1)}, bf16[2048,512]{1,0:T(8,128)(2,1)}, f32[2,2048]{1,0:T(2,128)}) custom-call(s32[1]{0:T(128)} %bitcast.place.plane, bf16[2048,512]{1,0:T(8,128)(2,1)} %tokens.1, f32[1,512]{1,0:T(1,128)} %bitcast.14, s32[2,2048]{1,0:T(2,128)} %bitcast.12, bf16[3,256,512]{2,1,0:T(8,128)(2,1)} %get-tuple-element.12.after), custom_call_target="tpu_custom_call" | custom-call | flops 4294967296 | bytes 8388608 | tf_op jit(solution)/shard_map/pallas_call | solution.py:90
  29.5 7.2 %all-to-all-start = ((bf16[32,64,512]{2,1,0:T(8,128)(2,1)}), bf16[32,64,512]{2,1,0:T(8,128)(2,1)S(1)}, u32[]{:S(2)}, u32[]{:S(2)}) async-start(bf16[32,64,512]{2,1,0:T(8,128)(2,1)} %bitcast.9), calls=%async_computation | async-start | bytes 4194304 | tf_op jit(solution)/shard_map/all_to_all | solution.py:284
  36.7 0.0 reduce-scatter.2.cloned.1.call-start
  36.7 0.0 collective-permute-done.rest_0_.refs_0_
  36.7 0.0 copy-start.1
  36.7 14.1 %collective-permute-done.1.rest_1_.refs_2_ = bf16[3,256,512]{2,1,0:T(8,128)(2,1)} collective-permute-done((bf16[3,256,512]{2,1,0:T(8,128)(2,1)}, bf16[3,256,512]{2,1,0:T(8,128)(2,1)}, u32[]{:S(2)}, u32[]{:S(2)}) %collective-permute-start.1) | collective-permute-done | bytes 786464 | tf_op jit(solution)/shard_map/ppermute | solution.py:277
  50.8 0.0 collective-permute-done.2.rest_2_.refs_4_
  50.9 2.8 %collective-permute-done.3.rest_3_.refs_6_ = bf16[3,256,512]{2,1,0:T(8,128)(2,1)} collective-permute-done((bf16[3,256,512]{2,1,0:T(8,128)(2,1)}, bf16[3,256,512]{2,1,0:T(8,128)(2,1)}, u32[]{:S(2)}, u32[]{:S(2)}) %collective-permute-start.3) | collective-permute-done | bytes 786464 | tf_op jit(solution)/shard_map/ppermute | solution.py:277
  53.6 0.0 copy-done.1
  53.6 6.9 %shard_map.102.after = bf16[4,2048,128]{2,1,0:T(8,128)(2,1)} custom-call(bf16[2048,512]{1,0:T(8,128)(2,1)} %get-tuple-element.15.normed, bf16[512,512]{1,0:T(8,128)(2,1)} %gate.3, bf16[512,512]{1,0:T(8,128)(2,1)} %up.3, bf16[512,512]{1,0:T(8,128)(2,1)} %down.3, bf16[3,256,512]{2,1,0:T(8,128)(2,1)} %copy-done.1, ...), custom_call_target="tpu_custom_call" | custom-call | flops 32212254720 | bytes 4194304 | tf_op jit(solution)/shard_map/pallas_call | solution.py:135
  60.5 0.0 reduce-scatter.2.cloned.1.call-update
  60.5 1.1 copy-done.2
  61.7 3.5 %collective-permute-start.4 = (bf16[3,256,512]{2,1,0:T(8,128)(2,1)S(1)}, bf16[3,256,512]{2,1,0:T(8,128)(2,1)S(1)}, u32[]{:S(2)}, u32[]{:S(2)}) collective-permute-start(bf16[3,256,512]{2,1,0:T(8,128)(2,1)S(1)} %copy-done.2), channel_id=1, source_target_pairs={{0,1},{1,0},{2,3},{3,2},{4,5},{5,4},{6,7},{7,6},{8,9},{9,8},{10,11... | collective-permute-start | bytes 2359304 | tf_op jit(solution)/shard_map/ppermute | solution.py:278
  65.2 0.0 collective-permute-start.5
  65.2 0.5 collective-permute-start.6
  65.7 0.0 collective-permute-start.7
  65.7 2.5 %collective-permute-done.4.refs_1_ = bf16[3,256,512]{2,1,0:T(8,128)(2,1)S(1)} collective-permute-done((bf16[3,256,512]{2,1,0:T(8,128)(2,1)S(1)}, bf16[3,256,512]{2,1,0:T(8,128)(2,1)S(1)}, u32[]{:S(2)}, u32[]{:S(2)}) %collective-permute-start.4) | collective-permute-done | bytes 786464 | tf_op jit(solution)/shard_map/ppermute | solution.py:278
  68.2 1.2 collective-permute-done.5.refs_3_
  69.4 1.3 collective-permute-done.6.refs_5_
  70.7 0.0 copy-done.3
  70.7 0.9 copy-done.5
  71.5 0.0 collective-permute-done.7.refs_7_
  71.5 0.0 all-to-all-done
  71.6 1.4 copy-done
  72.9 19.5 %shard_map.103 = bf16[4,2048,128]{2,1,0:T(8,128)(2,1)} custom-call(bf16[2048,512]{1,0:T(8,128)(2,1)} %bitcast.8, bf16[4,2048,128]{2,1,0:T(8,128)(2,1)} %shard_map.102.after, bf16[3,256,512]{2,1,0:T(8,128)(2,1)} %copy-done.1, bf16[3,256,512]{2,1,0:T(8,128)(2,1)} %copy-done.3, bf16[3,256,512]{2,1,0:T(8,128)(2,1)} %collective-permute-done.1.rest_1_.refs_2_, ...), custom_call_target="tpu_custom_call" | custom-call | flops 12884901888 | bytes 10485760 | tf_op jit(solution)/shard_map/pallas_call | solution.py:173
  92.4 37.5 %all_to_all.10 = bf16[128,64,128]{2,1,0:T(8,128)(2,1)} all-to-all(bf16[128,64,128]{2,1,0:T(8,128)(2,1)} %bitcast.10), channel_id=1, replica_groups=mesh['expert'=4,'sector'=32] {'expert','sector'}, dimensions={0} | all-to-all | bytes 4194304 | tf_op jit(solution)/shard_map/all_to_all | solution.py:289
  129.9 20.1 %shard_map.104 = bf16[2048,128]{1,0:T(8,128)(2,1)} custom-call(f32[2,2048]{1,0:T(2,128)} %get-tuple-element.13.position, f32[2,2048]{1,0:T(2,128)} %bitcast.13, bf16[8192,128]{1,0:T(8,128)(2,1)} %bitcast.11, bf16[1,2048,128]{2,1,0:T(8,128)(2,1)} %reduce-scatter.2.cloned.1.call-done.shared), custom_call_target="tpu_custom_call" | custom-call | flops 4294967296 | bytes 4718592 | tf_op jit(solution)/shard_map/pallas_call | solution.py:230
  (7 shorter events, 0.0 us)
Async XLA Ops:
  10.2 26.5 %collective-permute-start = (bf16[3,256,512]{2,1,0:T(8,128)(2,1)}, bf16[3,256,512]{2,1,0:T(8,128)(2,1)S(1)}, u32[]{:S(2)}, u32[]{:S(2)}) collective-permute-start(bf16[3,256,512]{2,1,0:T(8,128)(2,1)} %get-tuple-element.16), channel_id=1, source_target_pairs={{0,0},{1,64},{2,2},{3,66},{4,4},{5,68},{6,6},{7,70},{8,8},{9,72},{... | collective-permute-start | bytes 2359304 | tf_op jit(solution)/shard_map/ppermute | solution.py:277
  17.1 33.7 %collective-permute-start.1 = (bf16[3,256,512]{2,1,0:T(8,128)(2,1)}, bf16[3,256,512]{2,1,0:T(8,128)(2,1)}, u32[]{:S(2)}, u32[]{:S(2)}) collective-permute-start(bf16[3,256,512]{2,1,0:T(8,128)(2,1)} %get-tuple-element.17), channel_id=1, source_target_pairs={{0,1},{1,65},{2,3},{3,67},{4,5},{5,69},{6,7},{7,71},{8,9},{9,73},{... | collective-permute-start | bytes 2359304 | tf_op jit(solution)/shard_map/ppermute | solution.py:277
  18.5 32.3 %collective-permute-start.2 = (bf16[3,256,512]{2,1,0:T(8,128)(2,1)}, bf16[3,256,512]{2,1,0:T(8,128)(2,1)}, u32[]{:S(2)}, u32[]{:S(2)}) collective-permute-start(bf16[3,256,512]{2,1,0:T(8,128)(2,1)} %get-tuple-element.18), channel_id=1, source_target_pairs={{0,32},{1,96},{2,34},{3,98},{4,36},{5,100},{6,38},{7,102},{8,40},{... | collective-permute-start | bytes 2359304 | tf_op jit(solution)/shard_map/ppermute | solution.py:277
  18.5 35.1 %collective-permute-start.3 = (bf16[3,256,512]{2,1,0:T(8,128)(2,1)}, bf16[3,256,512]{2,1,0:T(8,128)(2,1)}, u32[]{:S(2)}, u32[]{:S(2)}) collective-permute-start(bf16[3,256,512]{2,1,0:T(8,128)(2,1)} %get-tuple-element.12.after), channel_id=1, source_target_pairs={{0,33},{1,97},{2,35},{3,99},{4,37},{5,101},{6,39},{7,103},{8,41},{... | collective-permute-start | bytes 2359304 | tf_op jit(solution)/shard_map/ppermute | solution.py:277
  29.5 42.1 %all-to-all-start = ((bf16[32,64,512]{2,1,0:T(8,128)(2,1)}), bf16[32,64,512]{2,1,0:T(8,128)(2,1)S(1)}, u32[]{:S(2)}, u32[]{:S(2)}) async-start(bf16[32,64,512]{2,1,0:T(8,128)(2,1)} %bitcast.9), calls=%async_computation | async-start | bytes 4194304 | tf_op jit(solution)/shard_map/all_to_all | solution.py:284
  36.7 93.2 %reduce-scatter.2.cloned.1.call-start = ((), (), s32[]{:S(2)}) async-start(), calls=%async_computation.3 | async-start | bytes 2621440 | tf_op jit(solution)/shard_map/reduce_scatter | solution.py:286
  36.7 16.9 %copy-start.1 = (bf16[3,256,512]{2,1,0:T(8,128)(2,1)}, bf16[3,256,512]{2,1,0:T(8,128)(2,1)S(1)}, u32[]{:S(2)}) copy-start(bf16[3,256,512]{2,1,0:T(8,128)(2,1)S(1)} %collective-permute-done.rest_0_.refs_0_) | copy-start | bytes 2359300
  60.5 1.1 copy-start.2
  61.7 6.5 %collective-permute-start.4 = (bf16[3,256,512]{2,1,0:T(8,128)(2,1)S(1)}, bf16[3,256,512]{2,1,0:T(8,128)(2,1)S(1)}, u32[]{:S(2)}, u32[]{:S(2)}) collective-permute-start(bf16[3,256,512]{2,1,0:T(8,128)(2,1)S(1)} %copy-done.2), channel_id=1, source_target_pairs={{0,1},{1,0},{2,3},{3,2},{4,5},{5,4},{6,7},{7,6},{8,9},{9,8},{10,11... | collective-permute-start | bytes 2359304 | tf_op jit(solution)/shard_map/ppermute | solution.py:278
  65.2 4.2 %collective-permute-start.5 = (bf16[3,256,512]{2,1,0:T(8,128)(2,1)}, bf16[3,256,512]{2,1,0:T(8,128)(2,1)S(1)}, u32[]{:S(2)}, u32[]{:S(2)}) collective-permute-start(bf16[3,256,512]{2,1,0:T(8,128)(2,1)} %collective-permute-done.1.rest_1_.refs_2_), channel_id=1, source_target_pairs={{0,1},{1,0},{2,3},{3,2},{4,5},{5,4},{6,7},{7,6},{8,9},{9,8},{10,11... | collective-permute-start | bytes 2359304 | tf_op jit(solution)/shard_map/ppermute | solution.py:278
  65.2 5.5 %collective-permute-start.6 = (bf16[3,256,512]{2,1,0:T(8,128)(2,1)}, bf16[3,256,512]{2,1,0:T(8,128)(2,1)S(1)}, u32[]{:S(2)}, u32[]{:S(2)}) collective-permute-start(bf16[3,256,512]{2,1,0:T(8,128)(2,1)} %collective-permute-done.2.rest_2_.refs_4_), channel_id=1, source_target_pairs={{0,1},{1,0},{2,3},{3,2},{4,5},{5,4},{6,7},{7,6},{8,9},{9,8},{10,11... | collective-permute-start | bytes 2359304 | tf_op jit(solution)/shard_map/ppermute | solution.py:278
  65.7 5.9 %collective-permute-start.7 = (bf16[3,256,512]{2,1,0:T(8,128)(2,1)}, bf16[3,256,512]{2,1,0:T(8,128)(2,1)}, u32[]{:S(2)}, u32[]{:S(2)}) collective-permute-start(bf16[3,256,512]{2,1,0:T(8,128)(2,1)} %collective-permute-done.3.rest_3_.refs_6_), channel_id=1, source_target_pairs={{0,1},{1,0},{2,3},{3,2},{4,5},{5,4},{6,7},{7,6},{8,9},{9,8},{10,11... | collective-permute-start | bytes 2359304 | tf_op jit(solution)/shard_map/ppermute | solution.py:278
  68.2 2.5 %copy-start.3 = (bf16[3,256,512]{2,1,0:T(8,128)(2,1)}, bf16[3,256,512]{2,1,0:T(8,128)(2,1)S(1)}, u32[]{:S(2)}) copy-start(bf16[3,256,512]{2,1,0:T(8,128)(2,1)S(1)} %collective-permute-done.4.refs_1_) | copy-start | bytes 2359300
  69.4 1.3 copy-start.4
  70.7 0.9 copy-start.5
  71.5 1.4 copy-start
Sparse Core Ops, SparseCore 0:
  60.7 31.6 reduce-scatter.1

commit v3 on v2

--- a/solution.py
+++ b/solution.py
@@ -121,28 +121,34 @@
         out[q] = values[:, q * part : (q + 1) * part]
 
 
-def shared_kernel(normed, gate, up, down, *rest):
-    out = rest[-1]
+def shared_kernel(plane, normed, gate, up, down, *rest):
+    outs, total = rest[:-1], rest[-1]
     x = normed[...]
-    split_columns(out, dot(swish(dot(x, gate[...]), dot(x, up[...])), down[...]).astype(BF16))
-
-
-def shared_expert(normed, gate, up, down, planes, after):
+    total[...] = dot(swish(dot(x, gate[...]), dot(x, up[...])), down[...])
+    planes, part = len(outs), outs[0].shape[1]
+    for k, out in enumerate(outs):
+        target = (plane[0] + k) % planes
+        out[...] = total[:, pl.ds(pl.multiple_of(target * part, part), part)].astype(BF16)
+
+
+def shared_expert(normed, gate, up, down, plane, planes):
     rows, width = normed.shape
     hidden = gate.shape[1]
     block = 512
+    part = width // planes
     whole = [pl.BlockSpec(w.shape, lambda i: (0, 0)) for w in (gate, up, down)]
     return pl.pallas_call(
         shared_kernel,
         grid=(rows // block,),
-        out_shape=jax.ShapeDtypeStruct((planes, rows, width // planes), BF16),
-        in_specs=[pl.BlockSpec((block, width), lambda i: (i, 0))] + whole + [pl.BlockSpec(memory_space=pl.ANY)] * len(after),
-        out_specs=pl.BlockSpec((planes, block, width // planes), lambda i: (0, i, 0)),
+        out_shape=[jax.ShapeDtypeStruct((rows, part), BF16)] * planes,
+        in_specs=[pl.BlockSpec(memory_space=pltpu.SMEM), pl.BlockSpec((block, width), lambda i: (i, 0))] + whole,
+        out_specs=[pl.BlockSpec((block, part), lambda i: (i, 0))] * planes,
+        scratch_shapes=[pltpu.VMEM((block, width), F32)],
         compiler_params=pltpu.CompilerParams(vmem_limit_bytes=VMEM_LIMIT),
         cost_estimate=pl.CostEstimate(
             flops=60 * rows * width * hidden, bytes_accessed=4 * rows * width, transcendentals=rows * hidden
         ),
-    )(normed, gate, up, down, *after)
+    )(plane, normed, gate, up, down)
 
 
 def expert_kernel(slots, after, *refs):
@@ -191,7 +197,23 @@
     )(slots, after, *weights)
 
 
-def combine_kernel(position, gates, back, shared, out, table, total):
+def hold_kernel(*refs):
+    pass
+
+
+def hold(array, *others):
+    anywhere = pl.BlockSpec(memory_space=pl.ANY)
+    return pl.pallas_call(
+        hold_kernel,
+        out_shape=jax.ShapeDtypeStruct(array.shape, array.dtype),
+        in_specs=[anywhere] * (1 + len(others)),
+        out_specs=anywhere,
+        input_output_aliases={0: 0},
+    )(array, *others)
+
+
+def combine_kernel(position, gates, back, *refs):
+    shared, (out, place, gate, total) = refs[:-4], refs[-4:]
     step = pl.program_id(0)
     chunk = back.shape[0]
     rows = out.shape[0]
@@ -202,19 +224,21 @@
         for b in range(rows // block):
             at = pl.ds(b * block, block)
             columns = jnp.concatenate([position[:, at], gates[:, at], jnp.zeros((4, block), F32)], axis=0).T
-            for n in range(4):
-                table[n, at, :] = jnp.broadcast_to(columns[:, n : n + 1], (block, 128))
-            total[at, :] = sum(shared[q, at, :].astype(F32) for q in range(shared.shape[0]))
-
-    lane = lax.broadcasted_iota(jnp.int32, (block, 128), 1).astype(F32)
-    low = (step * chunk).astype(F32)
+            for n in range(2):
+                place[n, at, :] = jnp.broadcast_to(columns[:, n : n + 1], (block, 128)).astype(jnp.int32).astype(jnp.int16)
+                gate[n, at, :] = jnp.broadcast_to(columns[:, n + 2 : n + 3], (block, 128)).astype(BF16)
+            total[at, :] = sum(part[at, :].astype(F32) for part in shared)
+
+    lane = lax.broadcasted_iota(jnp.int32, (16, 128), 1) + step * chunk
+    numbers = [
+        jnp.broadcast_to((lane + j * 128).astype(jnp.int16)[None], (block // 16, 16, 128)).reshape(block, 128)
+        for j in range(chunk // 128)
+    ]
     for b in range(rows // block):
         at = pl.ds(b * block, block)
-        first, second = table[0, at, :] - low, table[1, at, :] - low
-        gate, other = table[2, at, :], table[3, at, :]
+        first, second, one, two = place[0, at, :], place[1, at, :], gate[0, at, :], gate[1, at, :]
         weight = [
-            jnp.where(lane + j * 128 == first, gate, jnp.where(lane + j * 128 == second, other, 0.0)).astype(BF16)
-            for j in range(chunk // 128)
+            jnp.where(number == first, one, jnp.where(number == second, two, jnp.zeros((), BF16))) for number in numbers
         ]
         total[at, :] += dot(jnp.concatenate(weight, axis=1), back[...])
 
@@ -224,7 +248,7 @@
 
 
 def combine(position, gates, back, shared):
-    planes, rows, part = shared.shape
+    rows, part = shared[0].shape
     slots = back.shape[0]
     chunk = 1024
     return pl.pallas_call(
@@ -235,15 +259,19 @@
             pl.BlockSpec((2, rows), lambda i: (0, 0)),
             pl.BlockSpec((2, rows), lambda i: (0, 0)),
             pl.BlockSpec((chunk, part), lambda i: (i, 0)),
-            pl.BlockSpec((planes, rows, part), lambda i: (0, 0, 0)),
-        ],
+        ]
+        + [pl.BlockSpec((rows, part), lambda i: (0, 0))] * len(shared),
         out_specs=pl.BlockSpec((rows, part), lambda i: (0, 0)),
-        scratch_shapes=[pltpu.VMEM((4, rows, 128), F32), pltpu.VMEM((rows, part), F32)],
+        scratch_shapes=[
+            pltpu.VMEM((2, rows, 128), jnp.int16),
+            pltpu.VMEM((2, rows, 128), BF16),
+            pltpu.VMEM((rows, part), F32),
+        ],
         compiler_params=pltpu.CompilerParams(vmem_limit_bytes=VMEM_LIMIT),
         cost_estimate=pl.CostEstimate(
             flops=2 * rows * slots * part, bytes_accessed=10 * rows * part + 2 * slots * part, transcendentals=0
         ),
-    )(position, gates, back, shared)
+    )(position, gates, back, *shared)
 
 
 def per_device(
@@ -282,9 +310,12 @@
         tokens, norm_gain.reshape(1, width), routes.T, z, columns * planes, cap, planes, sends[-1]
     )
     slots = lax.all_to_all(outgoing.reshape(sectors, -1, width), "sector", 0, 0, tiled=True)
-    shared = shared_expert(normed, shared_gate, shared_up, shared_down, planes, weights[::2])
-    shared_parts = lax.psum_scatter(shared, "expert", scatter_dimension=0, tiled=True)
-    results = expert(slots.reshape(-1, width), weights, planes, shared)
+    shared = shared_expert(normed, shared_gate, shared_up, shared_down, z, planes)
+    shared_parts = [shared[0]] + [
+        lax.ppermute(shared[k], "expert", [(i, (i + k) % planes) for i in range(planes)]) for k in range(1, planes)
+    ]
+    results = expert(slots.reshape(-1, width), weights, planes, shared[0])
+    results = hold(results, *shared_parts[1:])
     part = width // planes
     back = lax.all_to_all(results.reshape(planes * sectors, -1, part), both, 0, 0, tiled=True)
     return combine(position, gates.T, back.reshape(-1, part), shared_parts)

time: 158 us -> 140 us (0.89)
  between operations: 13.5 us -> 0.1 us
  Pallas kernels: 58.8 us -> 53.5 us
  waiting for transfers between devices: 21.9 us -> 18.2 us
  starting transfers between devices: 21.8 us -> 24.9 us
  blocking collectives: 37.5 us -> 39.6 us
    pallas_call x1, Pallas kernels: 20.1 us -> 14.3 us  [combine(): pl.pallas_call(combine_kernel, grid=(slots // chunk,), out_shape=jax.Shap...]
    ppermute x4, waiting for transfers between devices: 4.98 us -> 0.01 us  [per_device(): other = lax.ppermute(half, 'sector', [(s, s ^ 1) for s in range(sectors)])]
    ppermute x0 -> x3, starting transfers between devices: none -> 2.8 us  [per_device(): lax.ppermute(shared[k], 'expert', [(i, (i + k) % planes) for i in range(p...]
    ppermute x0 -> x3, waiting for transfers between devices: none -> 2.07 us  [per_device(): lax.ppermute(shared[k], 'expert', [(i, (i + k) % planes) for i in range(p...]
    all_to_all x1, blocking collectives: 37.5 us -> 39.6 us  [per_device(): lax.all_to_all(results.reshape(planes * sectors, -1, part), both, 0, 0, t...]
    unnamed x12 -> x14, local copies, waits for them, and re-layouts: 3.35 us -> 2.79 us
    pallas_call x1 -> x2, Pallas kernels: 6.88 us -> 7.19 us  [the longest x1 7.19 us: shared_expert(): pl.pallas_call(shared_kernel, grid=(rows // block,), out_shape=[jax.Shape...]
  transfers between devices with their start and end apart: 10 -> 12, of which waited for: 5 -> 4; matrix products, arithmetic and copies ran while one was open for 0% -> 0% of each run, Pallas kernels for 22% -> 25%
where the time goes in v3:
time: 140 us; the launch traced here: 139 us
  Pallas kernels  53.5 us (38%)
  blocking collectives  39.6 us (28%)
  starting transfers between devices  24.9 us (18%)
  waiting for transfers between devices  18.2 us (13%)
  local copies, waits for them, and re-layouts  2.79 us (2%)
    all_to_all x1, blocking collectives, per_device(): lax.all_to_all(results.reshape(planes * sectors, -1, part), both, 0, 0, t...  39.6 us
    pallas_call x1, Pallas kernels, expert(): pl.pallas_call(expert_kernel, grid=(rows // block,), out_shape=jax.ShapeD...  19.5 us
    ppermute x4, waiting for transfers between devices, per_device(): half = lax.ppermute(send, both, moves)  16.1 us
    pallas_call x1, Pallas kernels, combine(): pl.pallas_call(combine_kernel, grid=(slots // chunk,), out_shape=jax.Shap...  14.3 us
    ppermute x4, starting transfers between devices, per_device(): half = lax.ppermute(send, both, moves)  10.6 us
    pallas_call x1, Pallas kernels, route(): pl.pallas_call(functools.partial(route_kernel, block, cap, stack), grid=(...  8.67 us
    all_to_all x1, starting transfers between devices, per_device(): lax.all_to_all(outgoing.reshape(sectors, -1, width), 'sector', 0, 0, tile...  7.2 us
    pallas_call x1, Pallas kernels, shared_expert(): pl.pallas_call(shared_kernel, grid=(rows // block,), out_shape=[jax.Shape...  7.19 us
  transfers between devices with their start and end apart: 12, of which 4 were waited for; matrix products, arithmetic and copies ran while one was open for 0% of the time, Pallas kernels for 25%

profile of v3, /device:TPU:1, one launch (start us, length us, event | category | flops | bytes accessed | tf_op | source)
XLA Modules:
  0.0 139.0 jit_solution(5965193915253713992)
XLA Ops:
  0.0 3.8 %shard_map.100 = (bf16[3,256,512]{2,1,0:T(8,128)(2,1)}, bf16[3,256,512]{2,1,0:T(8,128)(2,1)}, bf16[3,256,512]{2,1,0:T(8,128)(2,1)}, bf16[3,256,512]{2,1,0:T(8,128)(2,1)}) custom-call(s32[1]{0:T(128)} %bitcast.place.plane, bf16[2,512,512]{2,1,0:T(8,128)(2,1)} %gate.2, bf16[2,512,512]{2,1,0:T(8,128)(2,1)} %up.2, bf16[2,512,512]{2,1,0:T(8,128)(2,1)} %down.2), custom_call_target="tpu_custom_call" | custom-call | bytes 6291456 | tf_op jit(solution)/shard_map/pallas_call | solution.py:39
  3.8 6.9 %collective-permute-start = (bf16[3,256,512]{2,1,0:T(8,128)(2,1)}, bf16[3,256,512]{2,1,0:T(8,128)(2,1)S(1)}, u32[]{:S(2)}, u32[]{:S(2)}) collective-permute-start(bf16[3,256,512]{2,1,0:T(8,128)(2,1)} %get-tuple-element.21), channel_id=1, source_target_pairs={{0,0},{1,64},{2,2},{3,66},{4,4},{5,68},{6,6},{7,70},{8,8},{9,72},{... | collective-permute-start | bytes 2359304 | tf_op jit(solution)/shard_map/ppermute | solution.py:305
  10.7 1.4 %collective-permute-start.2 = (bf16[3,256,512]{2,1,0:T(8,128)(2,1)}, bf16[3,256,512]{2,1,0:T(8,128)(2,1)}, u32[]{:S(2)}, u32[]{:S(2)}) collective-permute-start(bf16[3,256,512]{2,1,0:T(8,128)(2,1)} %get-tuple-element.22), channel_id=1, source_target_pairs={{0,1},{1,65},{2,3},{3,67},{4,5},{5,69},{6,7},{7,71},{8,9},{9,73},{... | collective-permute-start | bytes 2359304 | tf_op jit(solution)/shard_map/ppermute | solution.py:305
  12.1 0.0 collective-permute-start.4
  12.1 2.3 %collective-permute-start.6 = (bf16[3,256,512]{2,1,0:T(8,128)(2,1)}, bf16[3,256,512]{2,1,0:T(8,128)(2,1)}, u32[]{:S(2)}, u32[]{:S(2)}) collective-permute-start(bf16[3,256,512]{2,1,0:T(8,128)(2,1)} %get-tuple-element.16.after), channel_id=1, source_target_pairs={{0,33},{1,97},{2,35},{3,99},{4,37},{5,101},{6,39},{7,103},{8,41},{... | collective-permute-start | bytes 2359304 | tf_op jit(solution)/shard_map/ppermute | solution.py:305
  14.4 8.7 %shard_map.101 = (bf16[2048,512]{1,0:T(8,128)(2,1)}, bf16[2048,512]{1,0:T(8,128)(2,1)}, f32[2,2048]{1,0:T(2,128)}) custom-call(s32[1]{0:T(128)} %bitcast.place.plane, bf16[2048,512]{1,0:T(8,128)(2,1)} %tokens.1, f32[1,512]{1,0:T(1,128)} %bitcast.14, s32[2,2048]{1,0:T(2,128)} %bitcast.12, bf16[3,256,512]{2,1,0:T(8,128)(2,1)} %get-tuple-element.16.after), custom_call_target="tpu_custom_call" | custom-call | flops 4294967296 | bytes 8388608 | tf_op jit(solution)/shard_map/pallas_call | solution.py:90
  23.0 7.2 %all-to-all-start = ((bf16[32,64,512]{2,1,0:T(8,128)(2,1)}), bf16[32,64,512]{2,1,0:T(8,128)(2,1)S(1)}, u32[]{:S(2)}, u32[]{:S(2)}) async-start(bf16[32,64,512]{2,1,0:T(8,128)(2,1)} %bitcast.10), calls=%async_computation | async-start | bytes 4194304 | tf_op jit(solution)/shard_map/all_to_all | solution.py:312
  30.2 0.0 collective-permute-done.refs_0_
  30.3 0.3 collective-permute-start.1
  30.6 13.8 %collective-permute-done.2.refs_2_ = bf16[3,256,512]{2,1,0:T(8,128)(2,1)} collective-permute-done((bf16[3,256,512]{2,1,0:T(8,128)(2,1)}, bf16[3,256,512]{2,1,0:T(8,128)(2,1)}, u32[]{:S(2)}, u32[]{:S(2)}) %collective-permute-start.2) | collective-permute-done | bytes 786464 | tf_op jit(solution)/shard_map/ppermute | solution.py:305
  44.4 0.0 collective-permute-start.3
  44.4 0.0 collective-permute-done.4.refs_4_
  44.4 0.5 collective-permute-start.5
  44.9 2.3 %collective-permute-done.6.refs_6_ = bf16[3,256,512]{2,1,0:T(8,128)(2,1)} collective-permute-done((bf16[3,256,512]{2,1,0:T(8,128)(2,1)}, bf16[3,256,512]{2,1,0:T(8,128)(2,1)}, u32[]{:S(2)}, u32[]{:S(2)}) %collective-permute-start.6) | collective-permute-done | bytes 786464 | tf_op jit(solution)/shard_map/ppermute | solution.py:305
  47.2 3.5 %collective-permute-start.7 = (bf16[3,256,512]{2,1,0:T(8,128)(2,1)}, bf16[3,256,512]{2,1,0:T(8,128)(2,1)}, u32[]{:S(2)}, u32[]{:S(2)}) collective-permute-start(bf16[3,256,512]{2,1,0:T(8,128)(2,1)} %collective-permute-done.6.refs_6_), channel_id=1, source_target_pairs={{0,1},{1,0},{2,3},{3,2},{4,5},{5,4},{6,7},{7,6},{8,9},{9,8},{10,11... | collective-permute-start | bytes 2359304 | tf_op jit(solution)/shard_map/ppermute | solution.py:306
  50.7 7.2 %shard_map.102 = (bf16[2048,128]{1,0:T(8,128)(2,1)}, bf16[2048,128]{1,0:T(8,128)(2,1)}, bf16[2048,128]{1,0:T(8,128)(2,1)}, bf16[2048,128]{1,0:T(8,128)(2,1)}) custom-call(s32[1]{0:T(128)} %bitcast.place.plane, bf16[2048,512]{1,0:T(8,128)(2,1)} %get-tuple-element.19.normed, bf16[512,512]{1,0:T(8,128)(2,1)} %gate.3, bf16[512,512]{1,0:T(8,128)(2,1)} %up.3, ...), custom_call_target="tpu_custom_call" | custom-call | flops 32212254720 | bytes 4194304 | tf_op jit(solution)/shard_map/pallas_call | solution.py:140
  57.9 0.1 collective-permute-start.8
  58.0 0.4 collective-permute-start.9
  58.4 2.3 %collective-permute-start.10 = (bf16[2048,128]{1,0:T(8,128)(2,1)}, bf16[2048,128]{1,0:T(8,128)(2,1)}, u32[]{:S(2)}, u32[]{:S(2)}) collective-permute-start(bf16[2048,128]{1,0:T(8,128)(2,1)} %get-tuple-element.26), channel_id=1, source_target_pairs={{0,96},{32,0},{64,32},{96,64},{1,97},{33,1},{65,33},{97,65},{2,98}... | collective-permute-start | bytes 1572872 | tf_op jit(solution)/shard_map/ppermute | solution.py:315
  60.7 0.0 collective-permute-done.5.refs_5_
  60.7 0.9 copy-done.6
  61.6 0.0 collective-permute-done.7.refs_7_
  61.7 0.0 all-to-all-done
  61.7 1.3 copy-done
  63.0 19.5 %shard_map.103.refs_0_ = bf16[4,2048,128]{2,1,0:T(8,128)(2,1)} custom-call(bf16[2048,512]{1,0:T(8,128)(2,1)} %bitcast.9, bf16[2048,128]{1,0:T(8,128)(2,1)} %get-tuple-element.20.after.refs_0_, bf16[3,256,512]{2,1,0:T(8,128)(2,1)} %copy-done.3, bf16[3,256,512]{2,1,0:T(8,128)(2,1)} %copy-done.4, bf16[3,256,512]{2,1,0:T(8,128)(2,1)} %collective-permute-done.2.refs_2_, ...), custom_call_target="tpu_custom_call" | custom-call | flops 12884901888 | bytes 10485760 | tf_op jit(solution)/shard_map/pallas_call | solution.py:179
  82.5 1.7 %collective-permute-done.8.refs_1_ = bf16[2048,128]{1,0:T(8,128)(2,1)S(1)} collective-permute-done((bf16[2048,128]{1,0:T(8,128)(2,1)}, bf16[2048,128]{1,0:T(8,128)(2,1)S(1)}, u32[]{:S(2)}, u32[]{:S(2)}) %collective-permute-start.8) | collective-permute-done | bytes 524320 | tf_op jit(solution)/shard_map/ppermute | solution.py:315
  84.1 0.0 collective-permute-done.9.refs_2_
  84.2 0.4 collective-permute-done.10.refs_3_
  84.6 0.4 copy-done.1
  85.0 0.2 copy-done.2
  85.1 39.6 %all_to_all.10 = bf16[128,64,128]{2,1,0:T(8,128)(2,1)} all-to-all(bf16[128,64,128]{2,1,0:T(8,128)(2,1)} %bitcast.8), channel_id=1, replica_groups=mesh['expert'=4,'sector'=32] {'expert','sector'}, dimensions={0} | all-to-all | bytes 4194304 | tf_op jit(solution)/shard_map/all_to_all | solution.py:320
  124.7 14.3 %shard_map.105 = bf16[2048,128]{1,0:T(8,128)(2,1)} custom-call(f32[2,2048]{1,0:T(2,128)} %get-tuple-element.17.position, f32[2,2048]{1,0:T(2,128)} %bitcast.13, bf16[8192,128]{1,0:T(8,128)(2,1)} %bitcast.11, bf16[2048,128]{1,0:T(8,128)(2,1)} %get-tuple-element.20.after.refs_0_, bf16[2048,128]{1,0:T(8,128)(2,1)} %copy-done.1, bf16[2048,128]{1,0:T(8,128)(2,1)} %copy-done.2, ...), custom_call_target="tpu_custom_call" | custom-call | flops 4294967296 | bytes 4718592 | tf_op jit(solution)/shard_map/pallas_call | solution.py:254
  (13 shorter events, 0.0 us)
Async XLA Ops:
  3.8 26.5 %collective-permute-start = (bf16[3,256,512]{2,1,0:T(8,128)(2,1)}, bf16[3,256,512]{2,1,0:T(8,128)(2,1)S(1)}, u32[]{:S(2)}, u32[]{:S(2)}) collective-permute-start(bf16[3,256,512]{2,1,0:T(8,128)(2,1)} %get-tuple-element.21), channel_id=1, source_target_pairs={{0,0},{1,64},{2,2},{3,66},{4,4},{5,68},{6,6},{7,70},{8,8},{9,72},{... | collective-permute-start | bytes 2359304 | tf_op jit(solution)/shard_map/ppermute | solution.py:305
  10.7 33.7 %collective-permute-start.2 = (bf16[3,256,512]{2,1,0:T(8,128)(2,1)}, bf16[3,256,512]{2,1,0:T(8,128)(2,1)}, u32[]{:S(2)}, u32[]{:S(2)}) collective-permute-start(bf16[3,256,512]{2,1,0:T(8,128)(2,1)} %get-tuple-element.22), channel_id=1, source_target_pairs={{0,1},{1,65},{2,3},{3,67},{4,5},{5,69},{6,7},{7,71},{8,9},{9,73},{... | collective-permute-start | bytes 2359304 | tf_op jit(solution)/shard_map/ppermute | solution.py:305
  12.1 32.3 %collective-permute-start.4 = (bf16[3,256,512]{2,1,0:T(8,128)(2,1)}, bf16[3,256,512]{2,1,0:T(8,128)(2,1)}, u32[]{:S(2)}, u32[]{:S(2)}) collective-permute-start(bf16[3,256,512]{2,1,0:T(8,128)(2,1)} %get-tuple-element.23), channel_id=1, source_target_pairs={{0,32},{1,96},{2,34},{3,98},{4,36},{5,100},{6,38},{7,102},{8,40},{... | collective-permute-start | bytes 2359304 | tf_op jit(solution)/shard_map/ppermute | solution.py:305
  12.1 35.1 %collective-permute-start.6 = (bf16[3,256,512]{2,1,0:T(8,128)(2,1)}, bf16[3,256,512]{2,1,0:T(8,128)(2,1)}, u32[]{:S(2)}, u32[]{:S(2)}) collective-permute-start(bf16[3,256,512]{2,1,0:T(8,128)(2,1)} %get-tuple-element.16.after), channel_id=1, source_target_pairs={{0,33},{1,97},{2,35},{3,99},{4,37},{5,101},{6,39},{7,103},{8,41},{... | collective-permute-start | bytes 2359304 | tf_op jit(solution)/shard_map/ppermute | solution.py:305
  23.0 38.6 %all-to-all-start = ((bf16[32,64,512]{2,1,0:T(8,128)(2,1)}), bf16[32,64,512]{2,1,0:T(8,128)(2,1)S(1)}, u32[]{:S(2)}, u32[]{:S(2)}) async-start(bf16[32,64,512]{2,1,0:T(8,128)(2,1)} %bitcast.10), calls=%async_computation | async-start | bytes 4194304 | tf_op jit(solution)/shard_map/all_to_all | solution.py:312
  30.3 27.6 %copy-start.3 = (bf16[3,256,512]{2,1,0:T(8,128)(2,1)}, bf16[3,256,512]{2,1,0:T(8,128)(2,1)S(1)}, u32[]{:S(2)}) copy-start(bf16[3,256,512]{2,1,0:T(8,128)(2,1)S(1)} %collective-permute-done.refs_0_) | copy-start | bytes 2359300
  30.3 27.7 %collective-permute-start.1 = (bf16[3,256,512]{2,1,0:T(8,128)(2,1)S(1)}, bf16[3,256,512]{2,1,0:T(8,128)(2,1)S(1)}, u32[]{:S(2)}, u32[]{:S(2)}) collective-permute-start(bf16[3,256,512]{2,1,0:T(8,128)(2,1)S(1)} %collective-permute-done.refs_0_), channel_id=1, source_target_pairs={{0,1},{1,0},{2,3},{3,2},{4,5},{5,4},{6,7},{7,6},{8,9},{9,8},{10,11... | collective-permute-start | bytes 2359304 | tf_op jit(solution)/shard_map/ppermute | solution.py:306
  44.4 14.0 %collective-permute-start.3 = (bf16[3,256,512]{2,1,0:T(8,128)(2,1)}, bf16[3,256,512]{2,1,0:T(8,128)(2,1)S(1)}, u32[]{:S(2)}, u32[]{:S(2)}) collective-permute-start(bf16[3,256,512]{2,1,0:T(8,128)(2,1)} %collective-permute-done.2.refs_2_), channel_id=1, source_target_pairs={{0,1},{1,0},{2,3},{3,2},{4,5},{5,4},{6,7},{7,6},{8,9},{9,8},{10,11... | collective-permute-start | bytes 2359304 | tf_op jit(solution)/shard_map/ppermute | solution.py:306
  44.4 16.3 %collective-permute-start.5 = (bf16[3,256,512]{2,1,0:T(8,128)(2,1)}, bf16[3,256,512]{2,1,0:T(8,128)(2,1)S(1)}, u32[]{:S(2)}, u32[]{:S(2)}) collective-permute-start(bf16[3,256,512]{2,1,0:T(8,128)(2,1)} %collective-permute-done.4.refs_4_), channel_id=1, source_target_pairs={{0,1},{1,0},{2,3},{3,2},{4,5},{5,4},{6,7},{7,6},{8,9},{9,8},{10,11... | collective-permute-start | bytes 2359304 | tf_op jit(solution)/shard_map/ppermute | solution.py:306
  47.2 14.5 %collective-permute-start.7 = (bf16[3,256,512]{2,1,0:T(8,128)(2,1)}, bf16[3,256,512]{2,1,0:T(8,128)(2,1)}, u32[]{:S(2)}, u32[]{:S(2)}) collective-permute-start(bf16[3,256,512]{2,1,0:T(8,128)(2,1)} %collective-permute-done.6.refs_6_), channel_id=1, source_target_pairs={{0,1},{1,0},{2,3},{3,2},{4,5},{5,4},{6,7},{7,6},{8,9},{9,8},{10,11... | collective-permute-start | bytes 2359304 | tf_op jit(solution)/shard_map/ppermute | solution.py:306
  57.9 26.2 %collective-permute-start.8 = (bf16[2048,128]{1,0:T(8,128)(2,1)}, bf16[2048,128]{1,0:T(8,128)(2,1)S(1)}, u32[]{:S(2)}, u32[]{:S(2)}) collective-permute-start(bf16[2048,128]{1,0:T(8,128)(2,1)} %get-tuple-element.24), channel_id=1, source_target_pairs={{0,32},{32,64},{64,96},{96,0},{1,33},{33,65},{65,97},{97,1},{2,34}... | collective-permute-start | bytes 1572872 | tf_op jit(solution)/shard_map/ppermute | solution.py:315
  58.0 2.8 %copy-start.4 = (bf16[3,256,512]{2,1,0:T(8,128)(2,1)}, bf16[3,256,512]{2,1,0:T(8,128)(2,1)S(1)}, u32[]{:S(2)}) copy-start(bf16[3,256,512]{2,1,0:T(8,128)(2,1)S(1)} %collective-permute-done.1.refs_1_) | copy-start | bytes 2359300
  58.0 26.2 %collective-permute-start.9 = (bf16[2048,128]{1,0:T(8,128)(2,1)}, bf16[2048,128]{1,0:T(8,128)(2,1)S(1)}, u32[]{:S(2)}, u32[]{:S(2)}) collective-permute-start(bf16[2048,128]{1,0:T(8,128)(2,1)} %get-tuple-element.25), channel_id=1, source_target_pairs={{0,64},{32,96},{64,0},{96,32},{1,65},{33,97},{65,1},{97,33},{2,66}... | collective-permute-start | bytes 1572872 | tf_op jit(solution)/shard_map/ppermute | solution.py:315
  58.4 2.3 %copy-start.5 = (bf16[3,256,512]{2,1,0:T(8,128)(2,1)}, bf16[3,256,512]{2,1,0:T(8,128)(2,1)S(1)}, u32[]{:S(2)}) copy-start(bf16[3,256,512]{2,1,0:T(8,128)(2,1)S(1)} %collective-permute-done.3.refs_3_) | copy-start | bytes 2359300
  58.4 26.2 %collective-permute-start.10 = (bf16[2048,128]{1,0:T(8,128)(2,1)}, bf16[2048,128]{1,0:T(8,128)(2,1)}, u32[]{:S(2)}, u32[]{:S(2)}) collective-permute-start(bf16[2048,128]{1,0:T(8,128)(2,1)} %get-tuple-element.26), channel_id=1, source_target_pairs={{0,96},{32,0},{64,32},{96,64},{1,97},{33,1},{65,33},{97,65},{2,98}... | collective-permute-start | bytes 1572872 | tf_op jit(solution)/shard_map/ppermute | solution.py:315
  60.7 0.9 copy-start.6
  61.7 1.3 copy-start
  84.1 0.8 copy-start.1
  84.2 1.0 copy-start.2

commit v4 on v3

--- a/solution.py
+++ b/solution.py
@@ -22,20 +22,21 @@
 
 
 def pack_kernel(half, place, gate, up, down, *sends):
+    width = gate.shape[1]
     for r, send in enumerate(sends):
         pick = place[0] ^ r
         expert, part = pick // 2, pick % 2
         cols = pl.ds(pl.multiple_of(part * half, half), half)
-        for n, w in enumerate((gate, up)):
-            send[n, :, :half] = w[expert, :half, cols]
-            send[n, :, half:] = w[expert, half:, cols]
-        send[2] = down[expert, cols, :]
+        send[:width, :] = gate[expert, :, cols]
+        send[width : 2 * width, :] = up[expert, :, cols]
+        for n in range(width // half):
+            send[2 * width + n * half : 2 * width + (n + 1) * half, :] = down[expert, cols, n * half : (n + 1) * half]
 
 
 def pack(gate, up, down, place):
     _, width, hidden = gate.shape
     half = hidden // 2
-    shape = jax.ShapeDtypeStruct((3, half, width), BF16)
+    shape = jax.ShapeDtypeStruct((3 * width, half), BF16)
     return pl.pallas_call(
         functools.partial(pack_kernel, half),
         out_shape=[shape] * 4,
@@ -60,7 +61,7 @@
         ).astype(F32).astype(BF16)
         m = lax.broadcasted_iota(jnp.int32, (experts, block), 0)
         name = (m % columns) * stack + m // columns
-        base = (m * cap).astype(F32)
+        core, turn = cap // 2, cap // 4
         seen = jnp.zeros((experts, 1), F32)
         for b in range(rows // block):
             at = pl.ds(b * block, block)
@@ -70,7 +71,9 @@
             rank = dot(named.astype(BF16), earlier) + seen
             chosen[:, at] = jnp.where(first | second, rank, -1.0)
             seen = seen + jnp.sum(named, axis=1, keepdims=True)
-            slot = rank + base
+            number = rank.astype(jnp.int32)
+            slot = m * core + number // core * turn + number % turn + number // turn % 2 * (experts * core)
+            slot = slot.astype(F32)
             position[0:1, at] = jnp.max(jnp.where(first, slot, -1.0), axis=0, keepdims=True)
             position[1:2, at] = jnp.max(jnp.where(second, slot, -1.0), axis=0, keepdims=True)
             values = tokens[at, :].astype(F32)
@@ -113,12 +116,6 @@
             flops=2 * slots * rows * width, bytes_accessed=6 * rows * width + 2 * slots * width, transcendentals=rows
         ),
     )(plane, tokens, gain, routes, after)
-
-
-def split_columns(out, values):
-    part = out.shape[2]
-    for q in range(out.shape[0]):
-        out[q] = values[:, q * part : (q + 1) * part]
 
 
 def shared_kernel(plane, normed, gate, up, down, *rest):
@@ -146,62 +143,67 @@
         scratch_shapes=[pltpu.VMEM((block, width), F32)],
         compiler_params=pltpu.CompilerParams(vmem_limit_bytes=VMEM_LIMIT),
         cost_estimate=pl.CostEstimate(
-            flops=60 * rows * width * hidden, bytes_accessed=4 * rows * width, transcendentals=rows * hidden
+            flops=6 * rows * width * hidden, bytes_accessed=4 * rows * width, transcendentals=rows * hidden
         ),
     )(plane, normed, gate, up, down)
 
 
-def expert_kernel(slots, after, *refs):
-    weights, (out, w_gate, w_up, w_down, hidden) = refs[:-5], refs[-5:]
-    half = slots.shape[1] // 2
-
-    @pl.when(pl.program_id(0) == 0)
-    def _():
-        for n, w in enumerate(weights):
-            at = pl.ds(n * half, half)
-            for whole, part in ((w_gate, 0), (w_up, 1)):
-                whole[:half, at] = w[part, :, :half]
-                whole[half:, at] = w[part, :, half:]
-            w_down[at, :] = w[2]
-
-    x = slots[...]
-    step = 512
-    for n in range(hidden.shape[1] // step):
-        at = pl.ds(n * step, step)
-        hidden[:, at] = swish(dot(x, w_gate[:, at]), dot(x, w_up[:, at]))
-    split_columns(out, dot(hidden[...], w_down[...]).astype(BF16))
-
-
-def expert(slots, weights, planes, after):
-    rows, width = slots.shape
-    block = 512
+def expert_kernel(turn, slots, *refs):
+    weights, (out, x, kept, total, arrived, sems) = refs[:8], refs[-6:]
+    rows, width = total.shape
+    each = x.shape[1]
+    half = kept.shape[2]
+    load = pltpu.make_async_copy(slots.at[:, pl.ds(turn * each, each), :], x, arrived)
+    load.start()
+    copies = [pltpu.make_async_copy(w, kept.at[n], sems.at[n]) for n, w in enumerate(weights)]
+    for copy in copies:
+        copy.start()
+    load.wait()
+    rows_in = x[...].reshape(rows, width)
+    for n, copy in enumerate(copies):
+        copy.wait()
+        w = kept.at[n]
+        hidden = swish(dot(rows_in, w[:width, :]), dot(rows_in, w[width : 2 * width, :]))
+        for c in range(width // half):
+            at = pl.ds(c * half, half)
+            part = dot(hidden, w[2 * width + c * half : 2 * width + (c + 1) * half, :])
+            total[:, at] = part if n == 0 else total[:, at] + part
+    part = out.shape[2]
+    for q in range(out.shape[0]):
+        out[q] = total[:, q * part : (q + 1) * part].astype(BF16)
+
+
+def expert(slots, weights, planes, turn, after):
+    sources, each, width = slots.shape
+    each = each // 2
+    rows = sources * each
     hidden = sum(w.shape[1] for w in weights)
-    return pl.pallas_call(
-        expert_kernel,
-        grid=(rows // block,),
+    anywhere = pl.BlockSpec(memory_space=pl.ANY)
+    return pl.pallas_call(
+        functools.partial(expert_kernel, turn),
         out_shape=jax.ShapeDtypeStruct((planes, rows, width // planes), BF16),
-        in_specs=[pl.BlockSpec((block, width), lambda i: (i, 0)), pl.BlockSpec(memory_space=pl.ANY)]
-        + [pl.BlockSpec(w.shape, lambda i: (0, 0, 0)) for w in weights],
-        out_specs=pl.BlockSpec((planes, block, width // planes), lambda i: (0, i, 0)),
+        in_specs=[anywhere] * (1 + len(weights) + len(after)),
+        out_specs=pl.BlockSpec(memory_space=pltpu.VMEM),
         scratch_shapes=[
-            pltpu.VMEM((width, hidden), BF16),
-            pltpu.VMEM((width, hidden), BF16),
-            pltpu.VMEM((hidden, width), BF16),
-            pltpu.VMEM((block, hidden), BF16),
+            pltpu.VMEM((sources, each, width), BF16),
+            pltpu.VMEM((len(weights), *weights[0].shape), BF16),
+            pltpu.VMEM((rows, width), F32),
+            pltpu.SemaphoreType.DMA,
+            pltpu.SemaphoreType.DMA((len(weights),)),
         ],
         compiler_params=pltpu.CompilerParams(vmem_limit_bytes=VMEM_LIMIT),
         cost_estimate=pl.CostEstimate(
             flops=6 * rows * width * hidden, bytes_accessed=4 * rows * width + 6 * width * hidden,
             transcendentals=rows * hidden,
         ),
-    )(slots, after, *weights)
+    )(slots, *weights, *after)
 
 
 def hold_kernel(*refs):
     pass
 
 
-def hold(array, *others):
+def hold(array, *others, flops=0):
     anywhere = pl.BlockSpec(memory_space=pl.ANY)
     return pl.pallas_call(
         hold_kernel,
@@ -209,11 +211,12 @@
         in_specs=[anywhere] * (1 + len(others)),
         out_specs=anywhere,
         input_output_aliases={0: 0},
+        cost_estimate=pl.CostEstimate(flops=flops, bytes_accessed=0, transcendentals=0),
     )(array, *others)
 
 
-def combine_kernel(position, gates, back, *refs):
-    shared, (out, place, gate, total) = refs[:-4], refs[-4:]
+def combine_kernel(base, position, gates, back, *refs):
+    addends, (out, place, gate, total) = refs[:-4], refs[-4:]
     step = pl.program_id(0)
     chunk = back.shape[0]
     rows = out.shape[0]
@@ -227,9 +230,9 @@
             for n in range(2):
                 place[n, at, :] = jnp.broadcast_to(columns[:, n : n + 1], (block, 128)).astype(jnp.int32).astype(jnp.int16)
                 gate[n, at, :] = jnp.broadcast_to(columns[:, n + 2 : n + 3], (block, 128)).astype(BF16)
-            total[at, :] = sum(part[at, :].astype(F32) for part in shared)
-
-    lane = lax.broadcasted_iota(jnp.int32, (16, 128), 1) + step * chunk
+            total[at, :] = sum(part[at, :].astype(F32) for part in addends)
+
+    lane = lax.broadcasted_iota(jnp.int32, (16, 128), 1) + (step * chunk + base)
     numbers = [
         jnp.broadcast_to((lane + j * 128).astype(jnp.int16)[None], (block // 16, 16, 128)).reshape(block, 128)
         for j in range(chunk // 128)
@@ -244,23 +247,23 @@
 
     @pl.when(step == pl.num_programs(0) - 1)
     def _():
-        out[...] = total[...].astype(BF16)
-
-
-def combine(position, gates, back, shared):
-    rows, part = shared[0].shape
+        out[...] = total[...].astype(out.dtype)
+
+
+def combine(position, gates, back, addends, base, kind):
+    rows, part = addends[0].shape
     slots = back.shape[0]
     chunk = 1024
     return pl.pallas_call(
-        combine_kernel,
+        functools.partial(combine_kernel, base),
         grid=(slots // chunk,),
-        out_shape=jax.ShapeDtypeStruct((rows, part), BF16),
+        out_shape=jax.ShapeDtypeStruct((rows, part), kind),
         in_specs=[
             pl.BlockSpec((2, rows), lambda i: (0, 0)),
             pl.BlockSpec((2, rows), lambda i: (0, 0)),
             pl.BlockSpec((chunk, part), lambda i: (i, 0)),
         ]
-        + [pl.BlockSpec((rows, part), lambda i: (0, 0))] * len(shared),
+        + [pl.BlockSpec((rows, part), lambda i: (0, 0))] * len(addends),
         out_specs=pl.BlockSpec((rows, part), lambda i: (0, 0)),
         scratch_shapes=[
             pltpu.VMEM((2, rows, 128), jnp.int16),
@@ -271,7 +274,7 @@
         cost_estimate=pl.CostEstimate(
             flops=2 * rows * slots * part, bytes_accessed=10 * rows * part + 2 * slots * part, transcendentals=0
         ),
-    )(position, gates, back, *shared)
+    )(position, gates, back, *addends)
 
 
 def per_device(
@@ -294,7 +297,7 @@
     z = lax.axis_index("expert").astype(jnp.int32).reshape(1)
 
     sends = pack(expert_gate, expert_up, expert_down, z)
-    weights = []
+    halves = []
     for r, send in enumerate(sends):
         moves = []
         for source in range(planes):
@@ -302,23 +305,28 @@
                 pick = source ^ r
                 target = 2 * (s % 2) + pick // 2
                 moves.append((source * sectors + s, target * sectors + (s // 2) * 2 + pick % 2))
-        half = lax.ppermute(send, both, moves)
-        other = lax.ppermute(half, "sector", [(s, s ^ 1) for s in range(sectors)])
-        weights += [half, other]
+        halves.append(lax.ppermute(send, both, moves))
 
     outgoing, normed, position = route(
         tokens, norm_gain.reshape(1, width), routes.T, z, columns * planes, cap, planes, sends[-1]
     )
     slots = lax.all_to_all(outgoing.reshape(sectors, -1, width), "sector", 0, 0, tiled=True)
-    shared = shared_expert(normed, shared_gate, shared_up, shared_down, z, planes)
+    shared = list(shared_expert(normed, shared_gate, shared_up, shared_down, z, planes))
+    shared[1] = hold(shared[1], *halves, flops=10**10)
     shared_parts = [shared[0]] + [
         lax.ppermute(shared[k], "expert", [(i, (i + k) % planes) for i in range(planes)]) for k in range(1, planes)
     ]
-    results = expert(slots.reshape(-1, width), weights, planes, shared[0])
-    results = hold(results, *shared_parts[1:])
+    halves[0] = hold(halves[0], shared[0])
+    weights = halves + [lax.ppermute(half, "sector", [(s, s ^ 1) for s in range(sectors)]) for half in halves]
+
     part = width // planes
-    back = lax.all_to_all(results.reshape(planes * sectors, -1, part), both, 0, 0, tiled=True)
-    return combine(position, gates.T, back.reshape(-1, part), shared_parts)
+    gates = gates.T
+    first = expert(slots, weights, planes, 0, shared[1:])
+    first = lax.all_to_all(first.reshape(planes * sectors, -1, part), both, 0, 0, tiled=True).reshape(-1, part)
+    second = expert(slots, weights, planes, 1, shared_parts[1:])
+    second = lax.all_to_all(second.reshape(planes * sectors, -1, part), both, 0, 0, tiled=True).reshape(-1, part)
+    mixed = combine(position, gates, first, shared_parts, 0, F32)
+    return combine(position, gates, second, [mixed], first.shape[0], BF16)
 
 
 def solution(mesh):

time: 140 us -> 137 us (0.979)
  blocking collectives: 39.6 us -> 0 us
  starting transfers between devices: 24.9 us -> 40.5 us
  waiting for transfers between devices: 18.2 us -> 29.5 us
  Pallas kernels: 53.5 us -> 62.1 us
    all_to_all x1 -> x0, blocking collectives: 39.6 us -> none  [per_device(): lax.all_to_all(results.reshape(planes * sectors, -1, part), both, 0, 0, t...]
    all_to_all x0 -> x2, waiting for transfers between devices: none -> 17.5 us  [the longest x1 10 us: per_device(): lax.all_to_all(second.reshape(planes * sectors, -1, part), both, 0, 0, ti...]
    ppermute x8, waiting for transfers between devices: 16.1 us -> 3.89 us  [the longest x4 3.88 us: per_device(): halves.append(lax.ppermute(send, both, moves))]
    all_to_all x0 -> x2, starting transfers between devices: none -> 11.5 us  [the longest x1 7.14 us: per_device(): lax.all_to_all(first.reshape(planes * sectors, -1, part), both, 0, 0, til...]
    all_to_all x1, waiting for transfers between devices: 0.01 us -> 8.08 us  [per_device(): lax.all_to_all(outgoing.reshape(sectors, -1, width), 'sector', 0, 0, tile...]
    pallas_call x2 -> x4, Pallas kernels: 33.9 us -> 41.7 us  [the longest x2 23.7 us: expert(): pl.pallas_call(functools.partial(expert_kernel, turn), out_shape=jax.Shap...]
    ppermute x3, starting transfers between devices: 2.8 us -> 5.82 us  [per_device(): lax.ppermute(shared[k], 'expert', [(i, (i + k) % planes) for i in range(p...]
    ppermute x3, waiting for transfers between devices: 2.07 us -> 0.01 us  [per_device(): lax.ppermute(shared[k], 'expert', [(i, (i + k) % planes) for i in range(p...]
  transfers between devices with their start and end apart: 12 -> 14, of which waited for: 4 -> 5; matrix products, arithmetic and copies ran while one was open for 0% -> 0% of each run, Pallas kernels for 25% -> 37%
where the time goes in v4:
time: 137 us; the launch traced here: 136 us
  Pallas kernels  62.1 us (45%)
  starting transfers between devices  40.5 us (30%)
  waiting for transfers between devices  29.5 us (22%)
  local copies, waits for them, and re-layouts  4.08 us (3%)
    pallas_call x2, Pallas kernels, expert(): pl.pallas_call(functools.partial(expert_kernel, turn), out_shape=jax.Shap...  23.7 us
    pallas_call x2, Pallas kernels, combine(): pl.pallas_call(functools.partial(combine_kernel, base), grid=(slots // ch...  17.9 us
    ppermute x4, starting transfers between devices, per_device(): halves.append(lax.ppermute(send, both, moves))  15 us
    all_to_all x1, waiting for transfers between devices, per_device(): lax.all_to_all(second.reshape(planes * sectors, -1, part), both, 0, 0, ti...  10 us
    pallas_call x1, Pallas kernels, route(): pl.pallas_call(functools.partial(route_kernel, block, cap, stack), grid=(...  9.49 us
    all_to_all x1, waiting for transfers between devices, per_device(): lax.all_to_all(outgoing.reshape(sectors, -1, width), 'sector', 0, 0, tile...  8.08 us
    all_to_all x1, waiting for transfers between devices, per_device(): lax.all_to_all(first.reshape(planes * sectors, -1, part), both, 0, 0, til...  7.45 us
    pallas_call x1, Pallas kernels, shared_expert(): pl.pallas_call(shared_kernel, grid=(rows // block,), out_shape=[jax.Shape...  7.22 us
  transfers between devices with their start and end apart: 14, of which 5 were waited for; matrix products, arithmetic and copies ran while one was open for 0% of the time, Pallas kernels for 37%

profile of v4, /device:TPU:1, one launch (start us, length us, event | category | flops | bytes accessed | tf_op | source)
XLA Modules:
  0.0 136.3 jit_solution(13514394000083902717)
XLA Ops:
  0.0 3.7 %shard_map.100 = (bf16[1536,256]{1,0:T(8,128)(2,1)}, bf16[1536,256]{1,0:T(8,128)(2,1)}, bf16[1536,256]{1,0:T(8,128)(2,1)}, bf16[1536,256]{1,0:T(8,128)(2,1)}) custom-call(s32[1]{0:T(128)} %bitcast.place.plane, bf16[2,512,512]{2,1,0:T(8,128)(2,1)} %gate.2, bf16[2,512,512]{2,1,0:T(8,128)(2,1)} %up.2, bf16[2,512,512]{2,1,0:T(8,128)(2,1)} %down.2), custom_call_target="tpu_custom_call" | custom-call | bytes 6291456 | tf_op jit(solution)/shard_map/pallas_call | solution.py:40
  3.7 6.5 %collective-permute-start.3 = (bf16[1536,256]{1,0:T(8,128)(2,1)}, bf16[1536,256]{1,0:T(8,128)(2,1)}, u32[]{:S(2)}, u32[]{:S(2)}) collective-permute-start(bf16[1536,256]{1,0:T(8,128)(2,1)} %get-tuple-element.16.after), channel_id=1, source_target_pairs={{0,33},{1,97},{2,35},{3,99},{4,37},{5,101},{6,39},{7,103},{8,41},{... | collective-permute-start | bytes 2359304 | tf_op jit(solution)/shard_map/ppermute | solution.py:308
  10.2 5.3 %collective-permute-start.1 = (bf16[1536,256]{1,0:T(8,128)(2,1)}, bf16[1536,256]{1,0:T(8,128)(2,1)}, u32[]{:S(2)}, u32[]{:S(2)}) collective-permute-start(bf16[1536,256]{1,0:T(8,128)(2,1)} %get-tuple-element.22), channel_id=1, source_target_pairs={{0,1},{1,65},{2,3},{3,67},{4,5},{5,69},{6,7},{7,71},{8,9},{9,73},{... | collective-permute-start | bytes 2359304 | tf_op jit(solution)/shard_map/ppermute | solution.py:308
  15.6 1.3 collective-permute-start.2
  16.8 1.9 %collective-permute-start = (bf16[1536,256]{1,0:T(8,128)(2,1)}, bf16[1536,256]{1,0:T(8,128)(2,1)S(1)}, u32[]{:S(2)}, u32[]{:S(2)}) collective-permute-start(bf16[1536,256]{1,0:T(8,128)(2,1)} %get-tuple-element.19), channel_id=1, source_target_pairs={{0,0},{1,64},{2,2},{3,66},{4,4},{5,68},{6,6},{7,70},{8,8},{9,72},{... | collective-permute-start | bytes 2359304 | tf_op jit(solution)/shard_map/ppermute | solution.py:308
  18.7 9.5 %shard_map.101 = (bf16[2048,512]{1,0:T(8,128)(2,1)}, bf16[2048,512]{1,0:T(8,128)(2,1)}, f32[2,2048]{1,0:T(2,128)}) custom-call(s32[1]{0:T(128)} %bitcast.place.plane, bf16[2048,512]{1,0:T(8,128)(2,1)} %tokens.1, f32[1,512]{1,0:T(1,128)} %bitcast.17, s32[2,2048]{1,0:T(2,128)} %bitcast.14, bf16[1536,256]{1,0:T(8,128)(2,1)} %get-tuple-element.16.after), custom_call_target="tpu_custom_call" | custom-call | flops 4294967296 | bytes 8388608 | tf_op jit(solution)/shard_map/pallas_call | solution.py:93
  28.2 7.2 %all-to-all-start = ((bf16[32,64,512]{2,1,0:T(8,128)(2,1)}), bf16[32,64,512]{2,1,0:T(8,128)(2,1)S(1)}, u32[]{:S(2)}, u32[]{:S(2)}) async-start(bf16[32,64,512]{2,1,0:T(8,128)(2,1)} %bitcast.9), calls=%async_computation | async-start | bytes 4194304 | tf_op jit(solution)/shard_map/all_to_all | solution.py:313
  35.4 7.2 %shard_map.102 = (bf16[2048,128]{1,0:T(8,128)(2,1)}, bf16[2048,128]{1,0:T(8,128)(2,1)}, bf16[2048,128]{1,0:T(8,128)(2,1)}, bf16[2048,128]{1,0:T(8,128)(2,1)}) custom-call(s32[1]{0:T(128)} %bitcast.place.plane, bf16[2048,512]{1,0:T(8,128)(2,1)} %get-tuple-element.20.normed, bf16[512,512]{1,0:T(8,128)(2,1)} %gate.3, bf16[512,512]{1,0:T(8,128)(2,1)} %up.3, ...), custom_call_target="tpu_custom_call" | custom-call | flops 3221225472 | bytes 4194304 | tf_op jit(solution)/shard_map/pallas_call | solution.py:137
  42.7 0.0 collective-permute-done.3.refs_4_.refs_3_
  42.7 3.4 %collective-permute-done.2.refs_3_.refs_2_ = bf16[1536,256]{1,0:T(8,128)(2,1)} collective-permute-done((bf16[1536,256]{1,0:T(8,128)(2,1)}, bf16[1536,256]{1,0:T(8,128)(2,1)}, u32[]{:S(2)}, u32[]{:S(2)}) %collective-permute-start.2) | collective-permute-done | bytes 786464 | tf_op jit(solution)/shard_map/ppermute | solution.py:308
  46.1 0.5 collective-permute-done.refs_0_.refs_1_
  46.5 0.9 copy-done.3
  47.4 0.0 collective-permute-start.4
  47.5 0.5 collective-permute-start.7
  48.0 0.0 collective-permute-start.5
  48.0 0.5 collective-permute-start.6
  48.5 1.5 %collective-permute-start.10 = (bf16[2048,128]{1,0:T(8,128)(2,1)}, bf16[2048,128]{1,0:T(8,128)(2,1)}, u32[]{:S(2)}, u32[]{:S(2)}) collective-permute-start(bf16[2048,128]{1,0:T(8,128)(2,1)} %get-tuple-element.26.refs_10_), channel_id=1, source_target_pairs={{0,96},{32,0},{64,32},{96,64},{1,97},{33,1},{65,33},{97,65},{2,98}... | collective-permute-start | bytes 1572872 | tf_op jit(solution)/shard_map/ppermute | solution.py:317
  50.0 2.3 %collective-permute-start.9 = (bf16[2048,128]{1,0:T(8,128)(2,1)S(1)}, bf16[2048,128]{1,0:T(8,128)(2,1)}, u32[]{:S(2)}, u32[]{:S(2)}) collective-permute-start(bf16[2048,128]{1,0:T(8,128)(2,1)S(1)} %copy-done.7), channel_id=1, source_target_pairs={{0,64},{32,96},{64,0},{96,32},{1,65},{33,97},{65,1},{97,33},{2,66}... | collective-permute-start | bytes 1572872 | tf_op jit(solution)/shard_map/ppermute | solution.py:317
  52.3 0.0 collective-permute-done.7.refs_7_
  52.3 2.0 %collective-permute-start.8 = (bf16[2048,128]{1,0:T(8,128)(2,1)}, bf16[2048,128]{1,0:T(8,128)(2,1)}, u32[]{:S(2)}, u32[]{:S(2)}) collective-permute-start(bf16[2048,128]{1,0:T(8,128)(2,1)} %shard_map.104.refs_8_), channel_id=1, source_target_pairs={{0,32},{32,64},{64,96},{96,0},{1,33},{33,65},{65,97},{97,1},{2,34}... | collective-permute-start | bytes 1572872 | tf_op jit(solution)/shard_map/ppermute | solution.py:317
  54.3 0.9 copy-done.6
  55.2 8.1 %all-to-all-done.slots = bf16[32,64,512]{2,1,0:T(8,128)(2,1)S(1)} async-done(((bf16[32,64,512]{2,1,0:T(8,128)(2,1)}), bf16[32,64,512]{2,1,0:T(8,128)(2,1)S(1)}, u32[]{:S(2)}, u32[]{:S(2)}) %all-to-all-start) | async-done | bytes 2097184 | tf_op jit(solution)/shard_map/all_to_all | solution.py:313
  63.3 1.3 copy-done
  64.6 11.9 %shard_map.106 = bf16[4,1024,128]{2,1,0:T(8,128)(2,1)} custom-call(bf16[32,64,512]{2,1,0:T(8,128)(2,1)} %copy-done, bf16[1536,256]{1,0:T(8,128)(2,1)} %shard_map.103.refs_0_, bf16[1536,256]{1,0:T(8,128)(2,1)} %collective-permute-done.1.refs_2_.refs_1_, bf16[1536,256]{1,0:T(8,128)(2,1)} %collective-permute-done.2.refs_3_.refs_2_, ...), custom_call_target="tpu_custom_call" | custom-call | flops 6442450944 | bytes 8388608 | tf_op jit(solution)/shard_map/pallas_call | solution.py:182
  76.5 7.1 %all-to-all-start.2 = ((bf16[128,32,128]{2,1,0:T(8,128)(2,1)}), bf16[128,32,128]{2,1,0:T(8,128)(2,1)S(1)}, u32[]{:S(2)}, u32[]{:S(2)}) async-start(bf16[128,32,128]{2,1,0:T(8,128)(2,1)} %bitcast.11), calls=%async_computation.2 | async-start | bytes 2097152 | tf_op jit(solution)/shard_map/all_to_all | solution.py:325
  83.7 11.9 %shard_map.105 = bf16[4,1024,128]{2,1,0:T(8,128)(2,1)} custom-call(bf16[32,64,512]{2,1,0:T(8,128)(2,1)} %copy-done, bf16[1536,256]{1,0:T(8,128)(2,1)} %shard_map.103.refs_0_, bf16[1536,256]{1,0:T(8,128)(2,1)} %collective-permute-done.1.refs_2_.refs_1_, bf16[1536,256]{1,0:T(8,128)(2,1)} %collective-permute-done.2.refs_3_.refs_2_, ...), custom_call_target="tpu_custom_call" | custom-call | flops 6442450944 | bytes 8388608 | tf_op jit(solution)/shard_map/pallas_call | solution.py:182
  95.5 7.4 %all-to-all-done.2 = bf16[128,32,128]{2,1,0:T(8,128)(2,1)S(1)} async-done(((bf16[128,32,128]{2,1,0:T(8,128)(2,1)}), bf16[128,32,128]{2,1,0:T(8,128)(2,1)S(1)}, u32[]{:S(2)}, u32[]{:S(2)}) %all-to-all-start.2) | async-done | bytes 1048608 | tf_op jit(solution)/shard_map/all_to_all | solution.py:325
  103.0 4.3 %all-to-all-start.1 = ((bf16[128,32,128]{2,1,0:T(8,128)(2,1)}), bf16[128,32,128]{2,1,0:T(8,128)(2,1)S(1)}, u32[]{:S(2)}, u32[]{:S(2)}) async-start(bf16[128,32,128]{2,1,0:T(8,128)(2,1)} %bitcast.12), calls=%async_computation.1 | async-start | bytes 2097152 | tf_op jit(solution)/shard_map/all_to_all | solution.py:327
  107.3 9.4 %shard_map.107.refs_0_ = f32[2048,128]{1,0:T(8,128)} custom-call(f32[2,2048]{1,0:T(2,128)} %get-tuple-element.17.position, f32[2,2048]{1,0:T(2,128)} %bitcast.15, bf16[4096,128]{1,0:T(8,128)(2,1)} %bitcast.10, bf16[2048,128]{1,0:T(8,128)(2,1)} %get-tuple-element.21.refs_1_.refs_0_, bf16[2048,128]{1,0:T(8,128)(2,1)} %collective-permute-done.8.refs_8_.refs_1_, ...), custom_call_target="tpu_custom_call" | custom-call | flops 2147483648 | bytes 3670016 | tf_op jit(solution)/shard_map/pallas_call | solution.py:257
  116.7 10.0 %all-to-all-done.1 = bf16[128,32,128]{2,1,0:T(8,128)(2,1)S(1)} async-done(((bf16[128,32,128]{2,1,0:T(8,128)(2,1)}), bf16[128,32,128]{2,1,0:T(8,128)(2,1)S(1)}, u32[]{:S(2)}, u32[]{:S(2)}) %all-to-all-start.1) | async-done | bytes 1048608 | tf_op jit(solution)/shard_map/all_to_all | solution.py:327
  126.8 0.9 copy-done.2
  127.7 8.6 %shard_map.108 = bf16[2048,128]{1,0:T(8,128)(2,1)} custom-call(f32[2,2048]{1,0:T(2,128)} %get-tuple-element.17.position, f32[2,2048]{1,0:T(2,128)} %bitcast.16, bf16[4096,128]{1,0:T(8,128)(2,1)} %bitcast.13, f32[2048,128]{1,0:T(8,128)} %shard_map.107.refs_0_), custom_call_target="tpu_custom_call" | custom-call | flops 2147483648 | bytes 3670016 | tf_op jit(solution)/shard_map/pallas_call | solution.py:257
  (21 shorter events, 0.0 us)
Async XLA Ops:
  3.7 38.9 %collective-permute-start.3 = (bf16[1536,256]{1,0:T(8,128)(2,1)}, bf16[1536,256]{1,0:T(8,128)(2,1)}, u32[]{:S(2)}, u32[]{:S(2)}) collective-permute-start(bf16[1536,256]{1,0:T(8,128)(2,1)} %get-tuple-element.16.after), channel_id=1, source_target_pairs={{0,33},{1,97},{2,35},{3,99},{4,37},{5,101},{6,39},{7,103},{8,41},{... | collective-permute-start | bytes 2359304 | tf_op jit(solution)/shard_map/ppermute | solution.py:308
  10.2 32.4 %collective-permute-start.1 = (bf16[1536,256]{1,0:T(8,128)(2,1)}, bf16[1536,256]{1,0:T(8,128)(2,1)}, u32[]{:S(2)}, u32[]{:S(2)}) collective-permute-start(bf16[1536,256]{1,0:T(8,128)(2,1)} %get-tuple-element.22), channel_id=1, source_target_pairs={{0,1},{1,65},{2,3},{3,67},{4,5},{5,69},{6,7},{7,71},{8,9},{9,73},{... | collective-permute-start | bytes 2359304 | tf_op jit(solution)/shard_map/ppermute | solution.py:308
  15.6 30.5 %collective-permute-start.2 = (bf16[1536,256]{1,0:T(8,128)(2,1)}, bf16[1536,256]{1,0:T(8,128)(2,1)}, u32[]{:S(2)}, u32[]{:S(2)}) collective-permute-start(bf16[1536,256]{1,0:T(8,128)(2,1)} %get-tuple-element.23), channel_id=1, source_target_pairs={{0,32},{1,96},{2,34},{3,98},{4,36},{5,100},{6,38},{7,102},{8,40},{... | collective-permute-start | bytes 2359304 | tf_op jit(solution)/shard_map/ppermute | solution.py:308
  16.8 29.7 %collective-permute-start = (bf16[1536,256]{1,0:T(8,128)(2,1)}, bf16[1536,256]{1,0:T(8,128)(2,1)S(1)}, u32[]{:S(2)}, u32[]{:S(2)}) collective-permute-start(bf16[1536,256]{1,0:T(8,128)(2,1)} %get-tuple-element.19), channel_id=1, source_target_pairs={{0,0},{1,64},{2,2},{3,66},{4,4},{5,68},{6,6},{7,70},{8,8},{9,72},{... | collective-permute-start | bytes 2359304 | tf_op jit(solution)/shard_map/ppermute | solution.py:308
  28.2 35.1 %all-to-all-start = ((bf16[32,64,512]{2,1,0:T(8,128)(2,1)}), bf16[32,64,512]{2,1,0:T(8,128)(2,1)S(1)}, u32[]{:S(2)}, u32[]{:S(2)}) async-start(bf16[32,64,512]{2,1,0:T(8,128)(2,1)} %bitcast.9), calls=%async_computation | async-start | bytes 4194304 | tf_op jit(solution)/shard_map/all_to_all | solution.py:313
  46.5 0.9 copy-start.3
  47.4 2.5 %copy-start.7 = (bf16[2048,128]{1,0:T(8,128)(2,1)S(1)}, bf16[2048,128]{1,0:T(8,128)(2,1)}, u32[]{:S(2)}) copy-start(bf16[2048,128]{1,0:T(8,128)(2,1)} %get-tuple-element.25.refs_9_) | copy-start | bytes 1572868
  47.4 2.5 %collective-permute-start.4 = (bf16[1536,256]{1,0:T(8,128)(2,1)}, bf16[1536,256]{1,0:T(8,128)(2,1)S(1)}, u32[]{:S(2)}, u32[]{:S(2)}) collective-permute-start(bf16[1536,256]{1,0:T(8,128)(2,1)} %shard_map.103.refs_0_), channel_id=1, source_target_pairs={{0,1},{1,0},{2,3},{3,2},{4,5},{5,4},{6,7},{7,6},{8,9},{9,8},{10,11... | collective-permute-start | bytes 2359304 | tf_op jit(solution)/shard_map/ppermute | solution.py:320
  47.5 4.9 %collective-permute-start.7 = (bf16[1536,256]{1,0:T(8,128)(2,1)}, bf16[1536,256]{1,0:T(8,128)(2,1)S(1)}, u32[]{:S(2)}, u32[]{:S(2)}) collective-permute-start(bf16[1536,256]{1,0:T(8,128)(2,1)} %collective-permute-done.3.refs_4_.refs_3_), channel_id=1, source_target_pairs={{0,1},{1,0},{2,3},{3,2},{4,5},{5,4},{6,7},{7,6},{8,9},{9,8},{10,11... | collective-permute-start | bytes 2359304 | tf_op jit(solution)/shard_map/ppermute | solution.py:320
  48.0 6.3 %collective-permute-start.5 = (bf16[1536,256]{1,0:T(8,128)(2,1)}, bf16[1536,256]{1,0:T(8,128)(2,1)S(1)}, u32[]{:S(2)}, u32[]{:S(2)}) collective-permute-start(bf16[1536,256]{1,0:T(8,128)(2,1)} %collective-permute-done.1.refs_2_.refs_1_), channel_id=1, source_target_pairs={{0,1},{1,0},{2,3},{3,2},{4,5},{5,4},{6,7},{7,6},{8,9},{9,8},{10,11... | collective-permute-start | bytes 2359304 | tf_op jit(solution)/shard_map/ppermute | solution.py:320
  48.0 7.2 %collective-permute-start.6 = (bf16[1536,256]{1,0:T(8,128)(2,1)}, bf16[1536,256]{1,0:T(8,128)(2,1)}, u32[]{:S(2)}, u32[]{:S(2)}) collective-permute-start(bf16[1536,256]{1,0:T(8,128)(2,1)} %collective-permute-done.2.refs_3_.refs_2_), channel_id=1, source_target_pairs={{0,1},{1,0},{2,3},{3,2},{4,5},{5,4},{6,7},{7,6},{8,9},{9,8},{10,11... | collective-permute-start | bytes 2359304 | tf_op jit(solution)/shard_map/ppermute | solution.py:320
  48.5 35.2 %collective-permute-start.10 = (bf16[2048,128]{1,0:T(8,128)(2,1)}, bf16[2048,128]{1,0:T(8,128)(2,1)}, u32[]{:S(2)}, u32[]{:S(2)}) collective-permute-start(bf16[2048,128]{1,0:T(8,128)(2,1)} %get-tuple-element.26.refs_10_), channel_id=1, source_target_pairs={{0,96},{32,0},{64,32},{96,64},{1,97},{33,1},{65,33},{97,65},{2,98}... | collective-permute-start | bytes 1572872 | tf_op jit(solution)/shard_map/ppermute | solution.py:317
  50.0 13.3 %copy-start.4 = (bf16[1536,256]{1,0:T(8,128)(2,1)}, bf16[1536,256]{1,0:T(8,128)(2,1)S(1)}, u32[]{:S(2)}) copy-start(bf16[1536,256]{1,0:T(8,128)(2,1)S(1)} %collective-permute-done.4.refs_4_) | copy-start | bytes 2359300
  50.0 33.7 %collective-permute-start.9 = (bf16[2048,128]{1,0:T(8,128)(2,1)S(1)}, bf16[2048,128]{1,0:T(8,128)(2,1)}, u32[]{:S(2)}, u32[]{:S(2)}) collective-permute-start(bf16[2048,128]{1,0:T(8,128)(2,1)S(1)} %copy-done.7), channel_id=1, source_target_pairs={{0,64},{32,96},{64,0},{96,32},{1,65},{33,97},{65,1},{97,33},{2,66}... | collective-permute-start | bytes 1572872 | tf_op jit(solution)/shard_map/ppermute | solution.py:317
  52.3 2.0 %copy-start.5 = (bf16[1536,256]{1,0:T(8,128)(2,1)}, bf16[1536,256]{1,0:T(8,128)(2,1)S(1)}, u32[]{:S(2)}) copy-start(bf16[1536,256]{1,0:T(8,128)(2,1)S(1)} %collective-permute-done.7.refs_7_) | copy-start | bytes 2359300
  52.3 31.3 %collective-permute-start.8 = (bf16[2048,128]{1,0:T(8,128)(2,1)}, bf16[2048,128]{1,0:T(8,128)(2,1)}, u32[]{:S(2)}, u32[]{:S(2)}) collective-permute-start(bf16[2048,128]{1,0:T(8,128)(2,1)} %shard_map.104.refs_8_), channel_id=1, source_target_pairs={{0,32},{32,64},{64,96},{96,0},{1,33},{33,65},{65,97},{97,1},{2,34}... | collective-permute-start | bytes 1572872 | tf_op jit(solution)/shard_map/ppermute | solution.py:317
  54.3 0.9 copy-start.6
  63.3 1.3 copy-start
  76.5 26.5 %all-to-all-start.2 = ((bf16[128,32,128]{2,1,0:T(8,128)(2,1)}), bf16[128,32,128]{2,1,0:T(8,128)(2,1)S(1)}, u32[]{:S(2)}, u32[]{:S(2)}) async-start(bf16[128,32,128]{2,1,0:T(8,128)(2,1)} %bitcast.11), calls=%async_computation.2 | async-start | bytes 2097152 | tf_op jit(solution)/shard_map/all_to_all | solution.py:325
  103.0 4.3 %copy-start.1 = (bf16[128,32,128]{2,1,0:T(8,128)(2,1)}, bf16[128,32,128]{2,1,0:T(8,128)(2,1)S(1)}, u32[]{:S(2)}) copy-start(bf16[128,32,128]{2,1,0:T(8,128)(2,1)S(1)} %all-to-all-done.2) | copy-start | bytes 3145732
  103.0 23.8 %all-to-all-start.1 = ((bf16[128,32,128]{2,1,0:T(8,128)(2,1)}), bf16[128,32,128]{2,1,0:T(8,128)(2,1)S(1)}, u32[]{:S(2)}, u32[]{:S(2)}) async-start(bf16[128,32,128]{2,1,0:T(8,128)(2,1)} %bitcast.12), calls=%async_computation.1 | async-start | bytes 2097152 | tf_op jit(solution)/shard_map/all_to_all | solution.py:327
  126.8 0.9 copy-start.2

commit v5 on v4

--- a/solution.py
+++ b/solution.py
@@ -143,7 +143,7 @@
         scratch_shapes=[pltpu.VMEM((block, width), F32)],
         compiler_params=pltpu.CompilerParams(vmem_limit_bytes=VMEM_LIMIT),
         cost_estimate=pl.CostEstimate(
-            flops=6 * rows * width * hidden, bytes_accessed=4 * rows * width, transcendentals=rows * hidden
+            flops=60 * rows * width * hidden, bytes_accessed=4 * rows * width, transcendentals=rows * hidden
         ),
     )(plane, normed, gate, up, down)
 
@@ -203,7 +203,7 @@
     pass
 
 
-def hold(array, *others, flops=0):
+def hold(array, *others):
     anywhere = pl.BlockSpec(memory_space=pl.ANY)
     return pl.pallas_call(
         hold_kernel,
@@ -211,66 +211,43 @@
         in_specs=[anywhere] * (1 + len(others)),
         out_specs=anywhere,
         input_output_aliases={0: 0},
-        cost_estimate=pl.CostEstimate(flops=flops, bytes_accessed=0, transcendentals=0),
     )(array, *others)
 
 
 def combine_kernel(base, position, gates, back, *refs):
-    addends, (out, place, gate, total) = refs[:-4], refs[-4:]
-    step = pl.program_id(0)
-    chunk = back.shape[0]
-    rows = out.shape[0]
-    block = 512
-
-    @pl.when(step == 0)
-    def _():
-        for b in range(rows // block):
-            at = pl.ds(b * block, block)
-            columns = jnp.concatenate([position[:, at], gates[:, at], jnp.zeros((4, block), F32)], axis=0).T
-            for n in range(2):
-                place[n, at, :] = jnp.broadcast_to(columns[:, n : n + 1], (block, 128)).astype(jnp.int32).astype(jnp.int16)
-                gate[n, at, :] = jnp.broadcast_to(columns[:, n + 2 : n + 3], (block, 128)).astype(BF16)
-            total[at, :] = sum(part[at, :].astype(F32) for part in addends)
-
-    lane = lax.broadcasted_iota(jnp.int32, (16, 128), 1) + (step * chunk + base)
-    numbers = [
-        jnp.broadcast_to((lane + j * 128).astype(jnp.int16)[None], (block // 16, 16, 128)).reshape(block, 128)
-        for j in range(chunk // 128)
-    ]
+    addends, out = refs[:-1], refs[-1]
+    rows, slots = out.shape[0], back.shape[0]
+    block, chunk = 512, 1024
+    lane = lax.broadcasted_iota(jnp.int32, (16, 128), 1) + base
+
+    def wide(column):
+        return jnp.broadcast_to(column, (block, 128))
+
     for b in range(rows // block):
         at = pl.ds(b * block, block)
-        first, second, one, two = place[0, at, :], place[1, at, :], gate[0, at, :], gate[1, at, :]
-        weight = [
-            jnp.where(number == first, one, jnp.where(number == second, two, jnp.zeros((), BF16))) for number in numbers
-        ]
-        total[at, :] += dot(jnp.concatenate(weight, axis=1), back[...])
-
-    @pl.when(step == pl.num_programs(0) - 1)
-    def _():
-        out[...] = total[...].astype(out.dtype)
+        columns = jnp.concatenate([position[:, at], gates[:, at], jnp.zeros((4, block), F32)], axis=0).T
+        first, second = [wide(columns[:, n : n + 1]).astype(jnp.int32).astype(jnp.int16) for n in (0, 1)]
+        one, two = [wide(columns[:, n : n + 1]).astype(BF16) for n in (2, 3)]
+        total = sum(part[at, :].astype(F32) for part in addends)
+        for c in range(0, slots, chunk):
+            weight = []
+            for j in range(c, c + chunk, 128):
+                number = (lane + j).astype(jnp.int16)[None]
+                number = jnp.broadcast_to(number, (block // 16, 16, 128)).reshape(block, 128)
+                weight.append(jnp.where(number == first, one, jnp.where(number == second, two, jnp.zeros((), BF16))))
+            total = total + dot(jnp.concatenate(weight, axis=1), back[c : c + chunk, :])
+        out[at, :] = total.astype(out.dtype)
 
 
 def combine(position, gates, back, addends, base, kind):
     rows, part = addends[0].shape
     slots = back.shape[0]
-    chunk = 1024
     return pl.pallas_call(
         functools.partial(combine_kernel, base),
-        grid=(slots // chunk,),
         out_shape=jax.ShapeDtypeStruct((rows, part), kind),
-        in_specs=[
-            pl.BlockSpec((2, rows), lambda i: (0, 0)),
-            pl.BlockSpec((2, rows), lambda i: (0, 0)),
-            pl.BlockSpec((chunk, part), lambda i: (i, 0)),
-        ]
-        + [pl.BlockSpec((rows, part), lambda i: (0, 0))] * len(addends),
-        out_specs=pl.BlockSpec((rows, part), lambda i: (0, 0)),
-        scratch_shapes=[
-            pltpu.VMEM((2, rows, 128), jnp.int16),
-            pltpu.VMEM((2, rows, 128), BF16),
-            pltpu.VMEM((rows, part), F32),
-        ],
-        compiler_params=pltpu.CompilerParams(vmem_limit_bytes=VMEM_LIMIT),
+        in_specs=[pl.BlockSpec(memory_space=pltpu.VMEM)] * (3 + len(addends)),
+        out_specs=pl.BlockSpec(memory_space=pltpu.VMEM),
+        compiler_params=pltpu.CompilerParams(vmem_limit_bytes=40 * 1024 * 1024),
         cost_estimate=pl.CostEstimate(
             flops=2 * rows * slots * part, bytes_accessed=10 * rows * part + 2 * slots * part, transcendentals=0
         ),
@@ -311,8 +288,7 @@
         tokens, norm_gain.reshape(1, width), routes.T, z, columns * planes, cap, planes, sends[-1]
     )
     slots = lax.all_to_all(outgoing.reshape(sectors, -1, width), "sector", 0, 0, tiled=True)
-    shared = list(shared_expert(normed, shared_gate, shared_up, shared_down, z, planes))
-    shared[1] = hold(shared[1], *halves, flops=10**10)
+    shared = shared_expert(normed, shared_gate, shared_up, shared_down, z, planes)
     shared_parts = [shared[0]] + [
         lax.ppermute(shared[k], "expert", [(i, (i + k) % planes) for i in range(planes)]) for k in range(1, planes)
     ]

time: 137 us -> 135 us (0.985)
  Pallas kernels: 62.1 us -> 55.5 us
  local copies, waits for them, and re-layouts: 4.08 us -> 7.71 us
  starting transfers between devices: 40.5 us -> 43.1 us
  waiting for transfers between devices: 29.5 us -> 27.4 us
    pallas_call x2, Pallas kernels: 17.9 us -> 11.4 us  [combine(): pl.pallas_call(functools.partial(combine_kernel, base), out_shape=jax.Sha...]
    ppermute x4, starting transfers between devices: 1.02 us -> 6.36 us  [per_device(): lax.ppermute(half, 'sector', [(s, s ^ 1) for s in range(sectors)])]
    all_to_all x1, waiting for transfers between devices: 8.08 us -> 2.95 us  [per_device(): lax.all_to_all(outgoing.reshape(sectors, -1, width), 'sector', 0, 0, tile...]
    ppermute x3, starting transfers between devices: 5.82 us -> 1.47 us  [per_device(): lax.ppermute(shared[k], 'expert', [(i, (i + k) % planes) for i in range(p...]
    ppermute x4, waiting for transfers between devices: 3.88 us -> 7.68 us  [per_device(): halves.append(lax.ppermute(send, both, moves))]
    unnamed x16 -> x30, local copies, waits for them, and re-layouts: 4.08 us -> 7.71 us
    all_to_all x1, waiting for transfers between devices: 7.45 us -> 4.94 us  [per_device(): lax.all_to_all(first.reshape(planes * sectors, -1, part), both, 0, 0, til...]
    all_to_all x1, starting transfers between devices: 4.33 us -> 6.08 us  [per_device(): lax.all_to_all(second.reshape(planes * sectors, -1, part), both, 0, 0, ti...]
  transfers between devices with their start and end apart: 14 -> 14, of which waited for: 5 -> 6; matrix products, arithmetic and copies ran while one was open for 0% -> 0% of each run, Pallas kernels for 37% -> 34%
where the time goes in v5:
time: 135 us; the launch traced here: 134 us
  Pallas kernels  55.5 us (41%)
  starting transfers between devices  43.1 us (32%)
  waiting for transfers between devices  27.4 us (20%)
  local copies, waits for them, and re-layouts  7.71 us (6%)
    pallas_call x2, Pallas kernels, expert(): pl.pallas_call(functools.partial(expert_kernel, turn), out_shape=jax.Shap...  23.7 us
    ppermute x4, starting transfers between devices, per_device(): halves.append(lax.ppermute(send, both, moves))  14.3 us
    pallas_call x2, Pallas kernels, combine(): pl.pallas_call(functools.partial(combine_kernel, base), out_shape=jax.Sha...  11.4 us
    all_to_all x1, waiting for transfers between devices, per_device(): lax.all_to_all(second.reshape(planes * sectors, -1, part), both, 0, 0, ti...  10.9 us
    pallas_call x1, Pallas kernels, route(): pl.pallas_call(functools.partial(route_kernel, block, cap, stack), grid=(...  9.49 us
    unnamed x30, local copies, waits for them, and re-layouts  7.71 us
    ppermute x4, waiting for transfers between devices, per_device(): halves.append(lax.ppermute(send, both, moves))  7.68 us
    all_to_all x1, starting transfers between devices, per_device(): lax.all_to_all(first.reshape(planes * sectors, -1, part), both, 0, 0, til...  7.56 us
  transfers between devices with their start and end apart: 14, of which 6 were waited for; matrix products, arithmetic and copies ran while one was open for 0% of the time, Pallas kernels for 34%

profile of v5, /device:TPU:1, one launch (start us, length us, event | category | flops | bytes accessed | tf_op | source)
XLA Modules:
  0.0 133.9 jit_solution(6668103368121157949)
XLA Ops:
  0.0 3.7 %shard_map.100 = (bf16[1536,256]{1,0:T(8,128)(2,1)}, bf16[1536,256]{1,0:T(8,128)(2,1)}, bf16[1536,256]{1,0:T(8,128)(2,1)}, bf16[1536,256]{1,0:T(8,128)(2,1)}) custom-call(s32[1]{0:T(128)} %bitcast.place.plane, bf16[2,512,512]{2,1,0:T(8,128)(2,1)} %gate.2, bf16[2,512,512]{2,1,0:T(8,128)(2,1)} %up.2, bf16[2,512,512]{2,1,0:T(8,128)(2,1)} %down.2), custom_call_target="tpu_custom_call" | custom-call | bytes 6291456 | tf_op jit(solution)/shard_map/pallas_call | solution.py:40
  3.7 6.9 %collective-permute-start = (bf16[1536,256]{1,0:T(8,128)(2,1)}, bf16[1536,256]{1,0:T(8,128)(2,1)}, u32[]{:S(2)}, u32[]{:S(2)}) collective-permute-start(bf16[1536,256]{1,0:T(8,128)(2,1)} %get-tuple-element.19), channel_id=1, source_target_pairs={{0,0},{1,64},{2,2},{3,66},{4,4},{5,68},{6,6},{7,70},{8,8},{9,72},{... | collective-permute-start | bytes 2359304 | tf_op jit(solution)/shard_map/ppermute | solution.py:285
  10.6 7.0 %collective-permute-start.3 = (bf16[1536,256]{1,0:T(8,128)(2,1)}, bf16[1536,256]{1,0:T(8,128)(2,1)S(1)}, u32[]{:S(2)}, u32[]{:S(2)}) collective-permute-start(bf16[1536,256]{1,0:T(8,128)(2,1)} %get-tuple-element.16.after), channel_id=1, source_target_pairs={{0,33},{1,97},{2,35},{3,99},{4,37},{5,101},{6,39},{7,103},{8,41},{... | collective-permute-start | bytes 2359304 | tf_op jit(solution)/shard_map/ppermute | solution.py:285
  17.7 9.5 %shard_map.101 = (bf16[2048,512]{1,0:T(8,128)(2,1)}, bf16[2048,512]{1,0:T(8,128)(2,1)}, f32[2,2048]{1,0:T(2,128)}) custom-call(s32[1]{0:T(128)} %bitcast.place.plane, bf16[2048,512]{1,0:T(8,128)(2,1)} %tokens.1, f32[1,512]{1,0:T(1,128)} %bitcast.17, s32[2,2048]{1,0:T(2,128)} %bitcast.16, bf16[1536,256]{1,0:T(8,128)(2,1)} %get-tuple-element.16.after), custom_call_target="tpu_custom_call" | custom-call | flops 4294967296 | bytes 8388608 | tf_op jit(solution)/shard_map/pallas_call | solution.py:93
  27.2 7.4 %all-to-all-start = ((bf16[32,64,512]{2,1,0:T(8,128)(2,1)}), bf16[32,64,512]{2,1,0:T(8,128)(2,1)}, u32[]{:S(2)}, u32[]{:S(2)}) async-start(bf16[32,64,512]{2,1,0:T(8,128)(2,1)} %bitcast.13), calls=%async_computation | async-start | bytes 4194304 | tf_op jit(solution)/shard_map/all_to_all | solution.py:290
  34.6 0.1 collective-permute-start.1
  34.7 0.3 collective-permute-start.2
  34.9 7.2 %shard_map.102 = (bf16[2048,128]{1,0:T(8,128)(2,1)}, bf16[2048,128]{1,0:T(8,128)(2,1)}, bf16[2048,128]{1,0:T(8,128)(2,1)}, bf16[2048,128]{1,0:T(8,128)(2,1)}) custom-call(s32[1]{0:T(128)} %bitcast.place.plane, bf16[2048,512]{1,0:T(8,128)(2,1)} %get-tuple-element.20.normed, bf16[512,512]{1,0:T(8,128)(2,1)} %gate.3, bf16[512,512]{1,0:T(8,128)(2,1)} %up.3, ...), custom_call_target="tpu_custom_call" | custom-call | flops 32212254720 | bytes 4194304 | tf_op jit(solution)/shard_map/pallas_call | solution.py:137
  42.1 2.1 %collective-permute-start.4 = (bf16[1536,256]{1,0:T(8,128)(2,1)}, bf16[1536,256]{1,0:T(8,128)(2,1)S(1)}, u32[]{:S(2)}, u32[]{:S(2)}) collective-permute-start(bf16[1536,256]{1,0:T(8,128)(2,1)} %shard_map.103.refs_0_), channel_id=1, source_target_pairs={{0,1},{1,0},{2,3},{3,2},{4,5},{5,4},{6,7},{7,6},{8,9},{9,8},{10,11... | collective-permute-start | bytes 2359304 | tf_op jit(solution)/shard_map/ppermute | solution.py:296
  44.3 0.1 collective-permute-start.7
  44.4 5.7 %collective-permute-done.1.refs_1_ = bf16[1536,256]{1,0:T(8,128)(2,1)} collective-permute-done((bf16[1536,256]{1,0:T(8,128)(2,1)}, bf16[1536,256]{1,0:T(8,128)(2,1)}, u32[]{:S(2)}, u32[]{:S(2)}) %collective-permute-start.1) | collective-permute-done | bytes 786464 | tf_op jit(solution)/shard_map/ppermute | solution.py:285
  50.0 4.1 %collective-permute-start.5 = (bf16[1536,256]{1,0:T(8,128)(2,1)}, bf16[1536,256]{1,0:T(8,128)(2,1)}, u32[]{:S(2)}, u32[]{:S(2)}) collective-permute-start(bf16[1536,256]{1,0:T(8,128)(2,1)} %collective-permute-done.1.refs_1_), channel_id=1, source_target_pairs={{0,1},{1,0},{2,3},{3,2},{4,5},{5,4},{6,7},{7,6},{8,9},{9,8},{10,11... | collective-permute-start | bytes 2359304 | tf_op jit(solution)/shard_map/ppermute | solution.py:296
  54.2 2.0 %collective-permute-done.2.refs_2_ = bf16[1536,256]{1,0:T(8,128)(2,1)} collective-permute-done((bf16[1536,256]{1,0:T(8,128)(2,1)S(1)}, bf16[1536,256]{1,0:T(8,128)(2,1)}, u32[]{:S(2)}, u32[]{:S(2)}) %collective-permute-start.2) | collective-permute-done | bytes 786464 | tf_op jit(solution)/shard_map/ppermute | solution.py:285
  56.2 0.9 copy-done.12
  57.1 1.4 %collective-permute-start.8 = (bf16[2048,128]{1,0:T(8,128)(2,1)}, bf16[2048,128]{1,0:T(8,128)(2,1)S(1)}, u32[]{:S(2)}, u32[]{:S(2)}) collective-permute-start(bf16[2048,128]{1,0:T(8,128)(2,1)} %get-tuple-element.24.refs_8_), channel_id=1, source_target_pairs={{0,32},{32,64},{64,96},{96,0},{1,33},{33,65},{65,97},{97,1},{2,34}... | collective-permute-start | bytes 1572872 | tf_op jit(solution)/shard_map/ppermute | solution.py:293
  58.6 0.9 copy-done.13
  59.5 3.0 %all-to-all-done.slots = bf16[32,64,512]{2,1,0:T(8,128)(2,1)} async-done(((bf16[32,64,512]{2,1,0:T(8,128)(2,1)}), bf16[32,64,512]{2,1,0:T(8,128)(2,1)}, u32[]{:S(2)}, u32[]{:S(2)}) %all-to-all-start) | async-done | bytes 2097184 | tf_op jit(solution)/shard_map/all_to_all | solution.py:290
  62.4 11.9 %shard_map.105 = bf16[4,1024,128]{2,1,0:T(8,128)(2,1)} custom-call(bf16[32,64,512]{2,1,0:T(8,128)(2,1)} %all-to-all-done.slots, bf16[1536,256]{1,0:T(8,128)(2,1)} %shard_map.103.refs_0_, bf16[1536,256]{1,0:T(8,128)(2,1)} %collective-permute-done.1.refs_1_, bf16[1536,256]{1,0:T(8,128)(2,1)} %collective-permute-done.2.refs_2_, bf16[1536,256]{1,0:T(8,128)(2,1)} %copy-done.11, ...), custom_call_target="tpu_custom_call" | custom-call | flops 6442450944 | bytes 8388608 | tf_op jit(solution)/shard_map/pallas_call | solution.py:182
  74.3 7.6 %all-to-all-start.2 = ((bf16[128,32,128]{2,1,0:T(8,128)(2,1)}), bf16[128,32,128]{2,1,0:T(8,128)(2,1)S(1)}, u32[]{:S(2)}, u32[]{:S(2)}) async-start(bf16[128,32,128]{2,1,0:T(8,128)(2,1)} %bitcast.14), calls=%async_computation.2 | async-start | bytes 2097152 | tf_op jit(solution)/shard_map/all_to_all | solution.py:301
  81.9 0.9 collective-permute-done.8.refs_8_.refs_1_
  82.8 0.8 copy-done.3
  83.6 0.8 copy-done.5
  84.4 11.8 %shard_map.104 = bf16[4,1024,128]{2,1,0:T(8,128)(2,1)} custom-call(bf16[32,64,512]{2,1,0:T(8,128)(2,1)} %all-to-all-done.slots, bf16[1536,256]{1,0:T(8,128)(2,1)} %shard_map.103.refs_0_, bf16[1536,256]{1,0:T(8,128)(2,1)} %collective-permute-done.1.refs_1_, bf16[1536,256]{1,0:T(8,128)(2,1)} %collective-permute-done.2.refs_2_, bf16[1536,256]{1,0:T(8,128)(2,1)} %copy-done.11, ...), custom_call_target="tpu_custom_call" | custom-call | flops 6442450944 | bytes 8388608 | tf_op jit(solution)/shard_map/pallas_call | solution.py:182
  96.3 4.9 %all-to-all-done.2 = bf16[128,32,128]{2,1,0:T(8,128)(2,1)S(1)} async-done(((bf16[128,32,128]{2,1,0:T(8,128)(2,1)}), bf16[128,32,128]{2,1,0:T(8,128)(2,1)S(1)}, u32[]{:S(2)}, u32[]{:S(2)}) %all-to-all-start.2) | async-done | bytes 1048608 | tf_op jit(solution)/shard_map/all_to_all | solution.py:301
  101.2 6.1 %all-to-all-start.1 = ((bf16[128,32,128]{2,1,0:T(8,128)(2,1)}), bf16[128,32,128]{2,1,0:T(8,128)(2,1)S(1)}, u32[]{:S(2)}, u32[]{:S(2)}) async-start(bf16[128,32,128]{2,1,0:T(8,128)(2,1)} %bitcast.15), calls=%async_computation.1 | async-start | bytes 2097152 | tf_op jit(solution)/shard_map/all_to_all | solution.py:303
  107.3 1.0 copy-done.4
  108.4 1.0 copy-done.6
  109.4 5.3 %shard_map.106.refs_0_ = f32[2048,128]{1,0:T(8,128)S(1)} custom-call(f32[2,2048]{1,0:T(2,128)S(1)} %copy-done.10, f32[2,2048]{1,0:T(2,128)S(1)} %bitcast.11, bf16[4096,128]{1,0:T(8,128)(2,1)S(1)} %bitcast.9, bf16[2048,128]{1,0:T(8,128)(2,1)S(1)} %copy-done, bf16[2048,128]{1,0:T(8,128)(2,1)S(1)} %copy-done.4, bf16[2048,128]{1,0:T(8,128)(2,1)S(1)} %copy-done.6, ...), custom_call_target="tpu_custom_call" | custom-call | flops 2147483648 | bytes 3670016 | tf_op jit(solution)/shard_map/pallas_call | solution.py:245
  114.7 1.0 copy-done.8
  115.7 10.9 %all-to-all-done.1 = bf16[128,32,128]{2,1,0:T(8,128)(2,1)S(1)} async-done(((bf16[128,32,128]{2,1,0:T(8,128)(2,1)}), bf16[128,32,128]{2,1,0:T(8,128)(2,1)S(1)}, u32[]{:S(2)}, u32[]{:S(2)}) %all-to-all-start.1) | async-done | bytes 1048608 | tf_op jit(solution)/shard_map/all_to_all | solution.py:303
  126.6 1.2 copy-done.9
  127.9 6.1 %shard_map.107 = bf16[2048,128]{1,0:T(8,128)(2,1)} custom-call(f32[2,2048]{1,0:T(2,128)S(1)} %copy-done.10, f32[2,2048]{1,0:T(2,128)S(1)} %bitcast.12, bf16[4096,128]{1,0:T(8,128)(2,1)S(1)} %bitcast.10, f32[2048,128]{1,0:T(8,128)S(1)} %copy-done.9), custom_call_target="tpu_custom_call" | custom-call | flops 2147483648 | bytes 3670016 | tf_op jit(solution)/shard_map/pallas_call | solution.py:245
  (34 shorter events, 0.1 us)
Async XLA Ops:
  3.7 38.4 %collective-permute-start = (bf16[1536,256]{1,0:T(8,128)(2,1)}, bf16[1536,256]{1,0:T(8,128)(2,1)}, u32[]{:S(2)}, u32[]{:S(2)}) collective-permute-start(bf16[1536,256]{1,0:T(8,128)(2,1)} %get-tuple-element.19), channel_id=1, source_target_pairs={{0,0},{1,64},{2,2},{3,66},{4,4},{5,68},{6,6},{7,70},{8,8},{9,72},{... | collective-permute-start | bytes 2359304 | tf_op jit(solution)/shard_map/ppermute | solution.py:285
  10.6 33.6 %collective-permute-start.3 = (bf16[1536,256]{1,0:T(8,128)(2,1)}, bf16[1536,256]{1,0:T(8,128)(2,1)S(1)}, u32[]{:S(2)}, u32[]{:S(2)}) collective-permute-start(bf16[1536,256]{1,0:T(8,128)(2,1)} %get-tuple-element.16.after), channel_id=1, source_target_pairs={{0,33},{1,97},{2,35},{3,99},{4,37},{5,101},{6,39},{7,103},{8,41},{... | collective-permute-start | bytes 2359304 | tf_op jit(solution)/shard_map/ppermute | solution.py:285
  27.2 7.5 %copy-start.14 = (bf16[1536,256]{1,0:T(8,128)(2,1)S(1)}, bf16[1536,256]{1,0:T(8,128)(2,1)}, u32[]{:S(2)}) copy-start(bf16[1536,256]{1,0:T(8,128)(2,1)} %get-tuple-element.23) | copy-start | bytes 2359300
  27.2 35.3 %all-to-all-start = ((bf16[32,64,512]{2,1,0:T(8,128)(2,1)}), bf16[32,64,512]{2,1,0:T(8,128)(2,1)}, u32[]{:S(2)}, u32[]{:S(2)}) async-start(bf16[32,64,512]{2,1,0:T(8,128)(2,1)} %bitcast.13), calls=%async_computation | async-start | bytes 4194304 | tf_op jit(solution)/shard_map/all_to_all | solution.py:290
  34.6 15.5 %collective-permute-start.1 = (bf16[1536,256]{1,0:T(8,128)(2,1)}, bf16[1536,256]{1,0:T(8,128)(2,1)}, u32[]{:S(2)}, u32[]{:S(2)}) collective-permute-start(bf16[1536,256]{1,0:T(8,128)(2,1)} %get-tuple-element.22), channel_id=1, source_target_pairs={{0,1},{1,65},{2,3},{3,67},{4,5},{5,69},{6,7},{7,71},{8,9},{9,73},{... | collective-permute-start | bytes 2359304 | tf_op jit(solution)/shard_map/ppermute | solution.py:285
  34.7 21.5 %collective-permute-start.2 = (bf16[1536,256]{1,0:T(8,128)(2,1)S(1)}, bf16[1536,256]{1,0:T(8,128)(2,1)}, u32[]{:S(2)}, u32[]{:S(2)}) collective-permute-start(bf16[1536,256]{1,0:T(8,128)(2,1)S(1)} %copy-done.14), channel_id=1, source_target_pairs={{0,32},{1,96},{2,34},{3,98},{4,36},{5,100},{6,38},{7,102},{8,40},{... | collective-permute-start | bytes 2359304 | tf_op jit(solution)/shard_map/ppermute | solution.py:285
  42.1 14.1 %collective-permute-start.4 = (bf16[1536,256]{1,0:T(8,128)(2,1)}, bf16[1536,256]{1,0:T(8,128)(2,1)S(1)}, u32[]{:S(2)}, u32[]{:S(2)}) collective-permute-start(bf16[1536,256]{1,0:T(8,128)(2,1)} %shard_map.103.refs_0_), channel_id=1, source_target_pairs={{0,1},{1,0},{2,3},{3,2},{4,5},{5,4},{6,7},{7,6},{8,9},{9,8},{10,11... | collective-permute-start | bytes 2359304 | tf_op jit(solution)/shard_map/ppermute | solution.py:296
  44.3 18.2 %copy-start.11 = (bf16[1536,256]{1,0:T(8,128)(2,1)}, bf16[1536,256]{1,0:T(8,128)(2,1)S(1)}, u32[]{:S(2)}) copy-start(bf16[1536,256]{1,0:T(8,128)(2,1)S(1)} %collective-permute-done.3.refs_3_) | copy-start | bytes 2359300
  44.3 14.3 %collective-permute-start.7 = (bf16[1536,256]{1,0:T(8,128)(2,1)S(1)}, bf16[1536,256]{1,0:T(8,128)(2,1)S(1)}, u32[]{:S(2)}, u32[]{:S(2)}) collective-permute-start(bf16[1536,256]{1,0:T(8,128)(2,1)S(1)} %collective-permute-done.3.refs_3_), channel_id=1, source_target_pairs={{0,1},{1,0},{2,3},{3,2},{4,5},{5,4},{6,7},{7,6},{8,9},{9,8},{10,11... | collective-permute-start | bytes 2359304 | tf_op jit(solution)/shard_map/ppermute | solution.py:296
  50.0 9.4 %collective-permute-start.5 = (bf16[1536,256]{1,0:T(8,128)(2,1)}, bf16[1536,256]{1,0:T(8,128)(2,1)}, u32[]{:S(2)}, u32[]{:S(2)}) collective-permute-start(bf16[1536,256]{1,0:T(8,128)(2,1)} %collective-permute-done.1.refs_1_), channel_id=1, source_target_pairs={{0,1},{1,0},{2,3},{3,2},{4,5},{5,4},{6,7},{7,6},{8,9},{9,8},{10,11... | collective-permute-start | bytes 2359304 | tf_op jit(solution)/shard_map/ppermute | solution.py:296
  56.2 3.3 %collective-permute-start.6 = (bf16[1536,256]{1,0:T(8,128)(2,1)}, bf16[1536,256]{1,0:T(8,128)(2,1)}, u32[]{:S(2)}, u32[]{:S(2)}) collective-permute-start(bf16[1536,256]{1,0:T(8,128)(2,1)} %collective-permute-done.2.refs_2_), channel_id=1, source_target_pairs={{0,1},{1,0},{2,3},{3,2},{4,5},{5,4},{6,7},{7,6},{8,9},{9,8},{10,11... | collective-permute-start | bytes 2359304 | tf_op jit(solution)/shard_map/ppermute | solution.py:296
  56.2 25.7 %collective-permute-start.10 = (bf16[2048,128]{1,0:T(8,128)(2,1)}, bf16[2048,128]{1,0:T(8,128)(2,1)S(1)}, u32[]{:S(2)}, u32[]{:S(2)}) collective-permute-start(bf16[2048,128]{1,0:T(8,128)(2,1)} %get-tuple-element.26.refs_10_), channel_id=1, source_target_pairs={{0,96},{32,0},{64,32},{96,64},{1,97},{33,1},{65,33},{97,65},{2,98}... | collective-permute-start | bytes 1572872 | tf_op jit(solution)/shard_map/ppermute | solution.py:293
  56.2 0.9 copy-start.12
  57.1 25.7 %collective-permute-start.8 = (bf16[2048,128]{1,0:T(8,128)(2,1)}, bf16[2048,128]{1,0:T(8,128)(2,1)S(1)}, u32[]{:S(2)}, u32[]{:S(2)}) collective-permute-start(bf16[2048,128]{1,0:T(8,128)(2,1)} %get-tuple-element.24.refs_8_), channel_id=1, source_target_pairs={{0,32},{32,64},{64,96},{96,0},{1,33},{33,65},{65,97},{97,1},{2,34}... | collective-permute-start | bytes 1572872 | tf_op jit(solution)/shard_map/ppermute | solution.py:293
  58.6 0.9 copy-start.13
  59.5 23.3 %collective-permute-start.9 = (bf16[2048,128]{1,0:T(8,128)(2,1)}, bf16[2048,128]{1,0:T(8,128)(2,1)S(1)}, u32[]{:S(2)}, u32[]{:S(2)}) collective-permute-start(bf16[2048,128]{1,0:T(8,128)(2,1)} %get-tuple-element.25.refs_9_), channel_id=1, source_target_pairs={{0,64},{32,96},{64,0},{96,32},{1,65},{33,97},{65,1},{97,33},{2,66}... | collective-permute-start | bytes 1572872 | tf_op jit(solution)/shard_map/ppermute | solution.py:293
  74.3 26.9 %all-to-all-start.2 = ((bf16[128,32,128]{2,1,0:T(8,128)(2,1)}), bf16[128,32,128]{2,1,0:T(8,128)(2,1)S(1)}, u32[]{:S(2)}, u32[]{:S(2)}) async-start(bf16[128,32,128]{2,1,0:T(8,128)(2,1)} %bitcast.14), calls=%async_computation.2 | async-start | bytes 2097152 | tf_op jit(solution)/shard_map/all_to_all | solution.py:301
  81.9 0.9 copy-start.1
  82.8 0.8 copy-start.3
  83.6 0.8 copy-start.5
  96.2 11.1 %copy-start = (bf16[2048,128]{1,0:T(8,128)(2,1)S(1)}, bf16[2048,128]{1,0:T(8,128)(2,1)}, u32[]{:S(2)}) copy-start(bf16[2048,128]{1,0:T(8,128)(2,1)} %get-tuple-element.21.refs_1_.refs_0_) | copy-start | bytes 1572868
  96.2 11.1 %copy-start.2 = (bf16[2048,128]{1,0:T(8,128)(2,1)S(1)}, bf16[2048,128]{1,0:T(8,128)(2,1)}, u32[]{:S(2)}) copy-start(bf16[2048,128]{1,0:T(8,128)(2,1)} %copy-done.1) | copy-start | bytes 1572868
  96.3 11.1 %copy-start.7 = (f32[2048,2]{0,1:T(2,128)S(1)}, f32[2048,2]{0,1:T(2,128)}, u32[]{:S(2)}) copy-start(f32[2048,2]{0,1:T(2,128)} %param.13) | copy-start | bytes 49156
  96.3 11.1 %copy-start.10 = (f32[2,2048]{1,0:T(2,128)S(1)}, f32[2,2048]{1,0:T(2,128)}, u32[]{:S(2)}) copy-start(f32[2,2048]{1,0:T(2,128)} %get-tuple-element.17.position) | copy-start | bytes 49156
  101.2 25.4 %all-to-all-start.1 = ((bf16[128,32,128]{2,1,0:T(8,128)(2,1)}), bf16[128,32,128]{2,1,0:T(8,128)(2,1)S(1)}, u32[]{:S(2)}, u32[]{:S(2)}) async-start(bf16[128,32,128]{2,1,0:T(8,128)(2,1)} %bitcast.15), calls=%async_computation.1 | async-start | bytes 2097152 | tf_op jit(solution)/shard_map/all_to_all | solution.py:303
  107.3 1.0 copy-start.4
  108.4 1.0 copy-start.6
  114.7 1.0 copy-start.8
  126.6 1.2 copy-start.9

commit v6 on v5

--- a/solution.py
+++ b/solution.py
@@ -297,12 +297,12 @@
 
     part = width // planes
     gates = gates.T
-    first = expert(slots, weights, planes, 0, shared[1:])
+    first = expert(slots, weights, planes, 0, ())
     first = lax.all_to_all(first.reshape(planes * sectors, -1, part), both, 0, 0, tiled=True).reshape(-1, part)
-    second = expert(slots, weights, planes, 1, shared_parts[1:])
+    second = expert(slots, weights, planes, 1, shared[1:])
     second = lax.all_to_all(second.reshape(planes * sectors, -1, part), both, 0, 0, tiled=True).reshape(-1, part)
-    mixed = combine(position, gates, first, shared_parts, 0, F32)
-    return combine(position, gates, second, [mixed], first.shape[0], BF16)
+    mixed = combine(position, gates, first, shared_parts[:1], 0, F32)
+    return combine(position, gates, second, [mixed] + shared_parts[1:], first.shape[0], BF16)
 
 
 def solution(mesh):

time: 135 us -> 170 us (1.26)
  waiting for transfers between devices: 27.4 us -> 54.6 us
  starting transfers between devices: 43.1 us -> 50 us
    ppermute x3, waiting for transfers between devices: 0.91 us -> 26.5 us  [per_device(): lax.ppermute(shared[k], 'expert', [(i, (i + k) % planes) for i in range(p...]
    all_to_all x1, waiting for transfers between devices: 10.9 us -> 0.01 us  [per_device(): lax.all_to_all(second.reshape(planes * sectors, -1, part), both, 0, 0, ti...]
    all_to_all x1, starting transfers between devices: 7.56 us -> 17 us  [per_device(): lax.all_to_all(first.reshape(planes * sectors, -1, part), both, 0, 0, til...]
    ppermute x4, waiting for transfers between devices: 7.68 us -> 16.6 us  [per_device(): halves.append(lax.ppermute(send, both, moves))]
    ppermute x4, starting transfers between devices: 6.36 us -> 0.78 us  [per_device(): lax.ppermute(half, 'sector', [(s, s ^ 1) for s in range(sectors)])]
    ppermute x3, starting transfers between devices: 1.47 us -> 5.52 us  [per_device(): lax.ppermute(shared[k], 'expert', [(i, (i + k) % planes) for i in range(p...]
    ppermute x4, waiting for transfers between devices: 0.01 us -> 3.96 us  [per_device(): lax.ppermute(half, 'sector', [(s, s ^ 1) for s in range(sectors)])]
    all_to_all x1, waiting for transfers between devices: 2.95 us -> 0.01 us  [per_device(): lax.all_to_all(outgoing.reshape(sectors, -1, width), 'sector', 0, 0, tile...]
  transfers between devices with their start and end apart: 14 -> 14, of which waited for: 6 -> 7; matrix products, arithmetic and copies ran while one was open for 0% -> 0% of each run, Pallas kernels for 34% -> 20%
where the time goes in v6:
time: 170 us; the launch traced here: 169 us
  Pallas kernels  55.5 us (33%)
  waiting for transfers between devices  54.6 us (32%)
  starting transfers between devices  50 us (29%)
  local copies, waits for them, and re-layouts  9.11 us (5%)
    ppermute x3, waiting for transfers between devices, per_device(): lax.ppermute(shared[k], 'expert', [(i, (i + k) % planes) for i in range(p...  26.5 us
    pallas_call x2, Pallas kernels, expert(): pl.pallas_call(functools.partial(expert_kernel, turn), out_shape=jax.Shap...  23.7 us
    all_to_all x1, starting transfers between devices, per_device(): lax.all_to_all(first.reshape(planes * sectors, -1, part), both, 0, 0, til...  17 us
    ppermute x4, waiting for transfers between devices, per_device(): halves.append(lax.ppermute(send, both, moves))  16.6 us
    ppermute x4, starting transfers between devices, per_device(): halves.append(lax.ppermute(send, both, moves))  15.2 us
    pallas_call x2, Pallas kernels, combine(): pl.pallas_call(functools.partial(combine_kernel, base), out_shape=jax.Sha...  11.4 us
    pallas_call x1, Pallas kernels, route(): pl.pallas_call(functools.partial(route_kernel, block, cap, stack), grid=(...  9.49 us
    unnamed x28, local copies, waits for them, and re-layouts  9.11 us
  transfers between devices with their start and end apart: 14, of which 7 were waited for; matrix products, arithmetic and copies ran while one was open for 0% of the time, Pallas kernels for 20%

profile of v6, /device:TPU:1, one launch (start us, length us, event | category | flops | bytes accessed | tf_op | source)
XLA Modules:
  0.0 169.4 jit_solution(12309890843933086931)
XLA Ops:
  0.0 3.7 %shard_map.100 = (bf16[1536,256]{1,0:T(8,128)(2,1)}, bf16[1536,256]{1,0:T(8,128)(2,1)}, bf16[1536,256]{1,0:T(8,128)(2,1)}, bf16[1536,256]{1,0:T(8,128)(2,1)}) custom-call(s32[1]{0:T(128)} %bitcast.place.plane, bf16[2,512,512]{2,1,0:T(8,128)(2,1)} %gate.2, bf16[2,512,512]{2,1,0:T(8,128)(2,1)} %up.2, bf16[2,512,512]{2,1,0:T(8,128)(2,1)} %down.2), custom_call_target="tpu_custom_call" | custom-call | bytes 6291456 | tf_op jit(solution)/shard_map/pallas_call | solution.py:40
  3.7 6.5 %collective-permute-start.3 = (bf16[1536,256]{1,0:T(8,128)(2,1)}, bf16[1536,256]{1,0:T(8,128)(2,1)}, u32[]{:S(2)}, u32[]{:S(2)}) collective-permute-start(bf16[1536,256]{1,0:T(8,128)(2,1)} %get-tuple-element.16.after), channel_id=1, source_target_pairs={{0,33},{1,97},{2,35},{3,99},{4,37},{5,101},{6,39},{7,103},{8,41},{... | collective-permute-start | bytes 2359304 | tf_op jit(solution)/shard_map/ppermute | solution.py:285
  10.2 9.5 %shard_map.101 = (bf16[2048,512]{1,0:T(8,128)(2,1)}, bf16[2048,512]{1,0:T(8,128)(2,1)}, f32[2,2048]{1,0:T(2,128)}) custom-call(s32[1]{0:T(128)} %bitcast.place.plane, bf16[2048,512]{1,0:T(8,128)(2,1)} %tokens.1, f32[1,512]{1,0:T(1,128)} %bitcast.17, s32[2,2048]{1,0:T(2,128)} %bitcast.16, bf16[1536,256]{1,0:T(8,128)(2,1)} %get-tuple-element.16.after), custom_call_target="tpu_custom_call" | custom-call | flops 4294967296 | bytes 8388608 | tf_op jit(solution)/shard_map/pallas_call | solution.py:93
  19.7 7.2 %all-to-all-start = ((bf16[32,64,512]{2,1,0:T(8,128)(2,1)}), bf16[32,64,512]{2,1,0:T(8,128)(2,1)S(1)}, u32[]{:S(2)}, u32[]{:S(2)}) async-start(bf16[32,64,512]{2,1,0:T(8,128)(2,1)} %bitcast.13), calls=%async_computation | async-start | bytes 4194304 | tf_op jit(solution)/shard_map/all_to_all | solution.py:290
  26.9 7.3 %collective-permute-start = (bf16[1536,256]{1,0:T(8,128)(2,1)}, bf16[1536,256]{1,0:T(8,128)(2,1)S(1)}, u32[]{:S(2)}, u32[]{:S(2)}) collective-permute-start(bf16[1536,256]{1,0:T(8,128)(2,1)} %get-tuple-element.19), channel_id=1, source_target_pairs={{0,0},{1,64},{2,2},{3,66},{4,4},{5,68},{6,6},{7,70},{8,8},{9,72},{... | collective-permute-start | bytes 2359304 | tf_op jit(solution)/shard_map/ppermute | solution.py:285
  34.4 1.3 collective-permute-start.2
  35.7 7.2 %shard_map.102 = (bf16[2048,128]{1,0:T(8,128)(2,1)}, bf16[2048,128]{1,0:T(8,128)(2,1)}, bf16[2048,128]{1,0:T(8,128)(2,1)}, bf16[2048,128]{1,0:T(8,128)(2,1)}) custom-call(s32[1]{0:T(128)} %bitcast.place.plane, bf16[2048,512]{1,0:T(8,128)(2,1)} %get-tuple-element.20.normed, bf16[512,512]{1,0:T(8,128)(2,1)} %gate.3, bf16[512,512]{1,0:T(8,128)(2,1)} %up.3, ...), custom_call_target="tpu_custom_call" | custom-call | flops 32212254720 | bytes 4194304 | tf_op jit(solution)/shard_map/pallas_call | solution.py:137
  42.8 8.3 %collective-permute-done.refs_0_ = bf16[1536,256]{1,0:T(8,128)(2,1)S(1)} collective-permute-done((bf16[1536,256]{1,0:T(8,128)(2,1)}, bf16[1536,256]{1,0:T(8,128)(2,1)S(1)}, u32[]{:S(2)}, u32[]{:S(2)}) %collective-permute-start) | collective-permute-done | bytes 786464 | tf_op jit(solution)/shard_map/ppermute | solution.py:285
  51.2 0.9 copy-done.10
  52.1 8.3 %collective-permute-done.1.refs_1_ = bf16[1536,256]{1,0:T(8,128)(2,1)} collective-permute-done((bf16[1536,256]{1,0:T(8,128)(2,1)}, bf16[1536,256]{1,0:T(8,128)(2,1)}, u32[]{:S(2)}, u32[]{:S(2)}) %collective-permute-start.1) | collective-permute-done | bytes 786464 | tf_op jit(solution)/shard_map/ppermute | solution.py:285
  61.2 1.7 %collective-permute-done.5.refs_5_ = bf16[1536,256]{1,0:T(8,128)(2,1)S(1)} collective-permute-done((bf16[1536,256]{1,0:T(8,128)(2,1)}, bf16[1536,256]{1,0:T(8,128)(2,1)S(1)}, u32[]{:S(2)}, u32[]{:S(2)}) %collective-permute-start.5) | collective-permute-done | bytes 786464 | tf_op jit(solution)/shard_map/ppermute | solution.py:296
  62.9 2.2 %collective-permute-done.6.refs_6_ = bf16[1536,256]{1,0:T(8,128)(2,1)S(1)} collective-permute-done((bf16[1536,256]{1,0:T(8,128)(2,1)}, bf16[1536,256]{1,0:T(8,128)(2,1)S(1)}, u32[]{:S(2)}, u32[]{:S(2)}) %collective-permute-start.6) | collective-permute-done | bytes 786464 | tf_op jit(solution)/shard_map/ppermute | solution.py:296
  65.1 1.0 copy-done.13
  66.1 1.3 copy-done.9
  67.5 11.9 %shard_map.105 = bf16[4,1024,128]{2,1,0:T(8,128)(2,1)} custom-call(bf16[32,64,512]{2,1,0:T(8,128)(2,1)} %copy-done.9, bf16[1536,256]{1,0:T(8,128)(2,1)} %shard_map.103.refs_0_, bf16[1536,256]{1,0:T(8,128)(2,1)} %collective-permute-done.1.refs_1_, bf16[1536,256]{1,0:T(8,128)(2,1)} %collective-permute-done.2.refs_2_, ...), custom_call_target="tpu_custom_call" | custom-call | flops 6442450944 | bytes 8388608 | tf_op jit(solution)/shard_map/pallas_call | solution.py:182
  79.3 17.0 %all-to-all-start.2 = ((bf16[128,32,128]{2,1,0:T(8,128)(2,1)}), bf16[128,32,128]{2,1,0:T(8,128)(2,1)S(1)}, u32[]{:S(2)}, u32[]{:S(2)}) async-start(bf16[128,32,128]{2,1,0:T(8,128)(2,1)} %bitcast.15), calls=%async_computation.2 | async-start | bytes 2097152 | tf_op jit(solution)/shard_map/all_to_all | solution.py:301
  96.4 11.8 %shard_map.104 = bf16[4,1024,128]{2,1,0:T(8,128)(2,1)} custom-call(bf16[32,64,512]{2,1,0:T(8,128)(2,1)} %copy-done.9, bf16[1536,256]{1,0:T(8,128)(2,1)} %shard_map.103.refs_0_, bf16[1536,256]{1,0:T(8,128)(2,1)} %collective-permute-done.1.refs_1_, bf16[1536,256]{1,0:T(8,128)(2,1)} %collective-permute-done.2.refs_2_, ...), custom_call_target="tpu_custom_call" | custom-call | flops 6442450944 | bytes 8388608 | tf_op jit(solution)/shard_map/pallas_call | solution.py:182
  108.3 7.5 %all-to-all-done.2 = bf16[128,32,128]{2,1,0:T(8,128)(2,1)S(1)} async-done(((bf16[128,32,128]{2,1,0:T(8,128)(2,1)}), bf16[128,32,128]{2,1,0:T(8,128)(2,1)S(1)}, u32[]{:S(2)}, u32[]{:S(2)}) %all-to-all-start.2) | async-done | bytes 1048608 | tf_op jit(solution)/shard_map/all_to_all | solution.py:301
  115.7 4.3 %all-to-all-start.1 = ((bf16[128,32,128]{2,1,0:T(8,128)(2,1)}), bf16[128,32,128]{2,1,0:T(8,128)(2,1)S(1)}, u32[]{:S(2)}, u32[]{:S(2)}) async-start(bf16[128,32,128]{2,1,0:T(8,128)(2,1)} %bitcast.14), calls=%async_computation.1 | async-start | bytes 2097152 | tf_op jit(solution)/shard_map/all_to_all | solution.py:303
  120.1 1.7 collective-permute-start.8
  121.7 2.9 %collective-permute-start.9 = (bf16[2048,128]{1,0:T(8,128)(2,1)}, bf16[2048,128]{1,0:T(8,128)(2,1)S(1)}, u32[]{:S(2)}, u32[]{:S(2)}) collective-permute-start(bf16[2048,128]{1,0:T(8,128)(2,1)} %get-tuple-element.25.refs_9_), channel_id=1, source_target_pairs={{0,64},{32,96},{64,0},{96,32},{1,65},{33,97},{65,1},{97,33},{2,66}... | collective-permute-start | bytes 1572872 | tf_op jit(solution)/shard_map/ppermute | solution.py:293
  124.7 0.9 collective-permute-start.10
  125.6 5.3 %shard_map.106.refs_0_ = f32[2048,128]{1,0:T(8,128)S(1)} custom-call(f32[2,2048]{1,0:T(2,128)S(1)} %copy-done.8, f32[2,2048]{1,0:T(2,128)S(1)} %bitcast.11, bf16[4096,128]{1,0:T(8,128)(2,1)S(1)} %bitcast.9, bf16[2048,128]{1,0:T(8,128)(2,1)S(1)} %copy-done), custom_call_target="tpu_custom_call" | custom-call | flops 2147483648 | bytes 3670016 | tf_op jit(solution)/shard_map/pallas_call | solution.py:245
  130.9 1.0 copy-done.6
  131.9 14.6 %collective-permute-done.8.refs_1_ = bf16[2048,128]{1,0:T(8,128)(2,1)S(1)} collective-permute-done((bf16[2048,128]{1,0:T(8,128)(2,1)}, bf16[2048,128]{1,0:T(8,128)(2,1)S(1)}, u32[]{:S(2)}, u32[]{:S(2)}) %collective-permute-start.8) | collective-permute-done | bytes 524320 | tf_op jit(solution)/shard_map/ppermute | solution.py:293
  146.5 11.9 %collective-permute-done.9.refs_2_ = bf16[2048,128]{1,0:T(8,128)(2,1)S(1)} collective-permute-done((bf16[2048,128]{1,0:T(8,128)(2,1)}, bf16[2048,128]{1,0:T(8,128)(2,1)S(1)}, u32[]{:S(2)}, u32[]{:S(2)}) %collective-permute-start.9) | collective-permute-done | bytes 524320 | tf_op jit(solution)/shard_map/ppermute | solution.py:293
  158.4 0.8 copy-done.1
  159.2 0.8 copy-done.3
  160.0 1.0 copy-done.2
  161.0 1.0 copy-done.4
  162.1 1.2 copy-done.7
  163.3 6.1 %shard_map.107 = bf16[2048,128]{1,0:T(8,128)(2,1)} custom-call(f32[2,2048]{1,0:T(2,128)S(1)} %copy-done.8, f32[2,2048]{1,0:T(2,128)S(1)} %bitcast.12, bf16[4096,128]{1,0:T(8,128)(2,1)S(1)} %bitcast.10, f32[2048,128]{1,0:T(8,128)S(1)} %copy-done.7, bf16[2048,128]{1,0:T(8,128)(2,1)S(1)} %collective-permute-done.8.refs_1_, bf16[2048,128]{1,0:T(8,128)(2,1)S(1)} %copy-done.2, ...), custom_call_target="tpu_custom_call" | custom-call | flops 2147483648 | bytes 3670016 | tf_op jit(solution)/shard_map/pallas_call | solution.py:245
  (32 shorter events, 0.9 us)
Async XLA Ops:
  3.7 57.1 %collective-permute-start.3 = (bf16[1536,256]{1,0:T(8,128)(2,1)}, bf16[1536,256]{1,0:T(8,128)(2,1)}, u32[]{:S(2)}, u32[]{:S(2)}) collective-permute-start(bf16[1536,256]{1,0:T(8,128)(2,1)} %get-tuple-element.16.after), channel_id=1, source_target_pairs={{0,33},{1,97},{2,35},{3,99},{4,37},{5,101},{6,39},{7,103},{8,41},{... | collective-permute-start | bytes 2359304 | tf_op jit(solution)/shard_map/ppermute | solution.py:285
  19.7 46.4 %all-to-all-start = ((bf16[32,64,512]{2,1,0:T(8,128)(2,1)}), bf16[32,64,512]{2,1,0:T(8,128)(2,1)S(1)}, u32[]{:S(2)}, u32[]{:S(2)}) async-start(bf16[32,64,512]{2,1,0:T(8,128)(2,1)} %bitcast.13), calls=%async_computation | async-start | bytes 4194304 | tf_op jit(solution)/shard_map/all_to_all | solution.py:290
  26.9 24.2 %collective-permute-start = (bf16[1536,256]{1,0:T(8,128)(2,1)}, bf16[1536,256]{1,0:T(8,128)(2,1)S(1)}, u32[]{:S(2)}, u32[]{:S(2)}) collective-permute-start(bf16[1536,256]{1,0:T(8,128)(2,1)} %get-tuple-element.19), channel_id=1, source_target_pairs={{0,0},{1,64},{2,2},{3,66},{4,4},{5,68},{6,6},{7,70},{8,8},{9,72},{... | collective-permute-start | bytes 2359304 | tf_op jit(solution)/shard_map/ppermute | solution.py:285
  34.3 26.1 %collective-permute-start.1 = (bf16[1536,256]{1,0:T(8,128)(2,1)}, bf16[1536,256]{1,0:T(8,128)(2,1)}, u32[]{:S(2)}, u32[]{:S(2)}) collective-permute-start(bf16[1536,256]{1,0:T(8,128)(2,1)} %get-tuple-element.22), channel_id=1, source_target_pairs={{0,1},{1,65},{2,3},{3,67},{4,5},{5,69},{6,7},{7,71},{8,9},{9,73},{... | collective-permute-start | bytes 2359304 | tf_op jit(solution)/shard_map/ppermute | solution.py:285
  34.4 26.0 %collective-permute-start.2 = (bf16[1536,256]{1,0:T(8,128)(2,1)}, bf16[1536,256]{1,0:T(8,128)(2,1)}, u32[]{:S(2)}, u32[]{:S(2)}) collective-permute-start(bf16[1536,256]{1,0:T(8,128)(2,1)} %get-tuple-element.23), channel_id=1, source_target_pairs={{0,32},{1,96},{2,34},{3,98},{4,36},{5,100},{6,38},{7,102},{8,40},{... | collective-permute-start | bytes 2359304 | tf_op jit(solution)/shard_map/ppermute | solution.py:285
  51.2 0.9 copy-start.10
  52.1 9.1 %collective-permute-start.4 = (bf16[1536,256]{1,0:T(8,128)(2,1)}, bf16[1536,256]{1,0:T(8,128)(2,1)S(1)}, u32[]{:S(2)}, u32[]{:S(2)}) collective-permute-start(bf16[1536,256]{1,0:T(8,128)(2,1)} %shard_map.103.refs_0_), channel_id=1, source_target_pairs={{0,1},{1,0},{2,3},{3,2},{4,5},{5,4},{6,7},{7,6},{8,9},{9,8},{10,11... | collective-permute-start | bytes 2359304 | tf_op jit(solution)/shard_map/ppermute | solution.py:296
  60.4 2.5 %collective-permute-start.5 = (bf16[1536,256]{1,0:T(8,128)(2,1)}, bf16[1536,256]{1,0:T(8,128)(2,1)S(1)}, u32[]{:S(2)}, u32[]{:S(2)}) collective-permute-start(bf16[1536,256]{1,0:T(8,128)(2,1)} %collective-permute-done.1.refs_1_), channel_id=1, source_target_pairs={{0,1},{1,0},{2,3},{3,2},{4,5},{5,4},{6,7},{7,6},{8,9},{9,8},{10,11... | collective-permute-start | bytes 2359304 | tf_op jit(solution)/shard_map/ppermute | solution.py:296
  60.4 4.7 %collective-permute-start.6 = (bf16[1536,256]{1,0:T(8,128)(2,1)}, bf16[1536,256]{1,0:T(8,128)(2,1)S(1)}, u32[]{:S(2)}, u32[]{:S(2)}) collective-permute-start(bf16[1536,256]{1,0:T(8,128)(2,1)} %collective-permute-done.2.refs_2_), channel_id=1, source_target_pairs={{0,1},{1,0},{2,3},{3,2},{4,5},{5,4},{6,7},{7,6},{8,9},{9,8},{10,11... | collective-permute-start | bytes 2359304 | tf_op jit(solution)/shard_map/ppermute | solution.py:296
  60.9 5.2 %collective-permute-start.7 = (bf16[1536,256]{1,0:T(8,128)(2,1)}, bf16[1536,256]{1,0:T(8,128)(2,1)}, u32[]{:S(2)}, u32[]{:S(2)}) collective-permute-start(bf16[1536,256]{1,0:T(8,128)(2,1)} %collective-permute-done.3.refs_3_), channel_id=1, source_target_pairs={{0,1},{1,0},{2,3},{3,2},{4,5},{5,4},{6,7},{7,6},{8,9},{9,8},{10,11... | collective-permute-start | bytes 2359304 | tf_op jit(solution)/shard_map/ppermute | solution.py:296
  61.2 4.9 %copy-start.11 = (bf16[1536,256]{1,0:T(8,128)(2,1)}, bf16[1536,256]{1,0:T(8,128)(2,1)S(1)}, u32[]{:S(2)}) copy-start(bf16[1536,256]{1,0:T(8,128)(2,1)S(1)} %collective-permute-done.4.refs_4_) | copy-start | bytes 2359300
  62.9 2.3 %copy-start.12 = (bf16[1536,256]{1,0:T(8,128)(2,1)}, bf16[1536,256]{1,0:T(8,128)(2,1)S(1)}, u32[]{:S(2)}) copy-start(bf16[1536,256]{1,0:T(8,128)(2,1)S(1)} %collective-permute-done.5.refs_5_) | copy-start | bytes 2359300
  65.1 1.0 copy-start.13
  66.1 1.4 copy-start.9
  79.3 36.4 %all-to-all-start.2 = ((bf16[128,32,128]{2,1,0:T(8,128)(2,1)}), bf16[128,32,128]{2,1,0:T(8,128)(2,1)S(1)}, u32[]{:S(2)}, u32[]{:S(2)}) async-start(bf16[128,32,128]{2,1,0:T(8,128)(2,1)} %bitcast.15), calls=%async_computation.2 | async-start | bytes 2097152 | tf_op jit(solution)/shard_map/all_to_all | solution.py:301
  108.2 17.4 %copy-start = (bf16[2048,128]{1,0:T(8,128)(2,1)S(1)}, bf16[2048,128]{1,0:T(8,128)(2,1)}, u32[]{:S(2)}) copy-start(bf16[2048,128]{1,0:T(8,128)(2,1)} %get-tuple-element.21.refs_1_.refs_0_) | copy-start | bytes 1572868
  108.2 17.3 %copy-start.5 = (f32[2048,2]{0,1:T(2,128)S(1)}, f32[2048,2]{0,1:T(2,128)}, u32[]{:S(2)}) copy-start(f32[2048,2]{0,1:T(2,128)} %param.13) | copy-start | bytes 49156
  108.2 17.3 %copy-start.8 = (f32[2,2048]{1,0:T(2,128)S(1)}, f32[2,2048]{1,0:T(2,128)}, u32[]{:S(2)}) copy-start(f32[2,2048]{1,0:T(2,128)} %get-tuple-element.17.position) | copy-start | bytes 49156
  115.7 44.2 %all-to-all-start.1 = ((bf16[128,32,128]{2,1,0:T(8,128)(2,1)}), bf16[128,32,128]{2,1,0:T(8,128)(2,1)S(1)}, u32[]{:S(2)}, u32[]{:S(2)}) async-start(bf16[128,32,128]{2,1,0:T(8,128)(2,1)} %bitcast.14), calls=%async_computation.1 | async-start | bytes 2097152 | tf_op jit(solution)/shard_map/all_to_all | solution.py:303
  120.1 26.4 %collective-permute-start.8 = (bf16[2048,128]{1,0:T(8,128)(2,1)}, bf16[2048,128]{1,0:T(8,128)(2,1)S(1)}, u32[]{:S(2)}, u32[]{:S(2)}) collective-permute-start(bf16[2048,128]{1,0:T(8,128)(2,1)} %get-tuple-element.24.refs_8_), channel_id=1, source_target_pairs={{0,32},{32,64},{64,96},{96,0},{1,33},{33,65},{65,97},{97,1},{2,34}... | collective-permute-start | bytes 1572872 | tf_op jit(solution)/shard_map/ppermute | solution.py:293
  121.7 36.6 %collective-permute-start.9 = (bf16[2048,128]{1,0:T(8,128)(2,1)}, bf16[2048,128]{1,0:T(8,128)(2,1)S(1)}, u32[]{:S(2)}, u32[]{:S(2)}) collective-permute-start(bf16[2048,128]{1,0:T(8,128)(2,1)} %get-tuple-element.25.refs_9_), channel_id=1, source_target_pairs={{0,64},{32,96},{64,0},{96,32},{1,65},{33,97},{65,1},{97,33},{2,66}... | collective-permute-start | bytes 1572872 | tf_op jit(solution)/shard_map/ppermute | solution.py:293
  124.7 34.5 %collective-permute-start.10 = (bf16[2048,128]{1,0:T(8,128)(2,1)}, bf16[2048,128]{1,0:T(8,128)(2,1)S(1)}, u32[]{:S(2)}, u32[]{:S(2)}) collective-permute-start(bf16[2048,128]{1,0:T(8,128)(2,1)} %get-tuple-element.26.refs_10_), channel_id=1, source_target_pairs={{0,96},{32,0},{64,32},{96,64},{1,97},{33,1},{65,33},{97,65},{2,98}... | collective-permute-start | bytes 1572872 | tf_op jit(solution)/shard_map/ppermute | solution.py:293
  130.9 1.0 copy-start.6
  158.4 0.8 copy-start.1
  159.2 0.8 copy-start.3
  160.0 1.0 copy-start.2
  161.0 1.0 copy-start.4
  162.0 1.2 copy-start.7

commit v7 on v5

--- a/solution.py
+++ b/solution.py
@@ -72,7 +72,9 @@
             chosen[:, at] = jnp.where(first | second, rank, -1.0)
             seen = seen + jnp.sum(named, axis=1, keepdims=True)
             number = rank.astype(jnp.int32)
-            slot = m * core + number // core * turn + number % turn + number // turn % 2 * (experts * core)
+            log = turn.bit_length() - 1
+            slot = m * core + ((number >> (log + 1)) << log) + (number & (turn - 1))
+            slot = slot + ((number >> log) & 1) * (experts * core)
             slot = slot.astype(F32)
             position[0:1, at] = jnp.max(jnp.where(first, slot, -1.0), axis=0, keepdims=True)
             position[1:2, at] = jnp.max(jnp.where(second, slot, -1.0), axis=0, keepdims=True)
@@ -80,9 +82,14 @@
             scale = lax.rsqrt(jnp.mean(values * values, axis=-1, keepdims=True) + 1e-05)
             normed[at, :] = (values * scale * gain[...]).astype(BF16)
 
-    ranks = lax.broadcasted_iota(jnp.int32, (cap, rows), 0).astype(F32)
+    ranks = lax.broadcasted_iota(jnp.int32, (cap, rows), 0).astype(jnp.int16)
     start = plane[0] * columns + step * per
-    masks = [jnp.where(ranks == chosen[pl.ds(start + i, 1), :], 1.0, 0.0).astype(BF16) for i in range(per)]
+    yes, no = jnp.ones((), BF16), jnp.zeros((), BF16)
+    masks = []
+    for i in range(per):
+        own = jnp.broadcast_to(chosen[pl.ds(start + i, 1), :], (16, rows)).astype(jnp.int32).astype(jnp.int16)[None]
+        own = jnp.broadcast_to(own, (cap // 16, 16, rows)).reshape(cap, rows)
+        masks.append(jnp.where(ranks == own, yes, no))
     outgoing[...] = dot(jnp.concatenate(masks, axis=0), normed[...]).astype(BF16)
 
 

time: 135 us -> 134 us (level)
  no operation moved by 1% of the time
where the time goes in v7:
time: 134 us; the launch traced here: 133 us
  Pallas kernels  54.8 us (41%)
  starting transfers between devices  43.1 us (32%)
  waiting for transfers between devices  27.4 us (20%)
  local copies, waits for them, and re-layouts  7.71 us (6%)
    pallas_call x2, Pallas kernels, expert(): pl.pallas_call(functools.partial(expert_kernel, turn), out_shape=jax.Shap...  23.7 us
    ppermute x4, starting transfers between devices, per_device(): halves.append(lax.ppermute(send, both, moves))  14.3 us
    pallas_call x2, Pallas kernels, combine(): pl.pallas_call(functools.partial(combine_kernel, base), out_shape=jax.Sha...  11.4 us
    all_to_all x1, waiting for transfers between devices, per_device(): lax.all_to_all(second.reshape(planes * sectors, -1, part), both, 0, 0, ti...  10.9 us
    pallas_call x1, Pallas kernels, route(): pl.pallas_call(functools.partial(route_kernel, block, cap, stack), grid=(...  8.83 us
    unnamed x30, local copies, waits for them, and re-layouts  7.71 us
    ppermute x4, waiting for transfers between devices, per_device(): halves.append(lax.ppermute(send, both, moves))  7.67 us
    all_to_all x1, starting transfers between devices, per_device(): lax.all_to_all(first.reshape(planes * sectors, -1, part), both, 0, 0, til...  7.56 us
  transfers between devices with their start and end apart: 14, of which 6 were waited for; matrix products, arithmetic and copies ran while one was open for 0% of the time, Pallas kernels for 34%

profile of v7, /device:TPU:1, one launch (start us, length us, event | category | flops | bytes accessed | tf_op | source)
XLA Modules:
  0.0 133.3 jit_solution(16989682456755859738)
XLA Ops:
  0.0 3.7 %shard_map.100 = (bf16[1536,256]{1,0:T(8,128)(2,1)}, bf16[1536,256]{1,0:T(8,128)(2,1)}, bf16[1536,256]{1,0:T(8,128)(2,1)}, bf16[1536,256]{1,0:T(8,128)(2,1)}) custom-call(s32[1]{0:T(128)} %bitcast.place.plane, bf16[2,512,512]{2,1,0:T(8,128)(2,1)} %gate.2, bf16[2,512,512]{2,1,0:T(8,128)(2,1)} %up.2, bf16[2,512,512]{2,1,0:T(8,128)(2,1)} %down.2), custom_call_target="tpu_custom_call" | custom-call | bytes 6291456 | tf_op jit(solution)/shard_map/pallas_call | solution.py:40
  3.7 6.9 %collective-permute-start = (bf16[1536,256]{1,0:T(8,128)(2,1)}, bf16[1536,256]{1,0:T(8,128)(2,1)}, u32[]{:S(2)}, u32[]{:S(2)}) collective-permute-start(bf16[1536,256]{1,0:T(8,128)(2,1)} %get-tuple-element.19), channel_id=1, source_target_pairs={{0,0},{1,64},{2,2},{3,66},{4,4},{5,68},{6,6},{7,70},{8,8},{9,72},{... | collective-permute-start | bytes 2359304 | tf_op jit(solution)/shard_map/ppermute | solution.py:292
  10.6 7.0 %collective-permute-start.3 = (bf16[1536,256]{1,0:T(8,128)(2,1)}, bf16[1536,256]{1,0:T(8,128)(2,1)S(1)}, u32[]{:S(2)}, u32[]{:S(2)}) collective-permute-start(bf16[1536,256]{1,0:T(8,128)(2,1)} %get-tuple-element.16.after), channel_id=1, source_target_pairs={{0,33},{1,97},{2,35},{3,99},{4,37},{5,101},{6,39},{7,103},{8,41},{... | collective-permute-start | bytes 2359304 | tf_op jit(solution)/shard_map/ppermute | solution.py:292
  17.7 8.8 %shard_map.101 = (bf16[2048,512]{1,0:T(8,128)(2,1)}, bf16[2048,512]{1,0:T(8,128)(2,1)}, f32[2,2048]{1,0:T(2,128)}) custom-call(s32[1]{0:T(128)} %bitcast.place.plane, bf16[2048,512]{1,0:T(8,128)(2,1)} %tokens.1, f32[1,512]{1,0:T(1,128)} %bitcast.17, s32[2,2048]{1,0:T(2,128)} %bitcast.16, bf16[1536,256]{1,0:T(8,128)(2,1)} %get-tuple-element.16.after), custom_call_target="tpu_custom_call" | custom-call | flops 4294967296 | bytes 8388608 | tf_op jit(solution)/shard_map/pallas_call | solution.py:100
  26.5 7.4 %all-to-all-start = ((bf16[32,64,512]{2,1,0:T(8,128)(2,1)}), bf16[32,64,512]{2,1,0:T(8,128)(2,1)}, u32[]{:S(2)}, u32[]{:S(2)}) async-start(bf16[32,64,512]{2,1,0:T(8,128)(2,1)} %bitcast.13), calls=%async_computation | async-start | bytes 4194304 | tf_op jit(solution)/shard_map/all_to_all | solution.py:297
  33.9 0.1 collective-permute-start.1
  34.0 0.3 collective-permute-start.2
  34.3 7.2 %shard_map.102 = (bf16[2048,128]{1,0:T(8,128)(2,1)}, bf16[2048,128]{1,0:T(8,128)(2,1)}, bf16[2048,128]{1,0:T(8,128)(2,1)}, bf16[2048,128]{1,0:T(8,128)(2,1)}) custom-call(s32[1]{0:T(128)} %bitcast.place.plane, bf16[2048,512]{1,0:T(8,128)(2,1)} %get-tuple-element.20.normed, bf16[512,512]{1,0:T(8,128)(2,1)} %gate.3, bf16[512,512]{1,0:T(8,128)(2,1)} %up.3, ...), custom_call_target="tpu_custom_call" | custom-call | flops 32212254720 | bytes 4194304 | tf_op jit(solution)/shard_map/pallas_call | solution.py:144
  41.5 2.1 %collective-permute-start.4 = (bf16[1536,256]{1,0:T(8,128)(2,1)}, bf16[1536,256]{1,0:T(8,128)(2,1)S(1)}, u32[]{:S(2)}, u32[]{:S(2)}) collective-permute-start(bf16[1536,256]{1,0:T(8,128)(2,1)} %shard_map.103.refs_0_), channel_id=1, source_target_pairs={{0,1},{1,0},{2,3},{3,2},{4,5},{5,4},{6,7},{7,6},{8,9},{9,8},{10,11... | collective-permute-start | bytes 2359304 | tf_op jit(solution)/shard_map/ppermute | solution.py:303
  43.6 0.1 collective-permute-start.7
  43.7 5.7 %collective-permute-done.1.refs_1_ = bf16[1536,256]{1,0:T(8,128)(2,1)} collective-permute-done((bf16[1536,256]{1,0:T(8,128)(2,1)}, bf16[1536,256]{1,0:T(8,128)(2,1)}, u32[]{:S(2)}, u32[]{:S(2)}) %collective-permute-start.1) | collective-permute-done | bytes 786464 | tf_op jit(solution)/shard_map/ppermute | solution.py:292
  49.4 4.1 %collective-permute-start.5 = (bf16[1536,256]{1,0:T(8,128)(2,1)}, bf16[1536,256]{1,0:T(8,128)(2,1)}, u32[]{:S(2)}, u32[]{:S(2)}) collective-permute-start(bf16[1536,256]{1,0:T(8,128)(2,1)} %collective-permute-done.1.refs_1_), channel_id=1, source_target_pairs={{0,1},{1,0},{2,3},{3,2},{4,5},{5,4},{6,7},{7,6},{8,9},{9,8},{10,11... | collective-permute-start | bytes 2359304 | tf_op jit(solution)/shard_map/ppermute | solution.py:303
  53.5 2.0 %collective-permute-done.2.refs_2_ = bf16[1536,256]{1,0:T(8,128)(2,1)} collective-permute-done((bf16[1536,256]{1,0:T(8,128)(2,1)S(1)}, bf16[1536,256]{1,0:T(8,128)(2,1)}, u32[]{:S(2)}, u32[]{:S(2)}) %collective-permute-start.2) | collective-permute-done | bytes 786464 | tf_op jit(solution)/shard_map/ppermute | solution.py:292
  55.5 0.9 copy-done.12
  56.5 1.4 %collective-permute-start.8 = (bf16[2048,128]{1,0:T(8,128)(2,1)}, bf16[2048,128]{1,0:T(8,128)(2,1)S(1)}, u32[]{:S(2)}, u32[]{:S(2)}) collective-permute-start(bf16[2048,128]{1,0:T(8,128)(2,1)} %get-tuple-element.24.refs_8_), channel_id=1, source_target_pairs={{0,32},{32,64},{64,96},{96,0},{1,33},{33,65},{65,97},{97,1},{2,34}... | collective-permute-start | bytes 1572872 | tf_op jit(solution)/shard_map/ppermute | solution.py:300
  57.9 0.9 copy-done.13
  58.8 3.0 %all-to-all-done.slots = bf16[32,64,512]{2,1,0:T(8,128)(2,1)} async-done(((bf16[32,64,512]{2,1,0:T(8,128)(2,1)}), bf16[32,64,512]{2,1,0:T(8,128)(2,1)}, u32[]{:S(2)}, u32[]{:S(2)}) %all-to-all-start) | async-done | bytes 2097184 | tf_op jit(solution)/shard_map/all_to_all | solution.py:297
  61.8 11.9 %shard_map.105 = bf16[4,1024,128]{2,1,0:T(8,128)(2,1)} custom-call(bf16[32,64,512]{2,1,0:T(8,128)(2,1)} %all-to-all-done.slots, bf16[1536,256]{1,0:T(8,128)(2,1)} %shard_map.103.refs_0_, bf16[1536,256]{1,0:T(8,128)(2,1)} %collective-permute-done.1.refs_1_, bf16[1536,256]{1,0:T(8,128)(2,1)} %collective-permute-done.2.refs_2_, bf16[1536,256]{1,0:T(8,128)(2,1)} %copy-done.11, ...), custom_call_target="tpu_custom_call" | custom-call | flops 6442450944 | bytes 8388608 | tf_op jit(solution)/shard_map/pallas_call | solution.py:189
  73.6 7.6 %all-to-all-start.2 = ((bf16[128,32,128]{2,1,0:T(8,128)(2,1)}), bf16[128,32,128]{2,1,0:T(8,128)(2,1)S(1)}, u32[]{:S(2)}, u32[]{:S(2)}) async-start(bf16[128,32,128]{2,1,0:T(8,128)(2,1)} %bitcast.14), calls=%async_computation.2 | async-start | bytes 2097152 | tf_op jit(solution)/shard_map/all_to_all | solution.py:308
  81.2 0.9 collective-permute-done.8.refs_8_.refs_1_
  82.1 0.8 copy-done.3
  82.9 0.8 copy-done.5
  83.7 11.8 %shard_map.104 = bf16[4,1024,128]{2,1,0:T(8,128)(2,1)} custom-call(bf16[32,64,512]{2,1,0:T(8,128)(2,1)} %all-to-all-done.slots, bf16[1536,256]{1,0:T(8,128)(2,1)} %shard_map.103.refs_0_, bf16[1536,256]{1,0:T(8,128)(2,1)} %collective-permute-done.1.refs_1_, bf16[1536,256]{1,0:T(8,128)(2,1)} %collective-permute-done.2.refs_2_, bf16[1536,256]{1,0:T(8,128)(2,1)} %copy-done.11, ...), custom_call_target="tpu_custom_call" | custom-call | flops 6442450944 | bytes 8388608 | tf_op jit(solution)/shard_map/pallas_call | solution.py:189
  95.6 4.9 %all-to-all-done.2 = bf16[128,32,128]{2,1,0:T(8,128)(2,1)S(1)} async-done(((bf16[128,32,128]{2,1,0:T(8,128)(2,1)}), bf16[128,32,128]{2,1,0:T(8,128)(2,1)S(1)}, u32[]{:S(2)}, u32[]{:S(2)}) %all-to-all-start.2) | async-done | bytes 1048608 | tf_op jit(solution)/shard_map/all_to_all | solution.py:308
  100.5 6.1 %all-to-all-start.1 = ((bf16[128,32,128]{2,1,0:T(8,128)(2,1)}), bf16[128,32,128]{2,1,0:T(8,128)(2,1)S(1)}, u32[]{:S(2)}, u32[]{:S(2)}) async-start(bf16[128,32,128]{2,1,0:T(8,128)(2,1)} %bitcast.15), calls=%async_computation.1 | async-start | bytes 2097152 | tf_op jit(solution)/shard_map/all_to_all | solution.py:310
  106.7 1.0 copy-done.4
  107.7 1.0 copy-done.6
  108.8 5.3 %shard_map.106.refs_0_ = f32[2048,128]{1,0:T(8,128)S(1)} custom-call(f32[2,2048]{1,0:T(2,128)S(1)} %copy-done.10, f32[2,2048]{1,0:T(2,128)S(1)} %bitcast.11, bf16[4096,128]{1,0:T(8,128)(2,1)S(1)} %bitcast.9, bf16[2048,128]{1,0:T(8,128)(2,1)S(1)} %copy-done, bf16[2048,128]{1,0:T(8,128)(2,1)S(1)} %copy-done.4, bf16[2048,128]{1,0:T(8,128)(2,1)S(1)} %copy-done.6, ...), custom_call_target="tpu_custom_call" | custom-call | flops 2147483648 | bytes 3670016 | tf_op jit(solution)/shard_map/pallas_call | solution.py:252
  114.1 1.0 copy-done.8
  115.0 10.9 %all-to-all-done.1 = bf16[128,32,128]{2,1,0:T(8,128)(2,1)S(1)} async-done(((bf16[128,32,128]{2,1,0:T(8,128)(2,1)}), bf16[128,32,128]{2,1,0:T(8,128)(2,1)S(1)}, u32[]{:S(2)}, u32[]{:S(2)}) %all-to-all-start.1) | async-done | bytes 1048608 | tf_op jit(solution)/shard_map/all_to_all | solution.py:310
  126.0 1.2 copy-done.9
  127.2 6.1 %shard_map.107 = bf16[2048,128]{1,0:T(8,128)(2,1)} custom-call(f32[2,2048]{1,0:T(2,128)S(1)} %copy-done.10, f32[2,2048]{1,0:T(2,128)S(1)} %bitcast.12, bf16[4096,128]{1,0:T(8,128)(2,1)S(1)} %bitcast.10, f32[2048,128]{1,0:T(8,128)S(1)} %copy-done.9), custom_call_target="tpu_custom_call" | custom-call | flops 2147483648 | bytes 3670016 | tf_op jit(solution)/shard_map/pallas_call | solution.py:252
  (34 shorter events, 0.1 us)
Async XLA Ops:
  3.7 37.7 %collective-permute-start = (bf16[1536,256]{1,0:T(8,128)(2,1)}, bf16[1536,256]{1,0:T(8,128)(2,1)}, u32[]{:S(2)}, u32[]{:S(2)}) collective-permute-start(bf16[1536,256]{1,0:T(8,128)(2,1)} %get-tuple-element.19), channel_id=1, source_target_pairs={{0,0},{1,64},{2,2},{3,66},{4,4},{5,68},{6,6},{7,70},{8,8},{9,72},{... | collective-permute-start | bytes 2359304 | tf_op jit(solution)/shard_map/ppermute | solution.py:292
  10.6 33.0 %collective-permute-start.3 = (bf16[1536,256]{1,0:T(8,128)(2,1)}, bf16[1536,256]{1,0:T(8,128)(2,1)S(1)}, u32[]{:S(2)}, u32[]{:S(2)}) collective-permute-start(bf16[1536,256]{1,0:T(8,128)(2,1)} %get-tuple-element.16.after), channel_id=1, source_target_pairs={{0,33},{1,97},{2,35},{3,99},{4,37},{5,101},{6,39},{7,103},{8,41},{... | collective-permute-start | bytes 2359304 | tf_op jit(solution)/shard_map/ppermute | solution.py:292
  26.5 7.5 %copy-start.14 = (bf16[1536,256]{1,0:T(8,128)(2,1)S(1)}, bf16[1536,256]{1,0:T(8,128)(2,1)}, u32[]{:S(2)}) copy-start(bf16[1536,256]{1,0:T(8,128)(2,1)} %get-tuple-element.23) | copy-start | bytes 2359300
  26.5 35.3 %all-to-all-start = ((bf16[32,64,512]{2,1,0:T(8,128)(2,1)}), bf16[32,64,512]{2,1,0:T(8,128)(2,1)}, u32[]{:S(2)}, u32[]{:S(2)}) async-start(bf16[32,64,512]{2,1,0:T(8,128)(2,1)} %bitcast.13), calls=%async_computation | async-start | bytes 4194304 | tf_op jit(solution)/shard_map/all_to_all | solution.py:297
  33.9 15.5 %collective-permute-start.1 = (bf16[1536,256]{1,0:T(8,128)(2,1)}, bf16[1536,256]{1,0:T(8,128)(2,1)}, u32[]{:S(2)}, u32[]{:S(2)}) collective-permute-start(bf16[1536,256]{1,0:T(8,128)(2,1)} %get-tuple-element.22), channel_id=1, source_target_pairs={{0,1},{1,65},{2,3},{3,67},{4,5},{5,69},{6,7},{7,71},{8,9},{9,73},{... | collective-permute-start | bytes 2359304 | tf_op jit(solution)/shard_map/ppermute | solution.py:292
  34.0 21.5 %collective-permute-start.2 = (bf16[1536,256]{1,0:T(8,128)(2,1)S(1)}, bf16[1536,256]{1,0:T(8,128)(2,1)}, u32[]{:S(2)}, u32[]{:S(2)}) collective-permute-start(bf16[1536,256]{1,0:T(8,128)(2,1)S(1)} %copy-done.14), channel_id=1, source_target_pairs={{0,32},{1,96},{2,34},{3,98},{4,36},{5,100},{6,38},{7,102},{8,40},{... | collective-permute-start | bytes 2359304 | tf_op jit(solution)/shard_map/ppermute | solution.py:292
  41.5 14.1 %collective-permute-start.4 = (bf16[1536,256]{1,0:T(8,128)(2,1)}, bf16[1536,256]{1,0:T(8,128)(2,1)S(1)}, u32[]{:S(2)}, u32[]{:S(2)}) collective-permute-start(bf16[1536,256]{1,0:T(8,128)(2,1)} %shard_map.103.refs_0_), channel_id=1, source_target_pairs={{0,1},{1,0},{2,3},{3,2},{4,5},{5,4},{6,7},{7,6},{8,9},{9,8},{10,11... | collective-permute-start | bytes 2359304 | tf_op jit(solution)/shard_map/ppermute | solution.py:303
  43.6 18.2 %copy-start.11 = (bf16[1536,256]{1,0:T(8,128)(2,1)}, bf16[1536,256]{1,0:T(8,128)(2,1)S(1)}, u32[]{:S(2)}) copy-start(bf16[1536,256]{1,0:T(8,128)(2,1)S(1)} %collective-permute-done.3.refs_3_) | copy-start | bytes 2359300
  43.6 14.3 %collective-permute-start.7 = (bf16[1536,256]{1,0:T(8,128)(2,1)S(1)}, bf16[1536,256]{1,0:T(8,128)(2,1)S(1)}, u32[]{:S(2)}, u32[]{:S(2)}) collective-permute-start(bf16[1536,256]{1,0:T(8,128)(2,1)S(1)} %collective-permute-done.3.refs_3_), channel_id=1, source_target_pairs={{0,1},{1,0},{2,3},{3,2},{4,5},{5,4},{6,7},{7,6},{8,9},{9,8},{10,11... | collective-permute-start | bytes 2359304 | tf_op jit(solution)/shard_map/ppermute | solution.py:303
  49.4 9.4 %collective-permute-start.5 = (bf16[1536,256]{1,0:T(8,128)(2,1)}, bf16[1536,256]{1,0:T(8,128)(2,1)}, u32[]{:S(2)}, u32[]{:S(2)}) collective-permute-start(bf16[1536,256]{1,0:T(8,128)(2,1)} %collective-permute-done.1.refs_1_), channel_id=1, source_target_pairs={{0,1},{1,0},{2,3},{3,2},{4,5},{5,4},{6,7},{7,6},{8,9},{9,8},{10,11... | collective-permute-start | bytes 2359304 | tf_op jit(solution)/shard_map/ppermute | solution.py:303
  55.5 3.3 %collective-permute-start.6 = (bf16[1536,256]{1,0:T(8,128)(2,1)}, bf16[1536,256]{1,0:T(8,128)(2,1)}, u32[]{:S(2)}, u32[]{:S(2)}) collective-permute-start(bf16[1536,256]{1,0:T(8,128)(2,1)} %collective-permute-done.2.refs_2_), channel_id=1, source_target_pairs={{0,1},{1,0},{2,3},{3,2},{4,5},{5,4},{6,7},{7,6},{8,9},{9,8},{10,11... | collective-permute-start | bytes 2359304 | tf_op jit(solution)/shard_map/ppermute | solution.py:303
  55.5 25.7 %collective-permute-start.10 = (bf16[2048,128]{1,0:T(8,128)(2,1)}, bf16[2048,128]{1,0:T(8,128)(2,1)S(1)}, u32[]{:S(2)}, u32[]{:S(2)}) collective-permute-start(bf16[2048,128]{1,0:T(8,128)(2,1)} %get-tuple-element.26.refs_10_), channel_id=1, source_target_pairs={{0,96},{32,0},{64,32},{96,64},{1,97},{33,1},{65,33},{97,65},{2,98}... | collective-permute-start | bytes 1572872 | tf_op jit(solution)/shard_map/ppermute | solution.py:300
  55.5 0.9 copy-start.12
  56.5 25.7 %collective-permute-start.8 = (bf16[2048,128]{1,0:T(8,128)(2,1)}, bf16[2048,128]{1,0:T(8,128)(2,1)S(1)}, u32[]{:S(2)}, u32[]{:S(2)}) collective-permute-start(bf16[2048,128]{1,0:T(8,128)(2,1)} %get-tuple-element.24.refs_8_), channel_id=1, source_target_pairs={{0,32},{32,64},{64,96},{96,0},{1,33},{33,65},{65,97},{97,1},{2,34}... | collective-permute-start | bytes 1572872 | tf_op jit(solution)/shard_map/ppermute | solution.py:300
  57.9 0.9 copy-start.13
  58.8 23.3 %collective-permute-start.9 = (bf16[2048,128]{1,0:T(8,128)(2,1)}, bf16[2048,128]{1,0:T(8,128)(2,1)S(1)}, u32[]{:S(2)}, u32[]{:S(2)}) collective-permute-start(bf16[2048,128]{1,0:T(8,128)(2,1)} %get-tuple-element.25.refs_9_), channel_id=1, source_target_pairs={{0,64},{32,96},{64,0},{96,32},{1,65},{33,97},{65,1},{97,33},{2,66}... | collective-permute-start | bytes 1572872 | tf_op jit(solution)/shard_map/ppermute | solution.py:300
  73.6 26.9 %all-to-all-start.2 = ((bf16[128,32,128]{2,1,0:T(8,128)(2,1)}), bf16[128,32,128]{2,1,0:T(8,128)(2,1)S(1)}, u32[]{:S(2)}, u32[]{:S(2)}) async-start(bf16[128,32,128]{2,1,0:T(8,128)(2,1)} %bitcast.14), calls=%async_computation.2 | async-start | bytes 2097152 | tf_op jit(solution)/shard_map/all_to_all | solution.py:308
  81.2 0.9 copy-start.1
  82.1 0.8 copy-start.3
  82.9 0.8 copy-start.5
  95.6 11.1 %copy-start = (bf16[2048,128]{1,0:T(8,128)(2,1)S(1)}, bf16[2048,128]{1,0:T(8,128)(2,1)}, u32[]{:S(2)}) copy-start(bf16[2048,128]{1,0:T(8,128)(2,1)} %get-tuple-element.21.refs_1_.refs_0_) | copy-start | bytes 1572868
  95.6 11.1 %copy-start.2 = (bf16[2048,128]{1,0:T(8,128)(2,1)S(1)}, bf16[2048,128]{1,0:T(8,128)(2,1)}, u32[]{:S(2)}) copy-start(bf16[2048,128]{1,0:T(8,128)(2,1)} %copy-done.1) | copy-start | bytes 1572868
  95.6 11.1 %copy-start.7 = (f32[2048,2]{0,1:T(2,128)S(1)}, f32[2048,2]{0,1:T(2,128)}, u32[]{:S(2)}) copy-start(f32[2048,2]{0,1:T(2,128)} %param.13) | copy-start | bytes 49156
  95.6 11.1 %copy-start.10 = (f32[2,2048]{1,0:T(2,128)S(1)}, f32[2,2048]{1,0:T(2,128)}, u32[]{:S(2)}) copy-start(f32[2,2048]{1,0:T(2,128)} %get-tuple-element.17.position) | copy-start | bytes 49156
  100.5 25.4 %all-to-all-start.1 = ((bf16[128,32,128]{2,1,0:T(8,128)(2,1)}), bf16[128,32,128]{2,1,0:T(8,128)(2,1)S(1)}, u32[]{:S(2)}, u32[]{:S(2)}) async-start(bf16[128,32,128]{2,1,0:T(8,128)(2,1)} %bitcast.15), calls=%async_computation.1 | async-start | bytes 2097152 | tf_op jit(solution)/shard_map/all_to_all | solution.py:310
  106.7 1.0 copy-start.4
  107.7 1.0 copy-start.6
  114.0 1.0 copy-start.8
  126.0 1.2 copy-start.9
